TPU v7x, 32 devices: a whole 2x2x4 slice. The times are simulated.
32 devices in a mesh: group: 8 (over z, x), module: 4 (over y, core).
Axes of the slice: x: 2, y: 2, z: 4, core: 2. Of those that a mesh axis runs over, the one named last changes fastest.
Arguments:
- train_grads: bfloat16 [2048, 4, 1024], P(('group', 'module')), may hold values from -6 to 6
- query_grads: bfloat16 [8, 32, 4, 1024], P('group', None, 'module'), may hold values from -6 to 6
- basis_out: bfloat16 [4, 32, 32], P('module'), may hold values from -1 to 1
- basis_in: bfloat16 [4, 32, 32], P('module'), may hold values from -1 to 1
- eigenvalues: float32 [4, 1024], P('module'), may hold values from 0.05 to 5
- owner_groups: int32 [4], replicated, may hold values from 0 to 7, as said below
- module_order: int32 [4], replicated, may hold values from 0 to 3, each once
Outputs:
- scores: float32 [2048, 128], P(('group', 'module'))
Inputs may be any that keep to these rules, and one draw needn't show every extreme that they name: `owner_groups`: 4 different groups, the first and the last group among them. `module_order`: each module exactly once.
All inputs are finite; a program needn't handle non-finite values.
Results may differ from a plain program's by a relative error of at most 0.0037.
Values may be sent and summed in bfloat16 or wider, within the bound.
No kernel may reach another device: no remote copies, remote signals or barrier semaphores. Data moves between devices by JAX's collectives and lax.ppermute only.
A program may use at most 64 MiB of HBM per device.

v0:
```python
import math

import jax
import jax.numpy as jnp
from jax import lax
from jax.sharding import PartitionSpec as P


def build_rotator(basis_out, basis_in):
    breadth = basis_out.shape[-1]
    product = (
        basis_out.astype(jnp.float32)[..., :, None, :, None]
        * basis_in.astype(jnp.float32)[..., None, :, None, :]
    )
    return product.reshape(basis_out.shape[:-2] + (breadth * breadth, breadth * breadth)).astype(
        jnp.bfloat16
    )


def local(train_grads, query_grads, basis_out, basis_in, eigenvalues, owner_groups, module_order):
    ex_rows, modules, width = train_grads.shape
    module_devices = lax.axis_size("module")
    slots_dev = modules // module_devices
    rotator = build_rotator(basis_out, basis_in)
    damping = 0.1 * jnp.mean(eigenvalues, axis=1, keepdims=True)
    divisor = eigenvalues + damping
    ordered = jnp.take(train_grads, module_order, axis=1)
    everyone = lax.all_gather(query_grads, "group", axis=0, tiled=True)
    picked = jnp.take(everyone, owner_groups, axis=0)
    queries = picked.reshape(-1, slots_dev, width)
    asked = (
        jnp.einsum("qtw,twv->qtv", queries, rotator, preferred_element_type=jnp.float32)
        / divisor[None]
    ).astype(jnp.bfloat16)
    factor = 1.0 / math.sqrt(modules * width)
    moved = lax.all_to_all(
        ordered.reshape(ex_rows, module_devices, slots_dev, width),
        "module",
        split_axis=1,
        concat_axis=0,
        tiled=True,
    )
    moved = moved.reshape(ex_rows * module_devices, slots_dev, width)
    turned = jnp.einsum("gtw,twv->gtv", moved, rotator, preferred_element_type=jnp.float32).astype(
        jnp.bfloat16
    )
    summed = lax.psum_scatter(
        jnp.einsum("gtv,qtv->gq", turned, asked, preferred_element_type=jnp.float32),
        "module",
        scatter_dimension=0,
        tiled=True,
    )
    return summed * factor


def solution(mesh):
    in_specs = (
        P(("group", "module"), None, None),
        P("group", None, "module", None),
        P("module", None, None),
        P("module", None, None),
        P("module", None),
        P(),
        P(),
    )
    out_specs = P(("group", "module"), None)
    return jax.shard_map(local, mesh=mesh, in_specs=in_specs, out_specs=out_specs, check_vma=False)
```

profile of v0, /device:TPU:0, one launch (start us, length us, event | category | flops | bytes accessed | tf_op | source)
XLA Modules:
  0.0 101.1 jit_solution(16768814958220227968)
XLA Ops:
  6.5 0.0 copy-start
  6.5 0.7 compare_select_fusion.1
  7.3 0.7 compare_and_fusion.1
  7.9 0.0 copy-done
  7.9 2.9 %gather_fusion = bf16[4,64,1024]{2,0,1:T(4,128)(2,1)S(1)} fusion(bf16[64,4,1024]{2,1,0:T(4,128)(2,1)S(1)} %copy-done, s32[1024]{0:T(1024)S(1)} %pad_clamp_fusion.1), kind=kCustom, calls=%fused_computation | custom fusion | bytes 1048592 | tf_op jit(solution)/shard_map/jit(_take)/gather | solution.py:27
  10.9 0.0 copy-start.5
  10.9 0.0 copy-start.3
  10.9 0.0 copy-start.4
  10.9 0.3 bitcast_select_fusion
  11.2 1.0 copy.9
  12.2 4.2 %all-to-all-start = ((bf16[64,4,1,1024]{3,0,2,1:T(8,128)(2,1)}), bf16[64,4,1,1024]{3,0,2,1:T(8,128)(2,1)}, u32[]{:S(2)}, u32[]{:S(2)}) async-start(bf16[64,4,1,1024]{3,0,2,1:T(8,128)(2,1)} %copy.9), calls=%async_computation | async-start | bytes 1048576 | tf_op jit(solution)/shard_map/all_to_all | solution.py:36
  16.4 0.0 reduce-scatter.2.cloned.1.call-start
  16.4 0.0 copy-done.5
  16.5 0.0 copy-done.3
  16.5 0.0 copy-done.4
  16.5 5.3 %multiply_convert_fusion = bf16[32,32,32,32]{3,2,1,0:T(8,128)(2,1)} fusion(f32[32,32]{1,0:T(8,128)S(1)} %get-tuple-element.5, f32[32,32]{1,0:T(8,128)S(1)} %get-tuple-element.6), kind=kLoop, calls=%fused_computation.2 | loop fusion | flops 2097152 | bytes 2105344 | tf_op jit(solution)/shard_map/convert_element_type | solution.py:15
  21.8 0.0 copy-start.1
  21.8 0.0 copy-start.2
  21.8 11.4 %convert_element_type.38 = bf16[1024,1024]{1,0:T(8,128)(2,1)S(1)} reshape(bf16[32,32,32,32]{3,2,1,0:T(8,128)(2,1)} %multiply_convert_fusion) | data formatting | bytes 4194304 | tf_op jit(solution)/shard_map/convert_element_type | solution.py:15
  33.1 0.0 copy-done.1
  33.1 33.3 %all_gather.3 = bf16[8,32,1,1024]{3,1,2,0:T(8,128)(2,1)S(1)} all-gather(bf16[1,32,1,1024]{3,1,2,0:T(8,128)(2,1)S(1)} %copy-done.1), channel_id=1, replica_groups=mesh['group'=8,'module'=4] {'group'}, dimensions={0}, use_global_device_ids=true | all-gather | bytes 589824 | tf_op jit(solution)/shard_map/all_gather | solution.py:28
  66.4 0.6 gather_fusion.1
  67.0 0.1 bitcast_select_fusion.1
  67.1 0.0 copy-done.2
  67.1 0.6 reduce_sum.9
  68.4 0.8 fusion.4
  69.2 0.0 all-to-all-done
  69.2 2.8 %fusion.1 = f32[256,128]{1,0:T(8,128)} fusion(bf16[128,1024]{0,1:T(8,128)(2,1)S(1)} %fusion.4, bf16[1024,1024]{1,0:T(8,128)(2,1)S(1)} %convert_element_type.38, bf16[256,1024]{1,0:T(8,128)(2,1)} %bitcast.6), kind=kOutput, calls=%fused_computation.5 | convolution fusion | flops 604241920 | bytes 3014656 | tf_op jit(solution)/shard_map/gtv,qtv->gq/dot_general | solution.py:48
  72.0 0.0 reduce-scatter.2.cloned.1.call-update
  72.0 20.9 %reduce-scatter.2.cloned.1.call-done = f32[64,128]{1,0:T(8,128)} async-done(((f32[256,128]{1,0:T(8,128)}), f32[64,128]{1,0:T(8,128)}) %reduce-scatter.2.cloned.1.call-update) | async-done | bytes 32784 | tf_op jit(solution)/shard_map/reduce_scatter | solution.py:47
  92.9 1.4 %broadcast_multiply_fusion = f32[64,128]{1,0:T(8,128)} fusion(f32[64,128]{1,0:T(8,128)} %reduce-scatter.2.cloned.1.call-done), kind=kLoop, calls=%fused_computation.12 | loop fusion | flops 8192 | bytes 65536 | tf_op jit(solution)/shard_map/mul | solution.py:53
  (6 shorter events, 0.0 us)
Async XLA Ops:
  6.5 1.4 %copy-start = (bf16[64,4,1024]{2,1,0:T(4,128)(2,1)S(1)}, bf16[64,4,1024]{2,1,0:T(4,128)(2,1)}, u32[]{:S(2)}) copy-start(bf16[64,4,1024]{2,1,0:T(4,128)(2,1)} %param.7) | copy-start | bytes 1572868
  10.9 5.6 %copy-start.5 = (s32[4]{0:T(128)S(1)}, s32[4]{0:T(128)}, u32[]{:S(2)}) copy-start(s32[4]{0:T(128)} %param.12) | copy-start | bytes 52
  10.9 5.6 %copy-start.3 = (bf16[1,32,32]{2,1,0:T(8,128)(2,1)S(1)}, bf16[1,32,32]{2,1,0:T(8,128)(2,1)}, u32[]{:S(2)}) copy-start(bf16[1,32,32]{2,1,0:T(8,128)(2,1)} %param.10) | copy-start | bytes 6148
  10.9 5.6 %copy-start.4 = (bf16[1,32,32]{2,1,0:T(8,128)(2,1)S(1)}, bf16[1,32,32]{2,1,0:T(8,128)(2,1)}, u32[]{:S(2)}) copy-start(bf16[1,32,32]{2,1,0:T(8,128)(2,1)} %param.9) | copy-start | bytes 6148
  12.2 57.0 %all-to-all-start = ((bf16[64,4,1,1024]{3,0,2,1:T(8,128)(2,1)}), bf16[64,4,1,1024]{3,0,2,1:T(8,128)(2,1)}, u32[]{:S(2)}, u32[]{:S(2)}) async-start(bf16[64,4,1,1024]{3,0,2,1:T(8,128)(2,1)} %copy.9), calls=%async_computation | async-start | bytes 1048576 | tf_op jit(solution)/shard_map/all_to_all | solution.py:36
  16.4 76.5 %reduce-scatter.2.cloned.1.call-start = ((), (), s32[]{:S(2)}) async-start(), calls=%async_computation.2 | async-start | bytes 163840 | tf_op jit(solution)/shard_map/reduce_scatter | solution.py:47
  21.8 11.4 %copy-start.1 = (bf16[1,32,1,1024]{3,1,2,0:T(8,128)(2,1)S(1)}, bf16[1,32,1,1024]{3,1,2,0:T(8,128)(2,1)}, u32[]{:S(2)}) copy-start(bf16[1,32,1,1024]{3,1,2,0:T(8,128)(2,1)} %param.8) | copy-start | bytes 196612
  21.8 45.3 %copy-start.2 = (f32[1,1024]{1,0:T(1,128)S(1)}, f32[1,1024]{1,0:T(1,128)}, u32[]{:S(2)}) copy-start(f32[1,1024]{1,0:T(1,128)} %param.11) | copy-start | bytes 12292
Sparse Core Ops, SparseCore 0:
  72.1 20.7 reduce-scatter.1
where the time goes:
time: 102 us; the launch traced here: 101 us
  blocking collectives  33.3 us (33%)
  waiting for transfers between devices  20.9 us (20%)
  local copies, waits for them, and re-layouts  15.9 us (16%)
  between operations  14.2 us (14%)
  other arithmetic  9.05 us (9%)
  starting transfers between devices  4.24 us (4%)
  matrix products  3.6 us (4%)
    all_gather x1, blocking collectives, local(): everyone = lax.all_gather(query_grads, 'group', axis=0, tiled=True)  33.3 us
    reduce_scatter x1, waiting for transfers between devices, local(): lax.psum_scatter(jnp.einsum('gtv,qtv->gq', turned, asked, preferred_eleme...  20.9 us
    convert_element_type x1, local copies, waits for them, and re-layouts, build_rotator(): product.reshape(basis_out.shape[:-2] + (breadth * breadth, breadth * brea...  11.4 us
    convert_element_type x1, other arithmetic, build_rotator(): product.reshape(basis_out.shape[:-2] + (breadth * breadth, breadth * brea...  5.27 us
    all_to_all x1, starting transfers between devices, local(): lax.all_to_all(ordered.reshape(ex_rows, module_devices, slots_dev, width)...  4.24 us
    gather x1, local copies, waits for them, and re-layouts, local(): ordered = jnp.take(train_grads, module_order, axis=1)  2.93 us
    dot_general x1, matrix products, local(): jnp.einsum('gtv,qtv->gq', turned, asked, preferred_element_type=jnp.float32)  2.83 us
  transfers between devices with their start and end apart: 2, of which 1 were waited for; matrix products, arithmetic and copies ran while one was open for 18% of the time, Pallas kernels for 0%

commit v1 on v0

v1 whole, which is shorter than its diff:
```python
import functools
import math

import jax
import jax.numpy as jnp
from jax import lax
from jax.experimental import pallas as pl
from jax.experimental.pallas import tpu as pltpu
from jax.sharding import PartitionSpec as P

VMEM = pl.BlockSpec(memory_space=pltpu.VMEM)
SMEM = pl.BlockSpec(memory_space=pltpu.SMEM)
LANES = 128
PARAMS = pltpu.CompilerParams(vmem_limit_bytes=32 * 1024 * 1024)


def slots_kernel(order_ref, train_ref, *refs):
    outs, wide = refs[:-1], refs[-1]
    rows, modules, _ = train_ref.shape
    me = lax.axis_index("module")
    tiles = wide.shape[0] // (rows * modules)
    for e in range(rows):
        example = train_ref[e].astype(jnp.float32)
        for t in range(tiles):
            wide[pl.ds((t * rows + e) * modules, modules), :] = example[:, t * LANES : (t + 1) * LANES]
    for j, out in enumerate(outs):
        held = order_ref[me ^ j]
        for t in range(tiles):
            piece = wide[pl.ds(t * rows * modules + held, rows, stride=modules), :]
            out[:, t * LANES : (t + 1) * LANES] = piece.astype(out.dtype)


def by_slot(module_order, train_grads):
    rows, modules, width = train_grads.shape
    piece = jax.ShapeDtypeStruct((rows, width), train_grads.dtype)
    return pl.pallas_call(
        slots_kernel,
        out_shape=(piece,) * modules,
        in_specs=[SMEM, VMEM],
        out_specs=(VMEM,) * modules,
        scratch_shapes=[pltpu.VMEM((rows * modules * width // LANES, LANES), jnp.float32)],
        compiler_params=PARAMS,
    )(module_order, train_grads)


def rotator_kernel(out_ref, in_ref, rotator_ref):
    side = out_ref.shape[0]
    width = rotator_ref.shape[0]
    column = lax.broadcasted_iota(jnp.int32, (side, width), 1)
    row = lax.broadcasted_iota(jnp.int32, (side, width), 0)
    spread = (column // side == row).astype(jnp.bfloat16)
    tiled = (column % side == row).astype(jnp.bfloat16)
    outer = jnp.dot(out_ref[...], spread, preferred_element_type=jnp.float32)
    inner = jnp.dot(in_ref[...], tiled, preferred_element_type=jnp.float32)
    for a in range(side):
        rotator_ref[pl.ds(a * side, side), :] = (outer[a : a + 1, :] * inner).astype(jnp.bfloat16)


def rotator_of(basis_out, basis_in):
    width = basis_out.shape[0] ** 2
    return pl.pallas_call(
        rotator_kernel,
        out_shape=jax.ShapeDtypeStruct((width, width), jnp.bfloat16),
        in_specs=[VMEM, VMEM],
        out_specs=VMEM,
        compiler_params=PARAMS,
    )(basis_out, basis_in)


def turn_kernel(rotator_ref, *refs):
    count = len(refs) // 2
    for piece, turned in zip(refs[:count], refs[count:]):
        turned[...] = jnp.dot(
            piece[...], rotator_ref[...], preferred_element_type=jnp.float32
        ).astype(turned.dtype)


def turn(rotator, pieces):
    return pl.pallas_call(
        turn_kernel,
        out_shape=tuple(jax.ShapeDtypeStruct(p.shape, p.dtype) for p in pieces),
        in_specs=[VMEM] * (1 + len(pieces)),
        out_specs=(VMEM,) * len(pieces),
        compiler_params=PARAMS,
    )(rotator, *pieces)


def score_kernel(groups, factor, owners_ref, rotator_ref, values_ref, *refs):
    blocks, refs = refs[:groups], refs[groups:]
    queries, refs = refs[-1], refs[:-1]
    count = len(refs) // 2
    turned, outs = refs[:count], refs[count:]
    each = blocks[0].shape[0]
    me = lax.axis_index("group")
    for k in range(owners_ref.shape[0]):
        wanted = owners_ref[k] ^ me
        for b, block in enumerate(blocks):

            @pl.when(wanted == b)
            def _():
                queries[pl.ds(k * each, each), :] = block[...]

    values = values_ref[...]
    divisor = values + 0.1 * jnp.mean(values, axis=1, keepdims=True)
    asked = (
        jnp.dot(queries[...], rotator_ref[...], preferred_element_type=jnp.float32) / divisor
    ).astype(jnp.bfloat16)
    for piece, out in zip(turned, outs):
        out[...] = factor * lax.dot_general(
            piece[...], asked, (((1,), (1,)), ((), ())), preferred_element_type=jnp.float32
        )


def scores_of(owner_groups, rotator, eigenvalues, blocks, turned, factor):
    each, width = blocks[0].shape
    asked_rows = owner_groups.shape[0] * each
    return pl.pallas_call(
        functools.partial(score_kernel, len(blocks), factor),
        out_shape=tuple(
            jax.ShapeDtypeStruct((t.shape[0], asked_rows), jnp.float32) for t in turned
        ),
        in_specs=[SMEM] + [VMEM] * (2 + len(blocks) + len(turned)),
        out_specs=(VMEM,) * len(turned),
        scratch_shapes=[pltpu.VMEM((asked_rows, width), jnp.bfloat16)],
        compiler_params=PARAMS,
    )(owner_groups, rotator, eigenvalues, *blocks, *turned)


def swap(array, axis, bits):
    return lax.ppermute(array, axis, [(i, i ^ bits) for i in range(lax.axis_size(axis))])


def local(train_grads, query_grads, basis_out, basis_in, eigenvalues, owner_groups, module_order):
    _, modules, width = train_grads.shape
    groups = lax.axis_size("group")
    inner = 1 << ((groups.bit_length() - 1) // 2)
    own = query_grads.reshape(-1, width)
    blocks = [None] * groups
    for far in reversed(range(0, groups, inner)):
        blocks[far] = swap(own, "group", far) if far else own
    pieces = by_slot(module_order, train_grads)
    rotator = rotator_of(basis_out[0], basis_in[0])
    here = [pieces[0]] + [swap(pieces[j], "module", j) for j in range(1, modules)]
    turned = turn(rotator, here)
    for far in reversed(range(0, groups, inner)):
        for near in range(1, inner):
            blocks[far + near] = swap(blocks[far], "group", near)
    parts = scores_of(
        owner_groups, rotator, eigenvalues, blocks, turned, 1.0 / math.sqrt(modules * width)
    )
    total = parts[0]
    for j in range(1, modules):
        total = total + swap(parts[j], "module", j)
    return total


def solution(mesh):
    in_specs = (
        P(("group", "module"), None, None),
        P("group", None, "module", None),
        P("module", None, None),
        P("module", None, None),
        P("module", None),
        P(),
        P(),
    )
    out_specs = P(("group", "module"), None)
    return jax.shard_map(local, mesh=mesh, in_specs=in_specs, out_specs=out_specs, check_vma=False)
```

time: 102 us -> 31 us (0.30)
  blocking collectives: 33.3 us -> 0 us
  between operations: 14.2 us -> 0.13 us
  waiting for transfers between devices: 20.9 us -> 8 us
  local copies, waits for them, and re-layouts: 15.9 us -> 3.1 us
  starting transfers between devices: 4.24 us -> 14.4 us
  other arithmetic: 9.05 us -> 0.63 us
  Pallas kernels: 0 us -> 4.46 us
  matrix products: 3.6 us -> 0 us
    all_gather x1 -> x0, blocking collectives: 33.3 us -> none  [local(): everyone = lax.all_gather(query_grads, 'group', axis=0, tiled=True)]
    reduce_scatter x1 -> x0, waiting for transfers between devices: 20.9 us -> none  [local(): lax.psum_scatter(jnp.einsum('gtv,qtv->gq', turned, asked, preferred_eleme...]
    ppermute x0 -> x13, starting transfers between devices: none -> 14.4 us  [swap(): lax.ppermute(array, axis, [(i, i ^ bits) for i in range(lax.axis_size(axi...]
    convert_element_type x1 -> x0, local copies, waits for them, and re-layouts: 11.4 us -> none  [build_rotator(): product.reshape(basis_out.shape[:-2] + (breadth * breadth, breadth * brea...]
    ppermute x0 -> x13, waiting for transfers between devices: none -> 8 us  [swap(): lax.ppermute(array, axis, [(i, i ^ bits) for i in range(lax.axis_size(axi...]
    convert_element_type x1 -> x0, other arithmetic: 5.27 us -> none  [build_rotator(): product.reshape(basis_out.shape[:-2] + (breadth * breadth, breadth * brea...]
    pallas_call x0 -> x4, Pallas kernels: none -> 4.46 us  [the longest x1 1.57 us: turn(): pl.pallas_call(turn_kernel, out_shape=tuple((jax.ShapeDtypeStruct(p.shape...]
    all_to_all x1 -> x0, starting transfers between devices: 4.24 us -> none  [local(): lax.all_to_all(ordered.reshape(ex_rows, module_devices, slots_dev, width)...]
  transfers between devices with their start and end apart: 2 -> 13, of which waited for: 1 -> 4; matrix products, arithmetic and copies ran while one was open for 18% -> 0% of each run, Pallas kernels for 0% -> 10%
where the time goes in v1:
time: 31 us; the launch traced here: 30.7 us
  starting transfers between devices  14.4 us (46%)
  waiting for transfers between devices  8 us (26%)
  Pallas kernels  4.46 us (14%)
  local copies, waits for them, and re-layouts  3.1 us (10%)
  other arithmetic  0.63 us (2%)
    ppermute x13, starting transfers between devices, swap(): lax.ppermute(array, axis, [(i, i ^ bits) for i in range(lax.axis_size(axi...  14.4 us
    ppermute x13, waiting for transfers between devices, swap(): lax.ppermute(array, axis, [(i, i ^ bits) for i in range(lax.axis_size(axi...  8 us
    unnamed x14, local copies, waits for them, and re-layouts  3.1 us
    pallas_call x1, Pallas kernels, turn(): pl.pallas_call(turn_kernel, out_shape=tuple((jax.ShapeDtypeStruct(p.shape...  1.57 us
    pallas_call x1, Pallas kernels, scores_of(): pl.pallas_call(functools.partial(score_kernel, len(blocks), factor), out_...  1.53 us
    pallas_call x1, Pallas kernels, by_slot(): pl.pallas_call(slots_kernel, out_shape=(piece,) * modules, in_specs=[SMEM...  0.81 us
    add x1, other arithmetic, local(): total = total + swap(parts[j], 'module', j)  0.63 us
  transfers between devices with their start and end apart: 13, of which 4 were waited for; matrix products, arithmetic and copies ran while one was open for 0% of the time, Pallas kernels for 10%

profile of v1, /device:TPU:0, one launch (start us, length us, event | category | flops | bytes accessed | tf_op | source)
XLA Modules:
  0.0 30.7 jit_solution(6958836033081273154)
XLA Ops:
  0.0 3.0 %collective-permute-start.1 = (bf16[32,1024]{1,0:T(8,128)(2,1)}, bf16[32,1024]{1,0:T(8,128)(2,1)S(1)}, u32[]{:S(2)}, u32[]{:S(2)}) collective-permute-start(bf16[32,1024]{1,0:T(8,128)(2,1)} %bitcast.3), channel_id=1, source_target_pairs={{0,8},{4,12},{8,0},{12,4},{16,24},{20,28},{24,16},{28,20},{1,9},{5... | collective-permute-start | bytes 196616 | tf_op jit(solution)/shard_map/ppermute | solution.py:130
  3.0 0.0 copy-start
  3.0 1.0 %copy-done = bf16[64,4,1024]{2,1,0:T(4,128)(2,1)S(1)} copy-done((bf16[64,4,1024]{2,1,0:T(4,128)(2,1)S(1)}, bf16[64,4,1024]{2,1,0:T(4,128)(2,1)}, u32[]{:S(2)}) %copy-start) | copy-done | bytes 524312
  4.1 0.0 copy-start.5
  4.1 0.7 %copy-done.5 = s32[4]{0:T(128)S(1)} copy-done((s32[4]{0:T(128)S(1)}, s32[4]{0:T(128)}, u32[]{:S(2)}) %copy-start.5) | copy-done | bytes 40
  4.7 0.8 %shard_map.74 = (bf16[64,1024]{1,0:T(8,128)(2,1)S(1)}, bf16[64,1024]{1,0:T(8,128)(2,1)S(1)}, bf16[64,1024]{1,0:T(8,128)(2,1)S(1)}, bf16[64,1024]{1,0:T(8,128)(2,1)S(1)}) custom-call(s32[4]{0:T(128)S(1)} %copy-done.5, bf16[64,4,1024]{2,1,0:T(4,128)(2,1)S(1)} %copy-done), custom_call_target="tpu_custom_call" | custom-call | tf_op jit(solution)/shard_map/pallas_call | solution.py:36
  5.5 0.1 collective-permute-start.7
  5.6 1.6 %collective-permute-start.8 = (bf16[64,1024]{1,0:T(8,128)(2,1)S(1)}, bf16[64,1024]{1,0:T(8,128)(2,1)S(1)}, u32[]{:S(2)}, u32[]{:S(2)}) collective-permute-start(bf16[64,1024]{1,0:T(8,128)(2,1)S(1)} %get-tuple-element.19), channel_id=1, source_target_pairs={{0,2},{1,3},{2,0},{3,1},{4,6},{5,7},{6,4},{7,5},{8,10},{9,11},{10,... | collective-permute-start | bytes 393224 | tf_op jit(solution)/shard_map/ppermute | solution.py:130
  7.2 2.6 %collective-permute-start.3 = (bf16[32,1024]{1,0:T(8,128)(2,1)}, bf16[32,1024]{1,0:T(8,128)(2,1)S(1)}, u32[]{:S(2)}, u32[]{:S(2)}) collective-permute-start(bf16[32,1024]{1,0:T(8,128)(2,1)} %bitcast.4), channel_id=1, source_target_pairs={{0,16},{4,20},{8,24},{12,28},{16,0},{20,4},{24,8},{28,12},{1,17},{... | collective-permute-start | bytes 196616 | tf_op jit(solution)/shard_map/ppermute | solution.py:130
  9.8 0.0 collective-permute-start.9
  9.8 0.0 collective-permute-done.1.refs_2_
  9.8 0.2 collective-permute-start.5
  10.0 3.8 %collective-permute-done.3.refs_4_ = bf16[32,1024]{1,0:T(8,128)(2,1)S(1)} collective-permute-done((bf16[32,1024]{1,0:T(8,128)(2,1)}, bf16[32,1024]{1,0:T(8,128)(2,1)S(1)}, u32[]{:S(2)}, u32[]{:S(2)}) %collective-permute-start.3) | collective-permute-done | bytes 65568 | tf_op jit(solution)/shard_map/ppermute | solution.py:130
  13.9 1.5 %collective-permute-start = (bf16[32,1024]{1,0:T(8,128)(2,1)}, bf16[32,1024]{1,0:T(8,128)(2,1)S(1)}, u32[]{:S(2)}, u32[]{:S(2)}) collective-permute-start(bf16[32,1024]{1,0:T(8,128)(2,1)} %bitcast.6), channel_id=1, source_target_pairs={{0,4},{4,0},{8,12},{12,8},{16,20},{20,16},{24,28},{28,24},{1,5},{5... | collective-permute-start | bytes 196616 | tf_op jit(solution)/shard_map/ppermute | solution.py:130
  15.4 1.2 %collective-permute-done.5.refs_6_ = bf16[32,1024]{1,0:T(8,128)(2,1)S(1)} collective-permute-done((bf16[32,1024]{1,0:T(8,128)(2,1)}, bf16[32,1024]{1,0:T(8,128)(2,1)S(1)}, u32[]{:S(2)}, u32[]{:S(2)}) %collective-permute-start.5) | collective-permute-done | bytes 65568 | tf_op jit(solution)/shard_map/ppermute | solution.py:130
  16.5 1.5 %collective-permute-start.2 = (bf16[32,1024]{1,0:T(8,128)(2,1)S(1)}, bf16[32,1024]{1,0:T(8,128)(2,1)S(1)}, u32[]{:S(2)}, u32[]{:S(2)}) collective-permute-start(bf16[32,1024]{1,0:T(8,128)(2,1)S(1)} %collective-permute-done.1.refs_2_), channel_id=1, source_target_pairs={{0,4},{4,0},{8,12},{12,8},{16,20},{20,16},{24,28},{28,24},{1,5},{5... | collective-permute-start | bytes 196616 | tf_op jit(solution)/shard_map/ppermute | solution.py:130
  18.0 0.0 collective-permute-done.7.refs_1_
  18.0 0.5 %collective-permute-start.4 = (bf16[32,1024]{1,0:T(8,128)(2,1)S(1)}, bf16[32,1024]{1,0:T(8,128)(2,1)S(1)}, u32[]{:S(2)}, u32[]{:S(2)}) collective-permute-start(bf16[32,1024]{1,0:T(8,128)(2,1)S(1)} %collective-permute-done.3.refs_4_), channel_id=1, source_target_pairs={{0,4},{4,0},{8,12},{12,8},{16,20},{20,16},{24,28},{28,24},{1,5},{5... | collective-permute-start | bytes 196616 | tf_op jit(solution)/shard_map/ppermute | solution.py:130
  18.6 0.0 collective-permute-done.8.refs_2_
  18.6 1.5 %collective-permute-start.6 = (bf16[32,1024]{1,0:T(8,128)(2,1)S(1)}, bf16[32,1024]{1,0:T(8,128)(2,1)S(1)}, u32[]{:S(2)}, u32[]{:S(2)}) collective-permute-start(bf16[32,1024]{1,0:T(8,128)(2,1)S(1)} %collective-permute-done.5.refs_6_), channel_id=1, source_target_pairs={{0,4},{4,0},{8,12},{12,8},{16,20},{20,16},{24,28},{28,24},{1,5},{5... | collective-permute-start | bytes 196616 | tf_op jit(solution)/shard_map/ppermute | solution.py:130
  20.1 0.0 copy-start.2
  20.1 0.7 %copy-done.2 = bf16[1,32,32]{2,1,0:T(8,128)(2,1)S(1)} copy-done((bf16[1,32,32]{2,1,0:T(8,128)(2,1)S(1)}, bf16[1,32,32]{2,1,0:T(8,128)(2,1)}, u32[]{:S(2)}) %copy-start.2) | copy-done | bytes 2072
  20.8 0.0 copy-start.3
  20.8 0.7 %copy-done.3 = bf16[1,32,32]{2,1,0:T(8,128)(2,1)S(1)} copy-done((bf16[1,32,32]{2,1,0:T(8,128)(2,1)S(1)}, bf16[1,32,32]{2,1,0:T(8,128)(2,1)}, u32[]{:S(2)}) %copy-start.3) | copy-done | bytes 2072
  21.5 0.0 copy-start.1
  21.5 0.0 copy-start.4
  21.5 0.0 copy-start.6
  21.5 0.5 %shard_map.73.rotator_ref = bf16[1024,1024]{1,0:T(8,128)(2,1)S(1)} custom-call(bf16[32,32]{1,0:T(8,128)(2,1)S(1)} %bitcast.8, bf16[32,32]{1,0:T(8,128)(2,1)S(1)} %bitcast.9), custom_call_target="tpu_custom_call" | custom-call | tf_op jit(solution)/shard_map/pallas_call | solution.py:61
  22.0 0.0 collective-permute-done.9.refs_3_
  22.0 1.6 %shard_map.75 = (bf16[64,1024]{1,0:T(8,128)(2,1)S(1)}, bf16[64,1024]{1,0:T(8,128)(2,1)S(1)}, bf16[64,1024]{1,0:T(8,128)(2,1)S(1)}, bf16[64,1024]{1,0:T(8,128)(2,1)S(1)}) custom-call(bf16[1024,1024]{1,0:T(8,128)(2,1)S(1)} %shard_map.73.rotator_ref, bf16[64,1024]{1,0:T(8,128)(2,1)S(1)} %get-tuple-element.17.refs_0_, ...), custom_call_target="tpu_custom_call" | custom-call | tf_op jit(solution)/shard_map/pallas_call | solution.py:79
  23.6 0.0 collective-permute-done.refs_1_
  23.6 0.0 collective-permute-done.2.refs_3_
  23.6 0.0 collective-permute-done.4.refs_5_
  23.6 0.0 collective-permute-done.6.refs_7_
  23.6 0.0 copy-done.1
  23.7 0.0 copy-done.4
  23.7 0.0 copy-done.6
  23.7 1.5 %shard_map.76 = (f32[64,128]{1,0:T(8,128)S(1)}, f32[64,128]{1,0:T(8,128)S(1)}, f32[64,128]{1,0:T(8,128)S(1)}, f32[64,128]{1,0:T(8,128)S(1)}) custom-call(s32[4]{0:T(128)S(1)} %copy-done.6, bf16[1024,1024]{1,0:T(8,128)(2,1)S(1)} %shard_map.73.rotator_ref, f32[1,1024]{1,0:T(1,128)S(1)} %copy-done.4, bf16[32,1024]{1,0:T(8,128)(2,1)S(1)} %bitcast.7, ...), custom_call_target="tpu_custom_call" | custom-call | tf_op jit(solution)/shard_map/pallas_call | solution.py:117
  25.2 0.1 collective-permute-start.10
  25.3 1.5 %collective-permute-start.11 = (f32[64,128]{1,0:T(8,128)S(1)}, f32[64,128]{1,0:T(8,128)S(1)}, u32[]{:S(2)}, u32[]{:S(2)}) collective-permute-start(f32[64,128]{1,0:T(8,128)S(1)} %get-tuple-element.27), channel_id=1, source_target_pairs={{0,2},{1,3},{2,0},{3,1},{4,6},{5,7},{6,4},{7,5},{8,10},{9,11},{10,... | collective-permute-start | bytes 98312 | tf_op jit(solution)/shard_map/ppermute | solution.py:130
  26.8 0.4 %collective-permute-start.12 = (f32[64,128]{1,0:T(8,128)S(1)}, f32[64,128]{1,0:T(8,128)S(1)}, u32[]{:S(2)}, u32[]{:S(2)}) collective-permute-start(f32[64,128]{1,0:T(8,128)S(1)} %get-tuple-element.28), channel_id=1, source_target_pairs={{0,3},{1,2},{2,1},{3,0},{4,7},{5,6},{6,5},{7,4},{8,11},{9,10},{10,... | collective-permute-start | bytes 98312 | tf_op jit(solution)/shard_map/ppermute | solution.py:130
  27.2 0.0 collective-permute-done.10
  27.2 2.1 %collective-permute-done.11 = f32[64,128]{1,0:T(8,128)S(1)} collective-permute-done((f32[64,128]{1,0:T(8,128)S(1)}, f32[64,128]{1,0:T(8,128)S(1)}, u32[]{:S(2)}, u32[]{:S(2)}) %collective-permute-start.11) | collective-permute-done | bytes 32800 | tf_op jit(solution)/shard_map/ppermute | solution.py:130
  29.3 0.8 %collective-permute-done.12 = f32[64,128]{1,0:T(8,128)S(1)} collective-permute-done((f32[64,128]{1,0:T(8,128)S(1)}, f32[64,128]{1,0:T(8,128)S(1)}, u32[]{:S(2)}, u32[]{:S(2)}) %collective-permute-start.12) | collective-permute-done | bytes 32800 | tf_op jit(solution)/shard_map/ppermute | solution.py:130
  30.1 0.6 %add_add_fusion = f32[64,128]{1,0:T(8,128)} fusion(f32[64,128]{1,0:T(8,128)S(1)} %collective-permute-done.12, f32[64,128]{1,0:T(8,128)S(1)} %collective-permute-done.11, f32[64,128]{1,0:T(8,128)S(1)} %get-tuple-element.25, f32[64,128]{1,0:T(8,128)S(1)} %collective-permute-done.10), kind=kLoop, calls=%fused_computation | loop fusion | flops 24576 | bytes 163840 | tf_op jit(solution)/shard_map/add | solution.py:153
Async XLA Ops:
  0.0 9.8 %collective-permute-start.1 = (bf16[32,1024]{1,0:T(8,128)(2,1)}, bf16[32,1024]{1,0:T(8,128)(2,1)S(1)}, u32[]{:S(2)}, u32[]{:S(2)}) collective-permute-start(bf16[32,1024]{1,0:T(8,128)(2,1)} %bitcast.3), channel_id=1, source_target_pairs={{0,8},{4,12},{8,0},{12,4},{16,24},{20,28},{24,16},{28,20},{1,9},{5... | collective-permute-start | bytes 196616 | tf_op jit(solution)/shard_map/ppermute | solution.py:130
  3.0 1.0 %copy-start = (bf16[64,4,1024]{2,1,0:T(4,128)(2,1)S(1)}, bf16[64,4,1024]{2,1,0:T(4,128)(2,1)}, u32[]{:S(2)}) copy-start(bf16[64,4,1024]{2,1,0:T(4,128)(2,1)} %train_ref.1) | copy-start | bytes 1572868
  4.1 0.7 %copy-start.5 = (s32[4]{0:T(128)S(1)}, s32[4]{0:T(128)}, u32[]{:S(2)}) copy-start(s32[4]{0:T(128)} %order_ref.1) | copy-start | bytes 52
  5.5 12.5 %collective-permute-start.7 = (bf16[64,1024]{1,0:T(8,128)(2,1)S(1)}, bf16[64,1024]{1,0:T(8,128)(2,1)S(1)}, u32[]{:S(2)}, u32[]{:S(2)}) collective-permute-start(bf16[64,1024]{1,0:T(8,128)(2,1)S(1)} %get-tuple-element.18), channel_id=1, source_target_pairs={{0,1},{1,0},{2,3},{3,2},{4,5},{5,4},{6,7},{7,6},{8,9},{9,8},{10,11... | collective-permute-start | bytes 393224 | tf_op jit(solution)/shard_map/ppermute | solution.py:130
  5.6 12.9 %collective-permute-start.8 = (bf16[64,1024]{1,0:T(8,128)(2,1)S(1)}, bf16[64,1024]{1,0:T(8,128)(2,1)S(1)}, u32[]{:S(2)}, u32[]{:S(2)}) collective-permute-start(bf16[64,1024]{1,0:T(8,128)(2,1)S(1)} %get-tuple-element.19), channel_id=1, source_target_pairs={{0,2},{1,3},{2,0},{3,1},{4,6},{5,7},{6,4},{7,5},{8,10},{9,11},{10,... | collective-permute-start | bytes 393224 | tf_op jit(solution)/shard_map/ppermute | solution.py:130
  7.2 6.7 %collective-permute-start.3 = (bf16[32,1024]{1,0:T(8,128)(2,1)}, bf16[32,1024]{1,0:T(8,128)(2,1)S(1)}, u32[]{:S(2)}, u32[]{:S(2)}) collective-permute-start(bf16[32,1024]{1,0:T(8,128)(2,1)} %bitcast.4), channel_id=1, source_target_pairs={{0,16},{4,20},{8,24},{12,28},{16,0},{20,4},{24,8},{28,12},{1,17},{... | collective-permute-start | bytes 196616 | tf_op jit(solution)/shard_map/ppermute | solution.py:130
  9.8 12.2 %collective-permute-start.9 = (bf16[64,1024]{1,0:T(8,128)(2,1)S(1)}, bf16[64,1024]{1,0:T(8,128)(2,1)S(1)}, u32[]{:S(2)}, u32[]{:S(2)}) collective-permute-start(bf16[64,1024]{1,0:T(8,128)(2,1)S(1)} %get-tuple-element.20), channel_id=1, source_target_pairs={{0,3},{1,2},{2,1},{3,0},{4,7},{5,6},{6,5},{7,4},{8,11},{9,10},{10,... | collective-permute-start | bytes 393224 | tf_op jit(solution)/shard_map/ppermute | solution.py:130
  9.8 6.7 %collective-permute-start.5 = (bf16[32,1024]{1,0:T(8,128)(2,1)}, bf16[32,1024]{1,0:T(8,128)(2,1)S(1)}, u32[]{:S(2)}, u32[]{:S(2)}) collective-permute-start(bf16[32,1024]{1,0:T(8,128)(2,1)} %bitcast.5), channel_id=1, source_target_pairs={{0,24},{4,28},{8,16},{12,20},{16,8},{20,12},{24,0},{28,4},{1,25},{... | collective-permute-start | bytes 196616 | tf_op jit(solution)/shard_map/ppermute | solution.py:130
  13.9 9.7 %collective-permute-start = (bf16[32,1024]{1,0:T(8,128)(2,1)}, bf16[32,1024]{1,0:T(8,128)(2,1)S(1)}, u32[]{:S(2)}, u32[]{:S(2)}) collective-permute-start(bf16[32,1024]{1,0:T(8,128)(2,1)} %bitcast.6), channel_id=1, source_target_pairs={{0,4},{4,0},{8,12},{12,8},{16,20},{20,16},{24,28},{28,24},{1,5},{5... | collective-permute-start | bytes 196616 | tf_op jit(solution)/shard_map/ppermute | solution.py:130
  16.5 7.1 %collective-permute-start.2 = (bf16[32,1024]{1,0:T(8,128)(2,1)S(1)}, bf16[32,1024]{1,0:T(8,128)(2,1)S(1)}, u32[]{:S(2)}, u32[]{:S(2)}) collective-permute-start(bf16[32,1024]{1,0:T(8,128)(2,1)S(1)} %collective-permute-done.1.refs_2_), channel_id=1, source_target_pairs={{0,4},{4,0},{8,12},{12,8},{16,20},{20,16},{24,28},{28,24},{1,5},{5... | collective-permute-start | bytes 196616 | tf_op jit(solution)/shard_map/ppermute | solution.py:130
  18.0 5.6 %collective-permute-start.4 = (bf16[32,1024]{1,0:T(8,128)(2,1)S(1)}, bf16[32,1024]{1,0:T(8,128)(2,1)S(1)}, u32[]{:S(2)}, u32[]{:S(2)}) collective-permute-start(bf16[32,1024]{1,0:T(8,128)(2,1)S(1)} %collective-permute-done.3.refs_4_), channel_id=1, source_target_pairs={{0,4},{4,0},{8,12},{12,8},{16,20},{20,16},{24,28},{28,24},{1,5},{5... | collective-permute-start | bytes 196616 | tf_op jit(solution)/shard_map/ppermute | solution.py:130
  18.6 5.1 %collective-permute-start.6 = (bf16[32,1024]{1,0:T(8,128)(2,1)S(1)}, bf16[32,1024]{1,0:T(8,128)(2,1)S(1)}, u32[]{:S(2)}, u32[]{:S(2)}) collective-permute-start(bf16[32,1024]{1,0:T(8,128)(2,1)S(1)} %collective-permute-done.5.refs_6_), channel_id=1, source_target_pairs={{0,4},{4,0},{8,12},{12,8},{16,20},{20,16},{24,28},{28,24},{1,5},{5... | collective-permute-start | bytes 196616 | tf_op jit(solution)/shard_map/ppermute | solution.py:130
  20.1 0.7 %copy-start.2 = (bf16[1,32,32]{2,1,0:T(8,128)(2,1)S(1)}, bf16[1,32,32]{2,1,0:T(8,128)(2,1)}, u32[]{:S(2)}) copy-start(bf16[1,32,32]{2,1,0:T(8,128)(2,1)} %param.9) | copy-start | bytes 6148
  20.8 0.7 %copy-start.3 = (bf16[1,32,32]{2,1,0:T(8,128)(2,1)S(1)}, bf16[1,32,32]{2,1,0:T(8,128)(2,1)}, u32[]{:S(2)}) copy-start(bf16[1,32,32]{2,1,0:T(8,128)(2,1)} %param.10) | copy-start | bytes 6148
  21.5 2.2 %copy-start.1 = (bf16[1,32,1,1024]{3,1,2,0:T(8,128)(2,1)S(1)}, bf16[1,32,1,1024]{3,1,2,0:T(8,128)(2,1)}, u32[]{:S(2)}) copy-start(bf16[1,32,1,1024]{3,1,2,0:T(8,128)(2,1)} %param.8) | copy-start | bytes 196612
  21.5 2.2 %copy-start.4 = (f32[1,1024]{1,0:T(1,128)S(1)}, f32[1,1024]{1,0:T(1,128)}, u32[]{:S(2)}) copy-start(f32[1,1024]{1,0:T(1,128)} %values_ref.1) | copy-start | bytes 12292
  21.5 2.2 %copy-start.6 = (s32[4]{0:T(128)S(1)}, s32[4]{0:T(128)}, u32[]{:S(2)}) copy-start(s32[4]{0:T(128)} %owners_ref.1) | copy-start | bytes 52
  25.2 1.9 %collective-permute-start.10 = (f32[64,128]{1,0:T(8,128)S(1)}, f32[64,128]{1,0:T(8,128)S(1)}, u32[]{:S(2)}, u32[]{:S(2)}) collective-permute-start(f32[64,128]{1,0:T(8,128)S(1)} %get-tuple-element.26), channel_id=1, source_target_pairs={{0,1},{1,0},{2,3},{3,2},{4,5},{5,4},{6,7},{7,6},{8,9},{9,8},{10,11... | collective-permute-start | bytes 98312 | tf_op jit(solution)/shard_map/ppermute | solution.py:130
  25.3 4.0 %collective-permute-start.11 = (f32[64,128]{1,0:T(8,128)S(1)}, f32[64,128]{1,0:T(8,128)S(1)}, u32[]{:S(2)}, u32[]{:S(2)}) collective-permute-start(f32[64,128]{1,0:T(8,128)S(1)} %get-tuple-element.27), channel_id=1, source_target_pairs={{0,2},{1,3},{2,0},{3,1},{4,6},{5,7},{6,4},{7,5},{8,10},{9,11},{10,... | collective-permute-start | bytes 98312 | tf_op jit(solution)/shard_map/ppermute | solution.py:130
  26.8 3.3 %collective-permute-start.12 = (f32[64,128]{1,0:T(8,128)S(1)}, f32[64,128]{1,0:T(8,128)S(1)}, u32[]{:S(2)}, u32[]{:S(2)}) collective-permute-start(f32[64,128]{1,0:T(8,128)S(1)} %get-tuple-element.28), channel_id=1, source_target_pairs={{0,3},{1,2},{2,1},{3,0},{4,7},{5,6},{6,5},{7,4},{8,11},{9,10},{10,... | collective-permute-start | bytes 98312 | tf_op jit(solution)/shard_map/ppermute | solution.py:130

commit v2 on v1

v2 whole, which is shorter than its diff:
```python
import functools
import math

import jax
import jax.numpy as jnp
from jax import lax
from jax.experimental import pallas as pl
from jax.experimental.pallas import tpu as pltpu
from jax.sharding import PartitionSpec as P

VMEM = pl.BlockSpec(memory_space=pltpu.VMEM)
ANY = pl.BlockSpec(memory_space=pl.ANY)
SMEM = pl.BlockSpec(memory_space=pltpu.SMEM)
LANES = 128
def cost(us):
    return pl.CostEstimate(flops=0, bytes_accessed=int(us * 3.0e6), transcendentals=0)


PARAMS = pltpu.CompilerParams(vmem_limit_bytes=32 * 1024 * 1024)


def slots_kernel(order_hbm, train_hbm, *refs):
    outs, (order, train, wide, sems) = refs[:-4], refs[-4:]
    rows, modules, _ = train.shape
    tiles = wide.shape[0] // (rows * modules)
    loads = [
        pltpu.make_async_copy(order_hbm, order, sems.at[0]),
        pltpu.make_async_copy(train_hbm, train, sems.at[1]),
    ]
    for load in loads:
        load.start()
    for load in loads:
        load.wait()
    me = lax.axis_index("module")
    for e in range(rows):
        example = train[e].astype(jnp.float32)
        for t in range(tiles):
            wide[pl.ds((t * rows + e) * modules, modules), :] = example[:, t * LANES : (t + 1) * LANES]
    for j in range(modules):
        held = order[me ^ j]
        out, at = outs[j // 2], j % 2 * rows
        for t in range(tiles):
            piece = wide[pl.ds(t * rows * modules + held, rows, stride=modules), :]
            out[at : at + rows, t * LANES : (t + 1) * LANES] = piece.astype(out.dtype)


def by_slot(module_order, train_grads):
    rows, modules, width = train_grads.shape
    pair = jax.ShapeDtypeStruct((2 * rows, width), train_grads.dtype)
    shapes = (pair,) * (modules // 2)
    return pl.pallas_call(
        slots_kernel,
        out_shape=shapes,
        in_specs=[ANY, ANY],
        out_specs=(VMEM,) * len(shapes),
        scratch_shapes=[
            pltpu.SMEM(module_order.shape, jnp.int32),
            pltpu.VMEM(train_grads.shape, train_grads.dtype),
            pltpu.VMEM((rows * modules * width // LANES, LANES), jnp.float32),
            pltpu.SemaphoreType.DMA((2,)),
        ],
        compiler_params=PARAMS,
        cost_estimate=cost(0.8),
    )(module_order, train_grads)


def rotator_kernel(out_hbm, in_hbm, rotator_ref, out_ref, in_ref, sems):
    side = out_ref.shape[0]
    width = rotator_ref.shape[0]
    loads = [
        pltpu.make_async_copy(out_hbm, out_ref, sems.at[0]),
        pltpu.make_async_copy(in_hbm, in_ref, sems.at[1]),
    ]
    for load in loads:
        load.start()
    column = lax.broadcasted_iota(jnp.int32, (side, width), 1)
    row = lax.broadcasted_iota(jnp.int32, (side, width), 0)
    spread = (column // side == row).astype(jnp.bfloat16)
    tiled = (column % side == row).astype(jnp.bfloat16)
    for load in loads:
        load.wait()
    outer = jnp.dot(out_ref[...], spread, preferred_element_type=jnp.float32)
    inner = jnp.dot(in_ref[...], tiled, preferred_element_type=jnp.float32)
    for a in range(side):
        rotator_ref[pl.ds(a * side, side), :] = (outer[a : a + 1, :] * inner).astype(jnp.bfloat16)


def rotator_of(basis_out, basis_in):
    width = basis_out.shape[0] ** 2
    return pl.pallas_call(
        rotator_kernel,
        out_shape=jax.ShapeDtypeStruct((width, width), jnp.bfloat16),
        in_specs=[ANY, ANY],
        out_specs=VMEM,
        scratch_shapes=[
            pltpu.VMEM(basis_out.shape, basis_out.dtype),
            pltpu.VMEM(basis_in.shape, basis_in.dtype),
            pltpu.SemaphoreType.DMA((2,)),
        ],
        compiler_params=PARAMS,
        cost_estimate=cost(0.5),
    )(basis_out, basis_in)


def precondition_kernel(groups, owners_ref, rotator_ref, values_ref, *refs):
    blocks, (out, queries) = refs[:groups], refs[groups:]
    each = blocks[0].shape[0]
    me = lax.axis_index("group")
    for k in range(owners_ref.shape[0]):
        wanted = owners_ref[k] ^ me
        for b, block in enumerate(blocks):

            @pl.when(wanted == b)
            def _():
                queries[pl.ds(k * each, each), :] = block[...]

    values = values_ref[...]
    divisor = values + 0.1 * jnp.mean(values, axis=1, keepdims=True)
    asked = jnp.dot(queries[...], rotator_ref[...], preferred_element_type=jnp.float32) / divisor
    out[...] = lax.dot_general(
        asked.astype(jnp.bfloat16),
        rotator_ref[...],
        (((1,), (1,)), ((), ())),
        preferred_element_type=jnp.float32,
    ).astype(out.dtype)


def precondition(owner_groups, rotator, eigenvalues, blocks):
    each, width = blocks[0].shape
    rows = owner_groups.shape[0] * each
    return pl.pallas_call(
        functools.partial(precondition_kernel, len(blocks)),
        out_shape=jax.ShapeDtypeStruct((rows, width), jnp.bfloat16),
        in_specs=[SMEM] + [VMEM] * (2 + len(blocks)),
        out_specs=VMEM,
        scratch_shapes=[pltpu.VMEM((rows, width), jnp.bfloat16)],
        compiler_params=PARAMS,
        cost_estimate=cost(2.0),
    )(owner_groups, rotator, eigenvalues, *blocks)


def score_kernel(factor, mine_ref, other_ref, *refs):
    count = len(refs) // 2
    for pair, out in zip(refs[:count], refs[count:]):
        rows = out.shape[0]
        total = 0.0
        for half, asked in enumerate((mine_ref, other_ref)):
            total += lax.dot_general(
                pair[half * rows : (half + 1) * rows, :],
                asked[...],
                (((1,), (1,)), ((), ())),
                preferred_element_type=jnp.float32,
            )
        out[...] = factor * total


def score(mine, other, pairs, factor):
    part = jax.ShapeDtypeStruct((pairs[0].shape[0] // 2, mine.shape[0]), jnp.float32)
    return pl.pallas_call(
        functools.partial(score_kernel, factor),
        out_shape=(part,) * len(pairs),
        in_specs=[VMEM] * (2 + len(pairs)),
        out_specs=(VMEM,) * len(pairs),
        compiler_params=PARAMS,
        cost_estimate=cost(0.7),
    )(mine, other, *pairs)


def swap(array, axis, bits):
    return lax.ppermute(array, axis, [(i, i ^ bits) for i in range(lax.axis_size(axis))])


def after(array, *others):
    return lax.optimization_barrier((array,) + others)[0]


def local(train_grads, query_grads, basis_out, basis_in, eigenvalues, owner_groups, module_order):
    _, modules, width = train_grads.shape
    groups = lax.axis_size("group")
    inner = 1 << ((groups.bit_length() - 1) // 2)
    own = query_grads.reshape(-1, width)
    blocks = [None] * groups
    for far in reversed(range(inner, groups, inner)):
        blocks[far] = swap(own, "group", far)
    first = blocks[inner]
    blocks[0] = after(own, first)
    pairs = by_slot(module_order, after(train_grads, first))
    pairs = [pairs[0]] + [swap(pairs[j], "module", 2 * j) for j in range(1, modules // 2)]
    rotator = rotator_of(after(basis_out[0], first), basis_in[0])
    for far in range(0, groups, inner):
        if far > inner:
            blocks[far] = after(blocks[far], rotator)
        for near in range(1, inner):
            blocks[far + near] = swap(blocks[far], "group", near)
    mine = precondition(owner_groups, rotator, eigenvalues, blocks)
    other = swap(mine, "module", 1)
    parts = score(mine, other, pairs, 1.0 / math.sqrt(modules * width))
    total = parts[0]
    for j in range(1, modules // 2):
        total = total + swap(parts[j], "module", 2 * j)
    return total


def solution(mesh):
    in_specs = (
        P(("group", "module"), None, None),
        P("group", None, "module", None),
        P("module", None, None),
        P("module", None, None),
        P("module", None),
        P(),
        P(),
    )
    out_specs = P(("group", "module"), None)
    return jax.shard_map(local, mesh=mesh, in_specs=in_specs, out_specs=out_specs, check_vma=False)
```

time: 31 us -> 28.1 us (0.906)
  local copies, waits for them, and re-layouts: 3.1 us -> 1.41 us
  Pallas kernels: 4.46 us -> 3.73 us
  starting transfers between devices: 14.4 us -> 13.8 us
    unnamed x14, local copies, waits for them, and re-layouts: 3.1 us -> 1.41 us
    pallas_call x3, Pallas kernels: 3.91 us -> 3.14 us  [the longest x1 1.84 us: precondition(): pl.pallas_call(functools.partial(precondition_kernel, len(blocks)), out_s...]
    ppermute x13 -> x10, starting transfers between devices: 14.4 us -> 13.8 us  [swap(): lax.ppermute(array, axis, [(i, i ^ bits) for i in range(lax.axis_size(axi...]
    ppermute x13 -> x10, waiting for transfers between devices: 8 us -> 8.2 us  [swap(): lax.ppermute(array, axis, [(i, i ^ bits) for i in range(lax.axis_size(axi...]
  transfers between devices with their start and end apart: 13 -> 10, of which waited for: 4 -> 4; matrix products, arithmetic and copies ran while one was open for 0% -> 0% of each run, Pallas kernels for 10% -> 12%
where the time goes in v2:
time: 28.1 us; the launch traced here: 27.8 us
  starting transfers between devices  13.8 us (49%)
  waiting for transfers between devices  8.2 us (29%)
  Pallas kernels  3.73 us (13%)
  local copies, waits for them, and re-layouts  1.41 us (5%)
  other arithmetic  0.62 us (2%)
    ppermute x10, starting transfers between devices, swap(): lax.ppermute(array, axis, [(i, i ^ bits) for i in range(lax.axis_size(axi...  13.8 us
    ppermute x10, waiting for transfers between devices, swap(): lax.ppermute(array, axis, [(i, i ^ bits) for i in range(lax.axis_size(axi...  8.2 us
    pallas_call x1, Pallas kernels, precondition(): pl.pallas_call(functools.partial(precondition_kernel, len(blocks)), out_s...  1.84 us
    unnamed x14, local copies, waits for them, and re-layouts  1.41 us
    pallas_call x1, Pallas kernels, by_slot(): pl.pallas_call(slots_kernel, out_shape=shapes, in_specs=[ANY, ANY], out_s...  0.83 us
    add x1, other arithmetic, local(): total = total + swap(parts[j], 'module', 2 * j)  0.62 us
    pallas_call x1, Pallas kernels, rotator_of(): pl.pallas_call(rotator_kernel, out_shape=jax.ShapeDtypeStruct((width, wid...  0.6 us
  transfers between devices with their start and end apart: 10, of which 4 were waited for; matrix products, arithmetic and copies ran while one was open for 0% of the time, Pallas kernels for 12%

profile of v2, /device:TPU:0, one launch (start us, length us, event | category | flops | bytes accessed | tf_op | source)
XLA Modules:
  0.0 27.8 jit_solution(17740636121702847484)
XLA Ops:
  0.0 0.0 copy-start.1
  0.0 0.0 copy-start
  0.0 3.0 %collective-permute-start = (bf16[32,1024]{1,0:T(8,128)(2,1)}, bf16[32,1024]{1,0:T(8,128)(2,1)S(1)}, u32[]{:S(2)}, u32[]{:S(2)}) collective-permute-start(bf16[32,1024]{1,0:T(8,128)(2,1)} %bitcast.3), channel_id=1, source_target_pairs={{0,8},{4,12},{8,0},{12,4},{16,24},{20,28},{24,16},{28,20},{1,9},{5... | collective-permute-start | bytes 196616 | tf_op jit(solution)/shard_map/ppermute | solution.py:170
  3.0 2.6 %collective-permute-start.3 = (bf16[32,1024]{1,0:T(8,128)(2,1)}, bf16[32,1024]{1,0:T(8,128)(2,1)S(1)}, u32[]{:S(2)}, u32[]{:S(2)}) collective-permute-start(bf16[32,1024]{1,0:T(8,128)(2,1)} %bitcast.4), channel_id=1, source_target_pairs={{0,16},{4,20},{8,24},{12,28},{16,0},{20,4},{24,8},{28,12},{1,17},{... | collective-permute-start | bytes 196616 | tf_op jit(solution)/shard_map/ppermute | solution.py:170
  5.6 0.0 collective-permute-start.5
  5.6 0.0 collective-permute-done.refs_2_
  5.6 0.0 copy-start.2
  5.6 0.7 %copy-done.2 = bf16[1,32,32]{2,1,0:T(8,128)(2,1)S(1)} copy-done((bf16[1,32,32]{2,1,0:T(8,128)(2,1)S(1)}, bf16[1,32,32]{2,1,0:T(8,128)(2,1)}, u32[]{:S(2)}) %copy-start.2) | copy-done | bytes 2072
  6.3 0.0 copy-start.3
  6.3 0.7 %copy-done.3 = bf16[1,32,32]{2,1,0:T(8,128)(2,1)S(1)} copy-done((bf16[1,32,32]{2,1,0:T(8,128)(2,1)S(1)}, bf16[1,32,32]{2,1,0:T(8,128)(2,1)}, u32[]{:S(2)}) %copy-start.3) | copy-done | bytes 2072
  7.0 0.0 copy-start.5
  7.0 0.0 copy-start.4
  7.0 0.0 copy-start.6
  7.0 0.6 %shard_map.73.rotator_ref = bf16[1024,1024]{1,0:T(8,128)(2,1)S(1)} custom-call(bf16[32,32]{1,0:T(8,128)(2,1)S(1)} %bitcast.8, bf16[32,32]{1,0:T(8,128)(2,1)S(1)} %bitcast.9), custom_call_target="tpu_custom_call" | custom-call | bytes 1500000 | tf_op jit(solution)/shard_map/pallas_call | solution.py:90
  7.6 2.9 %collective-permute-done.3.refs_4_ = bf16[32,1024]{1,0:T(8,128)(2,1)S(1)} collective-permute-done((bf16[32,1024]{1,0:T(8,128)(2,1)}, bf16[32,1024]{1,0:T(8,128)(2,1)S(1)}, u32[]{:S(2)}, u32[]{:S(2)}) %collective-permute-start.3) | collective-permute-done | bytes 65568 | tf_op jit(solution)/shard_map/ppermute | solution.py:170
  10.5 1.5 %collective-permute-start.4 = (bf16[32,1024]{1,0:T(8,128)(2,1)S(1)}, bf16[32,1024]{1,0:T(8,128)(2,1)S(1)}, u32[]{:S(2)}, u32[]{:S(2)}) collective-permute-start(bf16[32,1024]{1,0:T(8,128)(2,1)S(1)} %collective-permute-done.3.refs_4_), channel_id=1, source_target_pairs={{0,4},{4,0},{8,12},{12,8},{16,20},{20,16},{24,28},{28,24},{1,5},{5... | collective-permute-start | bytes 196616 | tf_op jit(solution)/shard_map/ppermute | solution.py:170
  12.0 0.0 collective-permute-done.5.refs_6_
  12.0 1.4 %collective-permute-start.6 = (bf16[32,1024]{1,0:T(8,128)(2,1)S(1)}, bf16[32,1024]{1,0:T(8,128)(2,1)S(1)}, u32[]{:S(2)}, u32[]{:S(2)}) collective-permute-start(bf16[32,1024]{1,0:T(8,128)(2,1)S(1)} %collective-permute-done.5.refs_6_), channel_id=1, source_target_pairs={{0,4},{4,0},{8,12},{12,8},{16,20},{20,16},{24,28},{28,24},{1,5},{5... | collective-permute-start | bytes 196616 | tf_op jit(solution)/shard_map/ppermute | solution.py:170
  13.4 0.0 copy-done.1
  13.4 0.6 %collective-permute-start.1 = (bf16[32,1024]{1,0:T(8,128)(2,1)S(1)}, bf16[32,1024]{1,0:T(8,128)(2,1)S(1)}, u32[]{:S(2)}, u32[]{:S(2)}) collective-permute-start(bf16[32,1024]{1,0:T(8,128)(2,1)S(1)} %bitcast.6), channel_id=1, source_target_pairs={{0,4},{4,0},{8,12},{12,8},{16,20},{20,16},{24,28},{28,24},{1,5},{5... | collective-permute-start | bytes 196616 | tf_op jit(solution)/shard_map/ppermute | solution.py:170
  14.0 1.4 %collective-permute-start.2 = (bf16[32,1024]{1,0:T(8,128)(2,1)S(1)}, bf16[32,1024]{1,0:T(8,128)(2,1)S(1)}, u32[]{:S(2)}, u32[]{:S(2)}) collective-permute-start(bf16[32,1024]{1,0:T(8,128)(2,1)S(1)} %collective-permute-done.refs_2_), channel_id=1, source_target_pairs={{0,4},{4,0},{8,12},{12,8},{16,20},{20,16},{24,28},{28,24},{1,5},{5... | collective-permute-start | bytes 196616 | tf_op jit(solution)/shard_map/ppermute | solution.py:170
  15.4 0.0 copy-done
  15.4 0.0 copy-done.5
  15.4 0.8 %shard_map.75 = (bf16[128,1024]{1,0:T(8,128)(2,1)S(1)}, bf16[128,1024]{1,0:T(8,128)(2,1)S(1)}) custom-call(s32[4]{0:T(128)S(1)} %copy-done.5, bf16[64,4,1024]{2,1,0:T(4,128)(2,1)S(1)} %copy-done), custom_call_target="tpu_custom_call" | custom-call | bytes 2400000 | tf_op jit(solution)/shard_map/pallas_call | solution.py:51
  16.3 1.6 %collective-permute-start.8 = (bf16[128,1024]{1,0:T(8,128)(2,1)S(1)}, bf16[128,1024]{1,0:T(8,128)(2,1)S(1)}, u32[]{:S(2)}, u32[]{:S(2)}) collective-permute-start(bf16[128,1024]{1,0:T(8,128)(2,1)S(1)} %get-tuple-element.20), channel_id=1, source_target_pairs={{0,2},{1,3},{2,0},{3,1},{4,6},{5,7},{6,4},{7,5},{8,10},{9,11},{10,... | collective-permute-start | bytes 786440 | tf_op jit(solution)/shard_map/ppermute | solution.py:170
  17.9 0.0 collective-permute-done.4.refs_5_
  17.9 0.0 collective-permute-done.6.refs_7_
  17.9 0.0 collective-permute-done.1.refs_1_
  17.9 0.5 %collective-permute-done.2.refs_3_ = bf16[32,1024]{1,0:T(8,128)(2,1)S(1)} collective-permute-done((bf16[32,1024]{1,0:T(8,128)(2,1)S(1)}, bf16[32,1024]{1,0:T(8,128)(2,1)S(1)}, u32[]{:S(2)}, u32[]{:S(2)}) %collective-permute-start.2) | collective-permute-done | bytes 65568 | tf_op jit(solution)/shard_map/ppermute | solution.py:170
  18.4 0.0 copy-done.4
  18.4 0.0 copy-done.6
  18.4 1.8 %shard_map.74.mine_ref = bf16[128,1024]{1,0:T(8,128)(2,1)S(1)} custom-call(s32[4]{0:T(128)S(1)} %copy-done.6, bf16[1024,1024]{1,0:T(8,128)(2,1)S(1)} %shard_map.73.rotator_ref, f32[1,1024]{1,0:T(1,128)S(1)} %copy-done.4, bf16[32,1024]{1,0:T(8,128)(2,1)S(1)} %bitcast.7, bf16[32,1024]{1,0:T(8,128)(2,1)S(1)} %collective-permute-done.1.refs_1_, ...), custom_call_target="tpu_custom_call" | custom-call | bytes 6000000 | tf_op jit(solution)/shard_map/pallas_call | solution.py:131
  20.2 0.1 collective-permute-start.7
  20.3 2.4 %collective-permute-done.8.refs_1_ = bf16[128,1024]{1,0:T(8,128)(2,1)S(1)} collective-permute-done((bf16[128,1024]{1,0:T(8,128)(2,1)S(1)}, bf16[128,1024]{1,0:T(8,128)(2,1)S(1)}, u32[]{:S(2)}, u32[]{:S(2)}) %collective-permute-start.8) | collective-permute-done | bytes 262176 | tf_op jit(solution)/shard_map/ppermute | solution.py:170
  22.7 0.0 collective-permute-done.7.other_ref
  22.7 0.5 %shard_map.76 = (f32[64,128]{1,0:T(8,128)S(1)}, f32[64,128]{1,0:T(8,128)S(1)}) custom-call(bf16[128,1024]{1,0:T(8,128)(2,1)S(1)} %shard_map.74.mine_ref, bf16[128,1024]{1,0:T(8,128)(2,1)S(1)} %collective-permute-done.7.other_ref, bf16[128,1024]{1,0:T(8,128)(2,1)S(1)} %get-tuple-element.19.refs_0_, bf16[128,1024]{1,0:T(8,128)(2,1)S(1)} %collective-permute-done.8.refs_1_), custom_call_target="tpu_custom_call" | custom-call | bytes 2100000 | tf_op jit(solution)/shard_map/pallas_call | solution.py:159
  23.2 1.6 %collective-permute-start.9 = (f32[64,128]{1,0:T(8,128)S(1)}, f32[64,128]{1,0:T(8,128)S(1)}, u32[]{:S(2)}, u32[]{:S(2)}) collective-permute-start(f32[64,128]{1,0:T(8,128)S(1)} %get-tuple-element.22), channel_id=1, source_target_pairs={{0,2},{1,3},{2,0},{3,1},{4,6},{5,7},{6,4},{7,5},{8,10},{9,11},{10,... | collective-permute-start | bytes 98312 | tf_op jit(solution)/shard_map/ppermute | solution.py:170
  24.8 2.4 %collective-permute-done.9 = f32[64,128]{1,0:T(8,128)S(1)} collective-permute-done((f32[64,128]{1,0:T(8,128)S(1)}, f32[64,128]{1,0:T(8,128)S(1)}, u32[]{:S(2)}, u32[]{:S(2)}) %collective-permute-start.9) | collective-permute-done | bytes 32800 | tf_op jit(solution)/shard_map/ppermute | solution.py:170
  27.2 0.6 %add.3 = f32[64,128]{1,0:T(8,128)} add(f32[64,128]{1,0:T(8,128)S(1)} %get-tuple-element.21, f32[64,128]{1,0:T(8,128)S(1)} %collective-permute-done.9) | non-fusion elementwise | flops 8192 | bytes 98304 | tf_op jit(solution)/shard_map/add | solution.py:200
Async XLA Ops:
  0.0 13.4 %copy-start.1 = (bf16[1,32,1,1024]{3,1,2,0:T(8,128)(2,1)S(1)}, bf16[1,32,1,1024]{3,1,2,0:T(8,128)(2,1)}, u32[]{:S(2)}) copy-start(bf16[1,32,1,1024]{3,1,2,0:T(8,128)(2,1)} %param.8) | copy-start | bytes 196612
  0.0 15.4 %copy-start = (bf16[64,4,1024]{2,1,0:T(4,128)(2,1)S(1)}, bf16[64,4,1024]{2,1,0:T(4,128)(2,1)}, u32[]{:S(2)}) copy-start(bf16[64,4,1024]{2,1,0:T(4,128)(2,1)} %train_hbm) | copy-start | bytes 1572868
  0.0 5.6 %collective-permute-start = (bf16[32,1024]{1,0:T(8,128)(2,1)}, bf16[32,1024]{1,0:T(8,128)(2,1)S(1)}, u32[]{:S(2)}, u32[]{:S(2)}) collective-permute-start(bf16[32,1024]{1,0:T(8,128)(2,1)} %bitcast.3), channel_id=1, source_target_pairs={{0,8},{4,12},{8,0},{12,4},{16,24},{20,28},{24,16},{28,20},{1,9},{5... | collective-permute-start | bytes 196616 | tf_op jit(solution)/shard_map/ppermute | solution.py:170
  3.0 7.5 %collective-permute-start.3 = (bf16[32,1024]{1,0:T(8,128)(2,1)}, bf16[32,1024]{1,0:T(8,128)(2,1)S(1)}, u32[]{:S(2)}, u32[]{:S(2)}) collective-permute-start(bf16[32,1024]{1,0:T(8,128)(2,1)} %bitcast.4), channel_id=1, source_target_pairs={{0,16},{4,20},{8,24},{12,28},{16,0},{20,4},{24,8},{28,12},{1,17},{... | collective-permute-start | bytes 196616 | tf_op jit(solution)/shard_map/ppermute | solution.py:170
  5.6 6.4 %collective-permute-start.5 = (bf16[32,1024]{1,0:T(8,128)(2,1)}, bf16[32,1024]{1,0:T(8,128)(2,1)S(1)}, u32[]{:S(2)}, u32[]{:S(2)}) collective-permute-start(bf16[32,1024]{1,0:T(8,128)(2,1)} %bitcast.5), channel_id=1, source_target_pairs={{0,24},{4,28},{8,16},{12,20},{16,8},{20,12},{24,0},{28,4},{1,25},{... | collective-permute-start | bytes 196616 | tf_op jit(solution)/shard_map/ppermute | solution.py:170
  5.6 0.7 %copy-start.2 = (bf16[1,32,32]{2,1,0:T(8,128)(2,1)S(1)}, bf16[1,32,32]{2,1,0:T(8,128)(2,1)}, u32[]{:S(2)}) copy-start(bf16[1,32,32]{2,1,0:T(8,128)(2,1)} %param.9) | copy-start | bytes 6148
  6.3 0.7 %copy-start.3 = (bf16[1,32,32]{2,1,0:T(8,128)(2,1)S(1)}, bf16[1,32,32]{2,1,0:T(8,128)(2,1)}, u32[]{:S(2)}) copy-start(bf16[1,32,32]{2,1,0:T(8,128)(2,1)} %param.10) | copy-start | bytes 6148
  7.0 8.4 %copy-start.5 = (s32[4]{0:T(128)S(1)}, s32[4]{0:T(128)}, u32[]{:S(2)}) copy-start(s32[4]{0:T(128)} %order_hbm.1) | copy-start | bytes 52
  7.0 11.4 %copy-start.4 = (f32[1,1024]{1,0:T(1,128)S(1)}, f32[1,1024]{1,0:T(1,128)}, u32[]{:S(2)}) copy-start(f32[1,1024]{1,0:T(1,128)} %values_ref.1) | copy-start | bytes 12292
  7.0 11.4 %copy-start.6 = (s32[4]{0:T(128)S(1)}, s32[4]{0:T(128)}, u32[]{:S(2)}) copy-start(s32[4]{0:T(128)} %owners_ref.1) | copy-start | bytes 52
  10.5 7.4 %collective-permute-start.4 = (bf16[32,1024]{1,0:T(8,128)(2,1)S(1)}, bf16[32,1024]{1,0:T(8,128)(2,1)S(1)}, u32[]{:S(2)}, u32[]{:S(2)}) collective-permute-start(bf16[32,1024]{1,0:T(8,128)(2,1)S(1)} %collective-permute-done.3.refs_4_), channel_id=1, source_target_pairs={{0,4},{4,0},{8,12},{12,8},{16,20},{20,16},{24,28},{28,24},{1,5},{5... | collective-permute-start | bytes 196616 | tf_op jit(solution)/shard_map/ppermute | solution.py:170
  12.0 5.9 %collective-permute-start.6 = (bf16[32,1024]{1,0:T(8,128)(2,1)S(1)}, bf16[32,1024]{1,0:T(8,128)(2,1)S(1)}, u32[]{:S(2)}, u32[]{:S(2)}) collective-permute-start(bf16[32,1024]{1,0:T(8,128)(2,1)S(1)} %collective-permute-done.5.refs_6_), channel_id=1, source_target_pairs={{0,4},{4,0},{8,12},{12,8},{16,20},{20,16},{24,28},{28,24},{1,5},{5... | collective-permute-start | bytes 196616 | tf_op jit(solution)/shard_map/ppermute | solution.py:170
  13.4 4.5 %collective-permute-start.1 = (bf16[32,1024]{1,0:T(8,128)(2,1)S(1)}, bf16[32,1024]{1,0:T(8,128)(2,1)S(1)}, u32[]{:S(2)}, u32[]{:S(2)}) collective-permute-start(bf16[32,1024]{1,0:T(8,128)(2,1)S(1)} %bitcast.6), channel_id=1, source_target_pairs={{0,4},{4,0},{8,12},{12,8},{16,20},{20,16},{24,28},{28,24},{1,5},{5... | collective-permute-start | bytes 196616 | tf_op jit(solution)/shard_map/ppermute | solution.py:170
  14.0 4.3 %collective-permute-start.2 = (bf16[32,1024]{1,0:T(8,128)(2,1)S(1)}, bf16[32,1024]{1,0:T(8,128)(2,1)S(1)}, u32[]{:S(2)}, u32[]{:S(2)}) collective-permute-start(bf16[32,1024]{1,0:T(8,128)(2,1)S(1)} %collective-permute-done.refs_2_), channel_id=1, source_target_pairs={{0,4},{4,0},{8,12},{12,8},{16,20},{20,16},{24,28},{28,24},{1,5},{5... | collective-permute-start | bytes 196616 | tf_op jit(solution)/shard_map/ppermute | solution.py:170
  16.3 6.4 %collective-permute-start.8 = (bf16[128,1024]{1,0:T(8,128)(2,1)S(1)}, bf16[128,1024]{1,0:T(8,128)(2,1)S(1)}, u32[]{:S(2)}, u32[]{:S(2)}) collective-permute-start(bf16[128,1024]{1,0:T(8,128)(2,1)S(1)} %get-tuple-element.20), channel_id=1, source_target_pairs={{0,2},{1,3},{2,0},{3,1},{4,6},{5,7},{6,4},{7,5},{8,10},{9,11},{10,... | collective-permute-start | bytes 786440 | tf_op jit(solution)/shard_map/ppermute | solution.py:170
  20.2 2.5 %collective-permute-start.7 = (bf16[128,1024]{1,0:T(8,128)(2,1)S(1)}, bf16[128,1024]{1,0:T(8,128)(2,1)S(1)}, u32[]{:S(2)}, u32[]{:S(2)}) collective-permute-start(bf16[128,1024]{1,0:T(8,128)(2,1)S(1)} %shard_map.74.mine_ref), channel_id=1, source_target_pairs={{0,1},{1,0},{2,3},{3,2},{4,5},{5,4},{6,7},{7,6},{8,9},{9,8},{10,11... | collective-permute-start | bytes 786440 | tf_op jit(solution)/shard_map/ppermute | solution.py:170
  23.2 4.0 %collective-permute-start.9 = (f32[64,128]{1,0:T(8,128)S(1)}, f32[64,128]{1,0:T(8,128)S(1)}, u32[]{:S(2)}, u32[]{:S(2)}) collective-permute-start(f32[64,128]{1,0:T(8,128)S(1)} %get-tuple-element.22), channel_id=1, source_target_pairs={{0,2},{1,3},{2,0},{3,1},{4,6},{5,7},{6,4},{7,5},{8,10},{9,11},{10,... | collective-permute-start | bytes 98312 | tf_op jit(solution)/shard_map/ppermute | solution.py:170

commit v3 on v2

v3 whole, which is shorter than its diff:
```python
import functools
import math

import jax
import jax.numpy as jnp
from jax import lax
from jax.experimental import pallas as pl
from jax.experimental.pallas import tpu as pltpu
from jax.sharding import PartitionSpec as P

LANES = 128
VMEM = pl.BlockSpec(memory_space=pltpu.VMEM)
HBM = pl.BlockSpec(memory_space=pltpu.HBM)
PARAMS = pltpu.CompilerParams(vmem_limit_bytes=32 * 1024 * 1024)


def place_of(owners, k, me, inner):
    seen = [owners[j] ^ me for j in range(owners.shape[0])]
    near, far = seen[k] % inner, seen[k] // inner
    place = jnp.int32(0)
    for other in seen:
        place += jnp.logical_and(other % inner == near, other // inner < far).astype(jnp.int32)
    return near, far, place


def prepare_kernel(inner, each, order_hbm, owners_hbm, out_hbm, in_hbm, values_hbm, own_hbm, train_hbm, *refs):
    rotator_ref, inverse_ref, send_ref, pick_ref, own_ref, *pairs = refs[:-8]
    order, owners, out_ref, in_ref, values, train, wide, sems = refs[-8:]
    loads = [
        pltpu.make_async_copy(src, dst, sems.at[i])
        for i, (src, dst) in enumerate(
            (
                (out_hbm, out_ref),
                (in_hbm, in_ref),
                (order_hbm, order),
                (owners_hbm, owners),
                (values_hbm, values),
                (own_hbm, own_ref),
                (train_hbm, train),
            )
        )
    ]
    for load in loads:
        load.start()
    side, width = out_ref.shape[1], rotator_ref.shape[0]
    column = lax.broadcasted_iota(jnp.int32, (side, width), 1)
    row = lax.broadcasted_iota(jnp.int32, (side, width), 0)
    spread = (column // side == row).astype(jnp.bfloat16)
    tiled = (column % side == row).astype(jnp.bfloat16)
    for load in loads[:2]:
        load.wait()
    outer = jnp.dot(out_ref[0], spread, preferred_element_type=jnp.float32)
    inside = jnp.dot(in_ref[0], tiled, preferred_element_type=jnp.float32)
    for a in range(side):
        rotator_ref[pl.ds(a * side, side), :] = (outer[a : a + 1, :] * inside).astype(jnp.bfloat16)
    for load in loads[2:]:
        load.wait()
    spectrum = values[...]
    inverse_ref[...] = 1.0 / (spectrum + 0.1 * jnp.mean(spectrum, axis=1, keepdims=True))

    me = lax.axis_index("group")
    places = send_ref.shape[0] // each
    line = lax.broadcasted_iota(jnp.int32, send_ref.shape, 0)
    lane = lax.broadcasted_iota(jnp.int32, send_ref.shape, 1)
    send = jnp.zeros(send_ref.shape, jnp.float32)
    line_p = lax.broadcasted_iota(jnp.int32, pick_ref.shape, 0)
    lane_p = lax.broadcasted_iota(jnp.int32, pick_ref.shape, 1)
    pick = jnp.zeros(pick_ref.shape, jnp.float32)
    for k in range(owners.shape[0]):
        near, far, place = place_of(owners, k, me, inner)
        shift = jnp.where(near == 0, (far - place) * each, -2 * send_ref.shape[1])
        hit = jnp.logical_and(lane - line == shift, line // each == place)
        send = jnp.where(hit, 1.0, send)
        shift = (near * places + place - k) * each
        hit = jnp.logical_and(lane_p - line_p == shift, line_p // each == k)
        pick = jnp.where(hit, 1.0, pick)
    send_ref[...] = send.astype(jnp.bfloat16)
    pick_ref[...] = pick.astype(jnp.bfloat16)

    rows, modules, _ = train.shape
    tiles = width // LANES
    slot = lax.axis_index("module")
    for e in range(rows):
        example = train[e].astype(jnp.float32)
        for t in range(tiles):
            wide[pl.ds((t * rows + e) * modules, modules), :] = example[:, t * LANES : (t + 1) * LANES]
    for j in range(modules):
        held = order[slot ^ j]
        out, at = pairs[j // 2], j % 2 * rows
        for t in range(tiles):
            piece = wide[pl.ds(t * rows * modules + held, rows, stride=modules), :]
            out[at : at + rows, t * LANES : (t + 1) * LANES] = piece.astype(out.dtype)


def prepare(train_grads, own, basis_out, basis_in, eigenvalues, owner_groups, module_order, inner, blocks):
    each = own.shape[0]
    rows, modules, width = train_grads.shape
    asked = owner_groups.shape[0]
    places = min(blocks, asked - (inner > 1))
    pair = jax.ShapeDtypeStruct((2 * rows, width), train_grads.dtype)
    shapes = (
        jax.ShapeDtypeStruct((width, width), jnp.bfloat16),
        jax.ShapeDtypeStruct(eigenvalues.shape, jnp.float32),
        jax.ShapeDtypeStruct((places * each, blocks * each), jnp.bfloat16),
        jax.ShapeDtypeStruct((asked * each, inner * places * each), jnp.bfloat16),
        jax.ShapeDtypeStruct(own.shape, own.dtype),
    ) + (pair,) * (modules // 2)
    return pl.pallas_call(
        functools.partial(prepare_kernel, inner, each),
        out_shape=shapes,
        in_specs=[HBM] * 7,
        out_specs=(VMEM,) * len(shapes),
        scratch_shapes=[
            pltpu.SMEM(module_order.shape, jnp.int32),
            pltpu.SMEM(owner_groups.shape, jnp.int32),
            pltpu.VMEM(basis_out.shape, basis_out.dtype),
            pltpu.VMEM(basis_in.shape, basis_in.dtype),
            pltpu.VMEM(eigenvalues.shape, eigenvalues.dtype),
            pltpu.VMEM(train_grads.shape, train_grads.dtype),
            pltpu.VMEM((rows * modules * width // LANES, LANES), jnp.float32),
            pltpu.SemaphoreType.DMA((7,)),
        ],
        compiler_params=PARAMS,
    )(
        *(
            pltpu.with_memory_space_constraint(operand, pltpu.HBM)
            for operand in (module_order, owner_groups, basis_out, basis_in, eigenvalues, own, train_grads)
        )
    )


def precondition_kernel(send_ref, rotator_ref, inverse_ref, *refs):
    *blocks, out = refs
    each = blocks[0].shape[0]
    queries = 0.0
    for b, block in enumerate(blocks):
        queries += jnp.dot(
            send_ref[:, b * each : (b + 1) * each], block[...], preferred_element_type=jnp.float32
        )
    asked = inverse_ref[...] * jnp.dot(
        queries.astype(jnp.bfloat16), rotator_ref[...], preferred_element_type=jnp.float32
    )
    out[...] = lax.dot_general(
        asked.astype(jnp.bfloat16),
        rotator_ref[...],
        (((1,), (1,)), ((), ())),
        preferred_element_type=jnp.float32,
    ).astype(out.dtype)


def precondition(send, rotator, inverse, blocks):
    return pl.pallas_call(
        precondition_kernel,
        out_shape=jax.ShapeDtypeStruct((send.shape[0], rotator.shape[0]), jnp.bfloat16),
        in_specs=[VMEM] * (3 + len(blocks)),
        out_specs=VMEM,
        compiler_params=PARAMS,
    )(send, rotator, inverse, *blocks)


def score_kernel(inner, factor, pick_ref, *refs):
    columns, refs = refs[: 2 * inner], refs[2 * inner :]
    count = len(refs) // 2
    span = columns[0].shape[0]
    asked = []
    for half in range(2):
        chosen = 0.0
        for column in range(inner):
            chosen += jnp.dot(
                pick_ref[:, column * span : (column + 1) * span],
                columns[2 * column + half][...],
                preferred_element_type=jnp.float32,
            )
        asked.append(chosen.astype(jnp.bfloat16))
    for pair, out in zip(refs[:count], refs[count:]):
        rows = out.shape[0]
        total = 0.0
        for half in range(2):
            total += lax.dot_general(
                pair[half * rows : (half + 1) * rows, :],
                asked[half],
                (((1,), (1,)), ((), ())),
                preferred_element_type=jnp.float32,
            )
        out[...] = factor * total


def score(pick, columns, pairs, factor):
    part = jax.ShapeDtypeStruct((pairs[0].shape[0] // 2, pick.shape[0]), jnp.float32)
    return pl.pallas_call(
        functools.partial(score_kernel, len(columns) // 2, factor),
        out_shape=(part,) * len(pairs),
        in_specs=[VMEM] * (1 + len(columns) + len(pairs)),
        out_specs=(VMEM,) * len(pairs),
        compiler_params=PARAMS,
    )(pick, *columns, *pairs)


def swap(array, axis, bits):
    return lax.ppermute(array, axis, [(i, i ^ bits) for i in range(lax.axis_size(axis))])


def after(array, *others):
    return lax.optimization_barrier((array,) + others)[0]


def local(train_grads, query_grads, basis_out, basis_in, eigenvalues, owner_groups, module_order):
    _, modules, width = train_grads.shape
    groups = lax.axis_size("group")
    inner = 1 << ((groups.bit_length() - 1) // 2)
    own = query_grads.reshape(-1, width)
    each = own.shape[0]
    blocks = [own] + [swap(own, "group", far) for far in range(inner, groups, inner)]
    rotator, inverse, send, pick, own, *pairs = prepare(
        train_grads,
        own,
        basis_out,
        basis_in,
        eigenvalues,
        owner_groups,
        module_order,
        inner,
        len(blocks),
    )
    blocks[0] = own
    pairs = [pairs[0]] + [swap(pairs[j], "module", 2 * j) for j in range(1, modules // 2)]
    mine = precondition(send, rotator, inverse, blocks)
    columns = [mine, swap(mine, "module", 1)]
    for near in range(1, inner):
        theirs = swap(mine, "group", near)
        columns += [theirs, swap(after(theirs, *pairs), "module", 1)]
    parts = score(pick, columns, pairs, 1.0 / math.sqrt(modules * width))
    total = parts[0]
    for j in range(1, modules // 2):
        total = total + swap(parts[j], "module", 2 * j)
    return total


def solution(mesh):
    in_specs = (
        P(("group", "module"), None, None),
        P("group", None, "module", None),
        P("module", None, None),
        P("module", None, None),
        P("module", None),
        P(),
        P(),
    )
    out_specs = P(("group", "module"), None)
    return jax.shard_map(local, mesh=mesh, in_specs=in_specs, out_specs=out_specs, check_vma=False)
```

time: 28.1 us -> 26 us (0.925)
  starting transfers between devices: 13.8 us -> 10.8 us
  waiting for transfers between devices: 8.2 us -> 10.4 us
  local copies, waits for them, and re-layouts: 1.41 us -> 0 us
    ppermute x10 -> x8, starting transfers between devices: 13.8 us -> 10.8 us  [swap(): lax.ppermute(array, axis, [(i, i ^ bits) for i in range(lax.axis_size(axi...]
    ppermute x10 -> x8, waiting for transfers between devices: 8.2 us -> 10.4 us  [swap(): lax.ppermute(array, axis, [(i, i ^ bits) for i in range(lax.axis_size(axi...]
    unnamed x14 -> x0, local copies, waits for them, and re-layouts: 1.41 us -> none
    pallas_call x4 -> x3, Pallas kernels: 3.73 us -> 3.99 us  [the longest x1 1.68 us: prepare(): pl.pallas_call(functools.partial(prepare_kernel, inner, each), out_shape=...]
  transfers between devices with their start and end apart: 10 -> 8, of which waited for: 4 -> 4; matrix products, arithmetic and copies ran while one was open for 0% -> 0% of each run, Pallas kernels for 12% -> 12%
where the time goes in v3:
time: 26 us; the launch traced here: 25.8 us
  starting transfers between devices  10.8 us (42%)
  waiting for transfers between devices  10.4 us (40%)
  Pallas kernels  3.99 us (15%)
  other arithmetic  0.62 us (2%)
    ppermute x8, starting transfers between devices, swap(): lax.ppermute(array, axis, [(i, i ^ bits) for i in range(lax.axis_size(axi...  10.8 us
    ppermute x8, waiting for transfers between devices, swap(): lax.ppermute(array, axis, [(i, i ^ bits) for i in range(lax.axis_size(axi...  10.4 us
    pallas_call x1, Pallas kernels, prepare(): pl.pallas_call(functools.partial(prepare_kernel, inner, each), out_shape=...  1.68 us
    pallas_call x1, Pallas kernels, precondition(): pl.pallas_call(precondition_kernel, out_shape=jax.ShapeDtypeStruct((send....  1.43 us
    pallas_call x1, Pallas kernels, score(): pl.pallas_call(functools.partial(score_kernel, len(columns) // 2, factor)...  0.87 us
    add x1, other arithmetic, local(): total = total + swap(parts[j], 'module', 2 * j)  0.62 us
  transfers between devices with their start and end apart: 8, of which 4 were waited for; matrix products, arithmetic and copies ran while one was open for 0% of the time, Pallas kernels for 12%

profile of v3, /device:TPU:0, one launch (start us, length us, event | category | flops | bytes accessed | tf_op | source)
XLA Modules:
  0.0 25.8 jit_solution(6080459765455837984)
XLA Ops:
  0.0 5.0 %collective-permute-start.2 = (bf16[32,1024]{1,0:T(8,128)(2,1)}, bf16[32,1024]{1,0:T(8,128)(2,1)S(1)}, u32[]{:S(2)}, u32[]{:S(2)}) collective-permute-start(bf16[32,1024]{1,0:T(8,128)(2,1)} %bitcast.1), channel_id=1, source_target_pairs={{0,24},{4,28},{8,16},{12,20},{16,8},{20,12},{24,0},{28,4},{1,25},{... | collective-permute-start | bytes 196616 | tf_op jit(solution)/shard_map/ppermute | solution.py:200
  5.0 0.0 collective-permute-start.1
  5.1 0.6 %collective-permute-start = (bf16[32,1024]{1,0:T(8,128)(2,1)}, bf16[32,1024]{1,0:T(8,128)(2,1)S(1)}, u32[]{:S(2)}, u32[]{:S(2)}) collective-permute-start(bf16[32,1024]{1,0:T(8,128)(2,1)} %bitcast.3), channel_id=1, source_target_pairs={{0,8},{4,12},{8,0},{12,4},{16,24},{20,28},{24,16},{28,20},{1,9},{5... | collective-permute-start | bytes 196616 | tf_op jit(solution)/shard_map/ppermute | solution.py:200
  5.6 1.7 %shard_map.73 = (bf16[1024,1024]{1,0:T(8,128)(2,1)S(1)}, f32[1,1024]{1,0:T(1,128)S(1)}, bf16[96,128]{1,0:T(8,128)(2,1)S(1)}, bf16[128,192]{1,0:T(8,128)(2,1)S(1)...) custom-call(s32[4]{0:T(128)} %order_hbm.1, s32[4]{0:T(128)} %owners_hbm.1, ...), custom_call_target="tpu_custom_call" | custom-call | tf_op jit(solution)/shard_map/pallas_call | solution.py:108
  7.3 1.8 %collective-permute-start.5 = (bf16[128,1024]{1,0:T(8,128)(2,1)S(1)}, bf16[128,1024]{1,0:T(8,128)(2,1)S(1)}, u32[]{:S(2)}, u32[]{:S(2)}) collective-permute-start(bf16[128,1024]{1,0:T(8,128)(2,1)S(1)} %get-tuple-element.21), channel_id=1, source_target_pairs={{0,2},{1,3},{2,0},{3,1},{4,6},{5,7},{6,4},{7,5},{8,10},{9,11},{10,... | collective-permute-start | bytes 786440 | tf_op jit(solution)/shard_map/ppermute | solution.py:200
  9.1 0.0 collective-permute-done.2.refs_3_
  9.1 1.7 %collective-permute-done.1.refs_2_ = bf16[32,1024]{1,0:T(8,128)(2,1)S(1)} collective-permute-done((bf16[32,1024]{1,0:T(8,128)(2,1)}, bf16[32,1024]{1,0:T(8,128)(2,1)S(1)}, u32[]{:S(2)}, u32[]{:S(2)}) %collective-permute-start.1) | collective-permute-done | bytes 65568 | tf_op jit(solution)/shard_map/ppermute | solution.py:200
  10.9 0.0 collective-permute-done.refs_1_
  10.9 1.4 %shard_map.74.refs_0_ = bf16[96,1024]{1,0:T(8,128)(2,1)S(1)} custom-call(bf16[96,128]{1,0:T(8,128)(2,1)S(1)} %get-tuple-element.16.send_ref, bf16[1024,1024]{1,0:T(8,128)(2,1)S(1)} %get-tuple-element.17.rotator_ref, f32[1,1024]{1,0:T(1,128)S(1)} %get-tuple-element.18.inverse_ref, bf16[32,1024]{1,0:T(8,128)(2,1)S(1)} %get-tuple-element.19.refs_0_, ...), custom_call_target="tpu_custom_call" | custom-call | tf_op jit(solution)/shard_map/pallas_call | solution.py:152
  12.3 1.6 %collective-permute-start.4 = (bf16[96,1024]{1,0:T(8,128)(2,1)S(1)}, bf16[96,1024]{1,0:T(8,128)(2,1)S(1)}, u32[]{:S(2)}, u32[]{:S(2)}) collective-permute-start(bf16[96,1024]{1,0:T(8,128)(2,1)S(1)} %shard_map.74.refs_0_), channel_id=1, source_target_pairs={{0,4},{4,0},{8,12},{12,8},{16,20},{20,16},{24,28},{28,24},{1,5},{5... | collective-permute-start | bytes 589832 | tf_op jit(solution)/shard_map/ppermute | solution.py:200
  13.9 0.0 collective-permute-start.3
  13.9 5.0 %collective-permute-done.4.refs_2_ = bf16[96,1024]{1,0:T(8,128)(2,1)S(1)} collective-permute-done((bf16[96,1024]{1,0:T(8,128)(2,1)S(1)}, bf16[96,1024]{1,0:T(8,128)(2,1)S(1)}, u32[]{:S(2)}, u32[]{:S(2)}) %collective-permute-start.4) | collective-permute-done | bytes 196640 | tf_op jit(solution)/shard_map/ppermute | solution.py:200
  18.8 0.0 collective-permute-done.5.refs_5_
  18.8 0.0 collective-permute-start.6
  18.8 0.0 collective-permute-done.3.refs_1_
  18.8 1.4 %collective-permute-done.6.refs_3_ = bf16[96,1024]{1,0:T(8,128)(2,1)S(1)} collective-permute-done((bf16[96,1024]{1,0:T(8,128)(2,1)S(1)}, bf16[96,1024]{1,0:T(8,128)(2,1)S(1)}, u32[]{:S(2)}, u32[]{:S(2)}) %collective-permute-start.6) | collective-permute-done | bytes 196640 | tf_op jit(solution)/shard_map/ppermute | solution.py:200
  20.3 0.9 %shard_map.75 = (f32[64,128]{1,0:T(8,128)S(1)}, f32[64,128]{1,0:T(8,128)S(1)}) custom-call(bf16[128,192]{1,0:T(8,128)(2,1)S(1)} %get-tuple-element.15.pick_ref, bf16[96,1024]{1,0:T(8,128)(2,1)S(1)} %shard_map.74.refs_0_, bf16[96,1024]{1,0:T(8,128)(2,1)S(1)} %collective-permute-done.3.refs_1_, bf16[96,1024]{1,0:T(8,128)(2,1)S(1)} %collective-permute-done.4.refs_2_, ...), custom_call_target="tpu_custom_call" | custom-call | tf_op jit(solution)/shard_map/pallas_call | solution.py:190
  21.2 1.8 %collective-permute-start.7 = (f32[64,128]{1,0:T(8,128)S(1)}, f32[64,128]{1,0:T(8,128)S(1)}, u32[]{:S(2)}, u32[]{:S(2)}) collective-permute-start(f32[64,128]{1,0:T(8,128)S(1)} %get-tuple-element.24), channel_id=1, source_target_pairs={{0,2},{1,3},{2,0},{3,1},{4,6},{5,7},{6,4},{7,5},{8,10},{9,11},{10,... | collective-permute-start | bytes 98312 | tf_op jit(solution)/shard_map/ppermute | solution.py:200
  22.9 2.2 %collective-permute-done.7 = f32[64,128]{1,0:T(8,128)S(1)} collective-permute-done((f32[64,128]{1,0:T(8,128)S(1)}, f32[64,128]{1,0:T(8,128)S(1)}, u32[]{:S(2)}, u32[]{:S(2)}) %collective-permute-start.7) | collective-permute-done | bytes 32800 | tf_op jit(solution)/shard_map/ppermute | solution.py:200
  25.1 0.6 %add.3 = f32[64,128]{1,0:T(8,128)} add(f32[64,128]{1,0:T(8,128)S(1)} %get-tuple-element.23, f32[64,128]{1,0:T(8,128)S(1)} %collective-permute-done.7) | non-fusion elementwise | flops 8192 | bytes 98304 | tf_op jit(solution)/shard_map/add | solution.py:235
Async XLA Ops:
  0.0 9.1 %collective-permute-start.2 = (bf16[32,1024]{1,0:T(8,128)(2,1)}, bf16[32,1024]{1,0:T(8,128)(2,1)S(1)}, u32[]{:S(2)}, u32[]{:S(2)}) collective-permute-start(bf16[32,1024]{1,0:T(8,128)(2,1)} %bitcast.1), channel_id=1, source_target_pairs={{0,24},{4,28},{8,16},{12,20},{16,8},{20,12},{24,0},{28,4},{1,25},{... | collective-permute-start | bytes 196616 | tf_op jit(solution)/shard_map/ppermute | solution.py:200
  5.0 5.8 %collective-permute-start.1 = (bf16[32,1024]{1,0:T(8,128)(2,1)}, bf16[32,1024]{1,0:T(8,128)(2,1)S(1)}, u32[]{:S(2)}, u32[]{:S(2)}) collective-permute-start(bf16[32,1024]{1,0:T(8,128)(2,1)} %bitcast.2), channel_id=1, source_target_pairs={{0,16},{4,20},{8,24},{12,28},{16,0},{20,4},{24,8},{28,12},{1,17},{... | collective-permute-start | bytes 196616 | tf_op jit(solution)/shard_map/ppermute | solution.py:200
  5.1 5.8 %collective-permute-start = (bf16[32,1024]{1,0:T(8,128)(2,1)}, bf16[32,1024]{1,0:T(8,128)(2,1)S(1)}, u32[]{:S(2)}, u32[]{:S(2)}) collective-permute-start(bf16[32,1024]{1,0:T(8,128)(2,1)} %bitcast.3), channel_id=1, source_target_pairs={{0,8},{4,12},{8,0},{12,4},{16,24},{20,28},{24,16},{28,20},{1,9},{5... | collective-permute-start | bytes 196616 | tf_op jit(solution)/shard_map/ppermute | solution.py:200
  7.3 11.5 %collective-permute-start.5 = (bf16[128,1024]{1,0:T(8,128)(2,1)S(1)}, bf16[128,1024]{1,0:T(8,128)(2,1)S(1)}, u32[]{:S(2)}, u32[]{:S(2)}) collective-permute-start(bf16[128,1024]{1,0:T(8,128)(2,1)S(1)} %get-tuple-element.21), channel_id=1, source_target_pairs={{0,2},{1,3},{2,0},{3,1},{4,6},{5,7},{6,4},{7,5},{8,10},{9,11},{10,... | collective-permute-start | bytes 786440 | tf_op jit(solution)/shard_map/ppermute | solution.py:200
  12.3 6.5 %collective-permute-start.4 = (bf16[96,1024]{1,0:T(8,128)(2,1)S(1)}, bf16[96,1024]{1,0:T(8,128)(2,1)S(1)}, u32[]{:S(2)}, u32[]{:S(2)}) collective-permute-start(bf16[96,1024]{1,0:T(8,128)(2,1)S(1)} %shard_map.74.refs_0_), channel_id=1, source_target_pairs={{0,4},{4,0},{8,12},{12,8},{16,20},{20,16},{24,28},{28,24},{1,5},{5... | collective-permute-start | bytes 589832 | tf_op jit(solution)/shard_map/ppermute | solution.py:200
  13.9 5.0 %collective-permute-start.3 = (bf16[96,1024]{1,0:T(8,128)(2,1)S(1)}, bf16[96,1024]{1,0:T(8,128)(2,1)S(1)}, u32[]{:S(2)}, u32[]{:S(2)}) collective-permute-start(bf16[96,1024]{1,0:T(8,128)(2,1)S(1)} %shard_map.74.refs_0_), channel_id=1, source_target_pairs={{0,1},{1,0},{2,3},{3,2},{4,5},{5,4},{6,7},{7,6},{8,9},{9,8},{10,11... | collective-permute-start | bytes 589832 | tf_op jit(solution)/shard_map/ppermute | solution.py:200
  18.8 1.4 %collective-permute-start.6 = (bf16[96,1024]{1,0:T(8,128)(2,1)S(1)}, bf16[96,1024]{1,0:T(8,128)(2,1)S(1)}, u32[]{:S(2)}, u32[]{:S(2)}) collective-permute-start(bf16[96,1024]{1,0:T(8,128)(2,1)S(1)} %collective-permute-done.4.refs_2_), channel_id=1, source_target_pairs={{0,1},{1,0},{2,3},{3,2},{4,5},{5,4},{6,7},{7,6},{8,9},{9,8},{10,11... | collective-permute-start | bytes 589832 | tf_op jit(solution)/shard_map/ppermute | solution.py:200
  21.2 4.0 %collective-permute-start.7 = (f32[64,128]{1,0:T(8,128)S(1)}, f32[64,128]{1,0:T(8,128)S(1)}, u32[]{:S(2)}, u32[]{:S(2)}) collective-permute-start(f32[64,128]{1,0:T(8,128)S(1)} %get-tuple-element.24), channel_id=1, source_target_pairs={{0,2},{1,3},{2,0},{3,1},{4,6},{5,7},{6,4},{7,5},{8,10},{9,11},{10,... | collective-permute-start | bytes 98312 | tf_op jit(solution)/shard_map/ppermute | solution.py:200

commit v4 on v3

--- a/solution.py
+++ b/solution.py
@@ -23,8 +23,20 @@
     return near, far, place
 
 
+def build_rotator(basis_out, basis_in, rotator_ref):
+    side, width = basis_out.shape[0], rotator_ref.shape[0]
+    column = lax.broadcasted_iota(jnp.int32, (side, width), 1)
+    row = lax.broadcasted_iota(jnp.int32, (side, width), 0)
+    spread = (column // side == row).astype(jnp.bfloat16)
+    tiled = (column % side == row).astype(jnp.bfloat16)
+    outer = jnp.dot(basis_out, spread, preferred_element_type=jnp.float32)
+    inside = jnp.dot(basis_in, tiled, preferred_element_type=jnp.float32)
+    for a in range(side):
+        rotator_ref[pl.ds(a * side, side), :] = (outer[a : a + 1, :] * inside).astype(jnp.bfloat16)
+
+
 def prepare_kernel(inner, each, order_hbm, owners_hbm, out_hbm, in_hbm, values_hbm, own_hbm, train_hbm, *refs):
-    rotator_ref, inverse_ref, send_ref, pick_ref, own_ref, *pairs = refs[:-8]
+    rotator_ref, inverse_ref, send_ref, pick_ref, own_ref, bases_ref, *pairs = refs[:-8]
     order, owners, out_ref, in_ref, values, train, wide, sems = refs[-8:]
     loads = [
         pltpu.make_async_copy(src, dst, sems.at[i])
@@ -43,16 +55,11 @@
     for load in loads:
         load.start()
     side, width = out_ref.shape[1], rotator_ref.shape[0]
-    column = lax.broadcasted_iota(jnp.int32, (side, width), 1)
-    row = lax.broadcasted_iota(jnp.int32, (side, width), 0)
-    spread = (column // side == row).astype(jnp.bfloat16)
-    tiled = (column % side == row).astype(jnp.bfloat16)
     for load in loads[:2]:
         load.wait()
-    outer = jnp.dot(out_ref[0], spread, preferred_element_type=jnp.float32)
-    inside = jnp.dot(in_ref[0], tiled, preferred_element_type=jnp.float32)
-    for a in range(side):
-        rotator_ref[pl.ds(a * side, side), :] = (outer[a : a + 1, :] * inside).astype(jnp.bfloat16)
+    bases_ref[:side, :] = out_ref[0]
+    bases_ref[side:, :] = in_ref[0]
+    build_rotator(out_ref[0], in_ref[0], rotator_ref)
     for load in loads[2:]:
         load.wait()
     spectrum = values[...]
@@ -104,6 +111,7 @@
         jax.ShapeDtypeStruct((places * each, blocks * each), jnp.bfloat16),
         jax.ShapeDtypeStruct((asked * each, inner * places * each), jnp.bfloat16),
         jax.ShapeDtypeStruct(own.shape, own.dtype),
+        jax.ShapeDtypeStruct((2 * basis_out.shape[1], basis_out.shape[2]), basis_out.dtype),
     ) + (pair,) * (modules // 2)
     return pl.pallas_call(
         functools.partial(prepare_kernel, inner, each),
@@ -129,60 +137,96 @@
     )
 
 
-def precondition_kernel(send_ref, rotator_ref, inverse_ref, *refs):
+def ask_kernel(order, send_ref, rotator_ref, inverse_ref, *refs):
     *blocks, out = refs
     each = blocks[0].shape[0]
     queries = 0.0
-    for b, block in enumerate(blocks):
+    for b, block in zip(order, blocks):
         queries += jnp.dot(
             send_ref[:, b * each : (b + 1) * each], block[...], preferred_element_type=jnp.float32
         )
-    asked = inverse_ref[...] * jnp.dot(
-        queries.astype(jnp.bfloat16), rotator_ref[...], preferred_element_type=jnp.float32
-    )
-    out[...] = lax.dot_general(
-        asked.astype(jnp.bfloat16),
-        rotator_ref[...],
-        (((1,), (1,)), ((), ())),
-        preferred_element_type=jnp.float32,
+    out[...] = (
+        inverse_ref[...]
+        * jnp.dot(queries.astype(jnp.bfloat16), rotator_ref[...], preferred_element_type=jnp.float32)
     ).astype(out.dtype)
 
 
-def precondition(send, rotator, inverse, blocks):
-    return pl.pallas_call(
-        precondition_kernel,
+def ask(send, rotator, inverse, blocks):
+    order = (*range(2, len(blocks)), 1, 0)
+    return pl.pallas_call(
+        functools.partial(ask_kernel, order),
         out_shape=jax.ShapeDtypeStruct((send.shape[0], rotator.shape[0]), jnp.bfloat16),
         in_specs=[VMEM] * (3 + len(blocks)),
         out_specs=VMEM,
         compiler_params=PARAMS,
-    )(send, rotator, inverse, *blocks)
+    )(send, rotator, inverse, *(blocks[b] for b in order))
+
+
+def turn_kernel(bases_ref, rotator_ref, pair, other_ref, turned):
+    rows, side = pair.shape[0] // 2, bases_ref.shape[1]
+    build_rotator(bases_ref[:side, :], bases_ref[side:, :], other_ref)
+    turn_pair(rows, pair, rotator_ref, other_ref, turned)
+
+
+def turn_pair(rows, pair, rotator_ref, other_ref, turned):
+    for half, rotator in enumerate((rotator_ref, other_ref)):
+        at = slice(half * rows, (half + 1) * rows)
+        turned[at, :] = jnp.dot(
+            pair[at, :], rotator[...], preferred_element_type=jnp.float32
+        ).astype(turned.dtype)
+
+
+def turn_more_kernel(rotator_ref, other_ref, *refs):
+    count = len(refs) // 2
+    for pair, turned in zip(refs[:count], refs[count:]):
+        turn_pair(pair.shape[0] // 2, pair, rotator_ref, other_ref, turned)
+
+
+def turn(bases, rotator, pair):
+    return pl.pallas_call(
+        turn_kernel,
+        out_shape=(
+            jax.ShapeDtypeStruct(rotator.shape, rotator.dtype),
+            jax.ShapeDtypeStruct(pair.shape, pair.dtype),
+        ),
+        in_specs=[VMEM] * 3,
+        out_specs=(VMEM,) * 2,
+        compiler_params=PARAMS,
+    )(bases, rotator, pair)
+
+
+def turn_more(rotator, other, pairs):
+    return pl.pallas_call(
+        turn_more_kernel,
+        out_shape=tuple(jax.ShapeDtypeStruct(pair.shape, pair.dtype) for pair in pairs),
+        in_specs=[VMEM] * (2 + len(pairs)),
+        out_specs=(VMEM,) * len(pairs),
+        compiler_params=PARAMS,
+    )(rotator, other, *pairs)
 
 
 def score_kernel(inner, factor, pick_ref, *refs):
     columns, refs = refs[: 2 * inner], refs[2 * inner :]
-    count = len(refs) // 2
-    span = columns[0].shape[0]
-    asked = []
+    pairs, outs = refs[: len(refs) // 2], refs[len(refs) // 2 :]
+    span, rows = columns[0].shape[0], outs[0].shape[0]
+    total = 0.0
     for half in range(2):
-        chosen = 0.0
+        asked = 0.0
         for column in range(inner):
-            chosen += jnp.dot(
+            asked += jnp.dot(
                 pick_ref[:, column * span : (column + 1) * span],
                 columns[2 * column + half][...],
                 preferred_element_type=jnp.float32,
             )
-        asked.append(chosen.astype(jnp.bfloat16))
-    for pair, out in zip(refs[:count], refs[count:]):
-        rows = out.shape[0]
-        total = 0.0
-        for half in range(2):
-            total += lax.dot_general(
-                pair[half * rows : (half + 1) * rows, :],
-                asked[half],
-                (((1,), (1,)), ((), ())),
-                preferred_element_type=jnp.float32,
-            )
-        out[...] = factor * total
+        turned = [pair[half * rows : (half + 1) * rows, :] for pair in pairs]
+        total += lax.dot_general(
+            jnp.concatenate(turned, axis=0),
+            asked.astype(jnp.bfloat16),
+            (((1,), (1,)), ((), ())),
+            preferred_element_type=jnp.float32,
+        )
+    for j, out in enumerate(outs):
+        out[...] = factor * total[j * rows : (j + 1) * rows, :]
 
 
 def score(pick, columns, pairs, factor):
@@ -211,7 +255,7 @@
     own = query_grads.reshape(-1, width)
     each = own.shape[0]
     blocks = [own] + [swap(own, "group", far) for far in range(inner, groups, inner)]
-    rotator, inverse, send, pick, own, *pairs = prepare(
+    rotator, inverse, send, pick, own, bases, *pairs = prepare(
         train_grads,
         own,
         basis_out,
@@ -223,13 +267,15 @@
         len(blocks),
     )
     blocks[0] = own
-    pairs = [pairs[0]] + [swap(pairs[j], "module", 2 * j) for j in range(1, modules // 2)]
-    mine = precondition(send, rotator, inverse, blocks)
+    sent = [swap(pairs[j], "module", 2 * j) for j in range(1, modules // 2)]
+    mine = ask(send, rotator, inverse, blocks)
+    other, turned = turn(after(swap(bases, "module", 1), mine), rotator, pairs[0])
+    turned = [turned, *turn_more(rotator, other, sent)]
     columns = [mine, swap(mine, "module", 1)]
     for near in range(1, inner):
         theirs = swap(mine, "group", near)
-        columns += [theirs, swap(after(theirs, *pairs), "module", 1)]
-    parts = score(pick, columns, pairs, 1.0 / math.sqrt(modules * width))
+        columns += [theirs, swap(after(theirs, *turned), "module", 1)]
+    parts = score(pick, columns, turned, 1.0 / math.sqrt(modules * width))
     total = parts[0]
     for j in range(1, modules // 2):
         total = total + swap(parts[j], "module", 2 * j)

time: 26 us -> 24.3 us (0.935)
  waiting for transfers between devices: 10.4 us -> 7.23 us
  Pallas kernels: 3.99 us -> 5.31 us
    ppermute x8 -> x9, waiting for transfers between devices: 10.4 us -> 7.23 us  [swap(): lax.ppermute(array, axis, [(i, i ^ bits) for i in range(lax.axis_size(axi...]
    pallas_call x1 -> x3, Pallas kernels: 1.43 us -> 2.69 us  [the longest x1 1.05 us: turn(): pl.pallas_call(turn_kernel, out_shape=(jax.ShapeDtypeStruct(rotator.shape...]
    ppermute x8 -> x9, starting transfers between devices: 10.8 us -> 10.9 us  [swap(): lax.ppermute(array, axis, [(i, i ^ bits) for i in range(lax.axis_size(axi...]
  transfers between devices with their start and end apart: 8 -> 9, of which waited for: 4 -> 6; matrix products, arithmetic and copies ran while one was open for 0% -> 0% of each run, Pallas kernels for 12% -> 18%
where the time goes in v4:
time: 24.3 us; the launch traced here: 24.1 us
  starting transfers between devices  10.9 us (45%)
  waiting for transfers between devices  7.23 us (30%)
  Pallas kernels  5.31 us (22%)
  other arithmetic  0.62 us (3%)
    ppermute x9, starting transfers between devices, swap(): lax.ppermute(array, axis, [(i, i ^ bits) for i in range(lax.axis_size(axi...  10.9 us
    ppermute x9, waiting for transfers between devices, swap(): lax.ppermute(array, axis, [(i, i ^ bits) for i in range(lax.axis_size(axi...  7.23 us
    pallas_call x1, Pallas kernels, prepare(): pl.pallas_call(functools.partial(prepare_kernel, inner, each), out_shape=...  1.69 us
    pallas_call x1, Pallas kernels, turn(): pl.pallas_call(turn_kernel, out_shape=(jax.ShapeDtypeStruct(rotator.shape...  1.05 us
    pallas_call x1, Pallas kernels, score(): pl.pallas_call(functools.partial(score_kernel, len(columns) // 2, factor)...  0.93 us
    pallas_call x1, Pallas kernels, turn_more(): pl.pallas_call(turn_more_kernel, out_shape=tuple((jax.ShapeDtypeStruct(pa...  0.85 us
    pallas_call x1, Pallas kernels, ask(): pl.pallas_call(functools.partial(ask_kernel, order), out_shape=jax.ShapeD...  0.79 us
    add x1, other arithmetic, local(): total = total + swap(parts[j], 'module', 2 * j)  0.62 us
  transfers between devices with their start and end apart: 9, of which 6 were waited for; matrix products, arithmetic and copies ran while one was open for 0% of the time, Pallas kernels for 18%

profile of v4, /device:TPU:0, one launch (start us, length us, event | category | flops | bytes accessed | tf_op | source)
XLA Modules:
  0.0 24.1 jit_solution(1001622571897164619)
XLA Ops:
  0.0 4.0 %collective-permute-start = (bf16[32,1024]{1,0:T(8,128)(2,1)}, bf16[32,1024]{1,0:T(8,128)(2,1)S(1)}, u32[]{:S(2)}, u32[]{:S(2)}) collective-permute-start(bf16[32,1024]{1,0:T(8,128)(2,1)} %bitcast.1), channel_id=1, source_target_pairs={{0,16},{4,20},{8,24},{12,28},{16,0},{20,4},{24,8},{28,12},{1,17},{... | collective-permute-start | bytes 196616 | tf_op jit(solution)/shard_map/ppermute | solution.py:244
  4.0 1.3 %collective-permute-start.1 = (bf16[32,1024]{1,0:T(8,128)(2,1)}, bf16[32,1024]{1,0:T(8,128)(2,1)S(1)}, u32[]{:S(2)}, u32[]{:S(2)}) collective-permute-start(bf16[32,1024]{1,0:T(8,128)(2,1)} %bitcast.2), channel_id=1, source_target_pairs={{0,24},{4,28},{8,16},{12,20},{16,8},{20,12},{24,0},{28,4},{1,25},{... | collective-permute-start | bytes 196616 | tf_op jit(solution)/shard_map/ppermute | solution.py:244
  5.4 0.2 collective-permute-start.2
  5.6 1.7 %shard_map.73 = (bf16[1024,1024]{1,0:T(8,128)(2,1)S(1)}, f32[1,1024]{1,0:T(1,128)S(1)}, bf16[96,128]{1,0:T(8,128)(2,1)S(1)}, bf16[128,192]{1,0:T(8,128)(2,1)S(1)...) custom-call(s32[4]{0:T(128)} %order_hbm.1, ...), custom_call_target="tpu_custom_call" | custom-call | tf_op jit(solution)/shard_map/pallas_call | solution.py:116
  7.3 1.6 %collective-permute-start.6 = (bf16[128,1024]{1,0:T(8,128)(2,1)S(1)}, bf16[128,1024]{1,0:T(8,128)(2,1)S(1)}, u32[]{:S(2)}, u32[]{:S(2)}) collective-permute-start(bf16[128,1024]{1,0:T(8,128)(2,1)S(1)} %get-tuple-element.29), channel_id=1, source_target_pairs={{0,2},{1,3},{2,0},{3,1},{4,6},{5,7},{6,4},{7,5},{8,10},{9,11},{10,... | collective-permute-start | bytes 786440 | tf_op jit(solution)/shard_map/ppermute | solution.py:244
  8.9 0.0 collective-permute-done.refs_0_
  8.9 1.6 %collective-permute-done.1.refs_1_ = bf16[32,1024]{1,0:T(8,128)(2,1)S(1)} collective-permute-done((bf16[32,1024]{1,0:T(8,128)(2,1)}, bf16[32,1024]{1,0:T(8,128)(2,1)S(1)}, u32[]{:S(2)}, u32[]{:S(2)}) %collective-permute-start.1) | collective-permute-done | bytes 65568 | tf_op jit(solution)/shard_map/ppermute | solution.py:244
  10.5 0.1 collective-permute-done.2.refs_2_
  10.6 0.8 %shard_map.74.refs_0_ = bf16[96,1024]{1,0:T(8,128)(2,1)S(1)} custom-call(bf16[96,128]{1,0:T(8,128)(2,1)S(1)} %get-tuple-element.20.send_ref, bf16[1024,1024]{1,0:T(8,128)(2,1)S(1)} %get-tuple-element.21.rotator_ref, f32[1,1024]{1,0:T(1,128)S(1)} %get-tuple-element.22.inverse_ref, bf16[32,1024]{1,0:T(8,128)(2,1)S(1)} %collective-permute-done.refs_0_, ...), custom_call_target="tpu_custom_call" | custom-call | tf_op jit(solution)/shard_map/pallas_call | solution.py:156
  11.4 1.6 %collective-permute-start.4 = (bf16[96,1024]{1,0:T(8,128)(2,1)S(1)}, bf16[96,1024]{1,0:T(8,128)(2,1)S(1)}, u32[]{:S(2)}, u32[]{:S(2)}) collective-permute-start(bf16[96,1024]{1,0:T(8,128)(2,1)S(1)} %shard_map.74.refs_0_), channel_id=1, source_target_pairs={{0,4},{4,0},{8,12},{12,8},{16,20},{20,16},{24,28},{28,24},{1,5},{5... | collective-permute-start | bytes 589832 | tf_op jit(solution)/shard_map/ppermute | solution.py:244
  12.9 0.0 collective-permute-start.5
  12.9 0.5 %collective-permute-start.3 = (bf16[96,1024]{1,0:T(8,128)(2,1)S(1)}, bf16[96,1024]{1,0:T(8,128)(2,1)S(1)}, u32[]{:S(2)}, u32[]{:S(2)}) collective-permute-start(bf16[96,1024]{1,0:T(8,128)(2,1)S(1)} %shard_map.74.refs_0_), channel_id=1, source_target_pairs={{0,1},{1,0},{2,3},{3,2},{4,5},{5,4},{6,7},{7,6},{8,9},{9,8},{10,11... | collective-permute-start | bytes 589832 | tf_op jit(solution)/shard_map/ppermute | solution.py:244
  13.4 0.7 %collective-permute-done.5.bases_ref = bf16[64,32]{1,0:T(8,128)(2,1)S(1)} collective-permute-done((bf16[64,32]{1,0:T(8,128)(2,1)S(1)}, bf16[64,32]{1,0:T(8,128)(2,1)S(1)}, u32[]{:S(2)}, u32[]{:S(2)}) %collective-permute-start.5) | collective-permute-done | bytes 4128 | tf_op jit(solution)/shard_map/ppermute | solution.py:244
  14.1 1.1 %shard_map.75 = (bf16[1024,1024]{1,0:T(8,128)(2,1)S(1)}, bf16[128,1024]{1,0:T(8,128)(2,1)S(1)}) custom-call(bf16[64,32]{1,0:T(8,128)(2,1)S(1)} %collective-permute-done.5.bases_ref, bf16[1024,1024]{1,0:T(8,128)(2,1)S(1)} %get-tuple-element.21.rotator_ref, bf16[128,1024]{1,0:T(8,128)(2,1)S(1)} %get-tuple-element.26.pair), custom_call_target="tpu_custom_call" | custom-call | tf_op jit(solution)/shard_map/pallas_call | solution.py:186
  15.2 0.0 collective-permute-done.6.refs_0_
  15.2 0.8 %shard_map.76.refs_5_ = bf16[128,1024]{1,0:T(8,128)(2,1)S(1)} custom-call(bf16[1024,1024]{1,0:T(8,128)(2,1)S(1)} %get-tuple-element.21.rotator_ref, bf16[1024,1024]{1,0:T(8,128)(2,1)S(1)} %get-tuple-element.28.other_ref, bf16[128,1024]{1,0:T(8,128)(2,1)S(1)} %collective-permute-done.6.refs_0_), custom_call_target="tpu_custom_call" | custom-call | tf_op jit(solution)/shard_map/pallas_call | solution.py:199
  16.0 1.1 %collective-permute-done.4.refs_2_ = bf16[96,1024]{1,0:T(8,128)(2,1)S(1)} collective-permute-done((bf16[96,1024]{1,0:T(8,128)(2,1)S(1)}, bf16[96,1024]{1,0:T(8,128)(2,1)S(1)}, u32[]{:S(2)}, u32[]{:S(2)}) %collective-permute-start.4) | collective-permute-done | bytes 196640 | tf_op jit(solution)/shard_map/ppermute | solution.py:244
  17.1 0.0 collective-permute-start.7
  17.1 0.0 collective-permute-done.3.refs_1_
  17.1 1.4 %collective-permute-done.7.refs_3_ = bf16[96,1024]{1,0:T(8,128)(2,1)S(1)} collective-permute-done((bf16[96,1024]{1,0:T(8,128)(2,1)S(1)}, bf16[96,1024]{1,0:T(8,128)(2,1)S(1)}, u32[]{:S(2)}, u32[]{:S(2)}) %collective-permute-start.7) | collective-permute-done | bytes 196640 | tf_op jit(solution)/shard_map/ppermute | solution.py:244
  18.5 0.9 %shard_map.77 = (f32[64,128]{1,0:T(8,128)S(1)}, f32[64,128]{1,0:T(8,128)S(1)}) custom-call(bf16[128,192]{1,0:T(8,128)(2,1)S(1)} %get-tuple-element.19.pick_ref, bf16[96,1024]{1,0:T(8,128)(2,1)S(1)} %shard_map.74.refs_0_, bf16[96,1024]{1,0:T(8,128)(2,1)S(1)} %collective-permute-done.3.refs_1_, bf16[96,1024]{1,0:T(8,128)(2,1)S(1)} %collective-permute-done.4.refs_2_, ...), custom_call_target="tpu_custom_call" | custom-call | tf_op jit(solution)/shard_map/pallas_call | solution.py:234
  19.5 1.6 %collective-permute-start.8 = (f32[64,128]{1,0:T(8,128)S(1)}, f32[64,128]{1,0:T(8,128)S(1)}, u32[]{:S(2)}, u32[]{:S(2)}) collective-permute-start(f32[64,128]{1,0:T(8,128)S(1)} %get-tuple-element.32), channel_id=1, source_target_pairs={{0,2},{1,3},{2,0},{3,1},{4,6},{5,7},{6,4},{7,5},{8,10},{9,11},{10,... | collective-permute-start | bytes 98312 | tf_op jit(solution)/shard_map/ppermute | solution.py:244
  21.1 2.4 %collective-permute-done.8 = f32[64,128]{1,0:T(8,128)S(1)} collective-permute-done((f32[64,128]{1,0:T(8,128)S(1)}, f32[64,128]{1,0:T(8,128)S(1)}, u32[]{:S(2)}, u32[]{:S(2)}) %collective-permute-start.8) | collective-permute-done | bytes 32800 | tf_op jit(solution)/shard_map/ppermute | solution.py:244
  23.5 0.6 %add.3 = f32[64,128]{1,0:T(8,128)} add(f32[64,128]{1,0:T(8,128)S(1)} %get-tuple-element.31, f32[64,128]{1,0:T(8,128)S(1)} %collective-permute-done.8) | non-fusion elementwise | flops 8192 | bytes 98304 | tf_op jit(solution)/shard_map/add | solution.py:281
Async XLA Ops:
  0.0 8.9 %collective-permute-start = (bf16[32,1024]{1,0:T(8,128)(2,1)}, bf16[32,1024]{1,0:T(8,128)(2,1)S(1)}, u32[]{:S(2)}, u32[]{:S(2)}) collective-permute-start(bf16[32,1024]{1,0:T(8,128)(2,1)} %bitcast.1), channel_id=1, source_target_pairs={{0,16},{4,20},{8,24},{12,28},{16,0},{20,4},{24,8},{28,12},{1,17},{... | collective-permute-start | bytes 196616 | tf_op jit(solution)/shard_map/ppermute | solution.py:244
  4.0 6.4 %collective-permute-start.1 = (bf16[32,1024]{1,0:T(8,128)(2,1)}, bf16[32,1024]{1,0:T(8,128)(2,1)S(1)}, u32[]{:S(2)}, u32[]{:S(2)}) collective-permute-start(bf16[32,1024]{1,0:T(8,128)(2,1)} %bitcast.2), channel_id=1, source_target_pairs={{0,24},{4,28},{8,16},{12,20},{16,8},{20,12},{24,0},{28,4},{1,25},{... | collective-permute-start | bytes 196616 | tf_op jit(solution)/shard_map/ppermute | solution.py:244
  5.4 5.2 %collective-permute-start.2 = (bf16[32,1024]{1,0:T(8,128)(2,1)}, bf16[32,1024]{1,0:T(8,128)(2,1)S(1)}, u32[]{:S(2)}, u32[]{:S(2)}) collective-permute-start(bf16[32,1024]{1,0:T(8,128)(2,1)} %bitcast.3), channel_id=1, source_target_pairs={{0,8},{4,12},{8,0},{12,4},{16,24},{20,28},{24,16},{28,20},{1,9},{5... | collective-permute-start | bytes 196616 | tf_op jit(solution)/shard_map/ppermute | solution.py:244
  7.3 7.9 %collective-permute-start.6 = (bf16[128,1024]{1,0:T(8,128)(2,1)S(1)}, bf16[128,1024]{1,0:T(8,128)(2,1)S(1)}, u32[]{:S(2)}, u32[]{:S(2)}) collective-permute-start(bf16[128,1024]{1,0:T(8,128)(2,1)S(1)} %get-tuple-element.29), channel_id=1, source_target_pairs={{0,2},{1,3},{2,0},{3,1},{4,6},{5,7},{6,4},{7,5},{8,10},{9,11},{10,... | collective-permute-start | bytes 786440 | tf_op jit(solution)/shard_map/ppermute | solution.py:244
  11.4 5.7 %collective-permute-start.4 = (bf16[96,1024]{1,0:T(8,128)(2,1)S(1)}, bf16[96,1024]{1,0:T(8,128)(2,1)S(1)}, u32[]{:S(2)}, u32[]{:S(2)}) collective-permute-start(bf16[96,1024]{1,0:T(8,128)(2,1)S(1)} %shard_map.74.refs_0_), channel_id=1, source_target_pairs={{0,4},{4,0},{8,12},{12,8},{16,20},{20,16},{24,28},{28,24},{1,5},{5... | collective-permute-start | bytes 589832 | tf_op jit(solution)/shard_map/ppermute | solution.py:244
  12.9 1.2 %collective-permute-start.5 = (bf16[64,32]{1,0:T(8,128)(2,1)S(1)}, bf16[64,32]{1,0:T(8,128)(2,1)S(1)}, u32[]{:S(2)}, u32[]{:S(2)}) collective-permute-start(bf16[64,32]{1,0:T(8,128)(2,1)S(1)} %get-tuple-element.24), channel_id=1, source_target_pairs={{0,1},{1,0},{2,3},{3,2},{4,5},{5,4},{6,7},{7,6},{8,9},{9,8},{10,11... | collective-permute-start | bytes 12296 | tf_op jit(solution)/shard_map/ppermute | solution.py:244
  12.9 4.2 %collective-permute-start.3 = (bf16[96,1024]{1,0:T(8,128)(2,1)S(1)}, bf16[96,1024]{1,0:T(8,128)(2,1)S(1)}, u32[]{:S(2)}, u32[]{:S(2)}) collective-permute-start(bf16[96,1024]{1,0:T(8,128)(2,1)S(1)} %shard_map.74.refs_0_), channel_id=1, source_target_pairs={{0,1},{1,0},{2,3},{3,2},{4,5},{5,4},{6,7},{7,6},{8,9},{9,8},{10,11... | collective-permute-start | bytes 589832 | tf_op jit(solution)/shard_map/ppermute | solution.py:244
  17.1 1.4 %collective-permute-start.7 = (bf16[96,1024]{1,0:T(8,128)(2,1)S(1)}, bf16[96,1024]{1,0:T(8,128)(2,1)S(1)}, u32[]{:S(2)}, u32[]{:S(2)}) collective-permute-start(bf16[96,1024]{1,0:T(8,128)(2,1)S(1)} %collective-permute-done.4.refs_2_), channel_id=1, source_target_pairs={{0,1},{1,0},{2,3},{3,2},{4,5},{5,4},{6,7},{7,6},{8,9},{9,8},{10,11... | collective-permute-start | bytes 589832 | tf_op jit(solution)/shard_map/ppermute | solution.py:244
  19.5 4.0 %collective-permute-start.8 = (f32[64,128]{1,0:T(8,128)S(1)}, f32[64,128]{1,0:T(8,128)S(1)}, u32[]{:S(2)}, u32[]{:S(2)}) collective-permute-start(f32[64,128]{1,0:T(8,128)S(1)} %get-tuple-element.32), channel_id=1, source_target_pairs={{0,2},{1,3},{2,0},{3,1},{4,6},{5,7},{6,4},{7,5},{8,10},{9,11},{10,... | collective-permute-start | bytes 98312 | tf_op jit(solution)/shard_map/ppermute | solution.py:244

commit v5 on v4

--- a/solution.py
+++ b/solution.py
@@ -139,12 +139,11 @@
 
 def ask_kernel(order, send_ref, rotator_ref, inverse_ref, *refs):
     *blocks, out = refs
-    each = blocks[0].shape[0]
-    queries = 0.0
-    for b, block in zip(order, blocks):
-        queries += jnp.dot(
-            send_ref[:, b * each : (b + 1) * each], block[...], preferred_element_type=jnp.float32
-        )
+    queries = jnp.dot(
+        send_ref[...],
+        jnp.concatenate([blocks[order.index(b)][...] for b in range(len(order))], axis=0),
+        preferred_element_type=jnp.float32,
+    )
     out[...] = (
         inverse_ref[...]
         * jnp.dot(queries.astype(jnp.bfloat16), rotator_ref[...], preferred_element_type=jnp.float32)
@@ -205,39 +204,56 @@
     )(rotator, other, *pairs)
 
 
-def score_kernel(inner, factor, pick_ref, *refs):
-    columns, refs = refs[: 2 * inner], refs[2 * inner :]
+def add_scores(total, pick_ref, columns, half, pairs):
+    span, rows = columns[0][1].shape[0], pairs[0].shape[0] // 2
+    first, last = columns[0][0], columns[-1][0]
+    asked = jnp.dot(
+        pick_ref[:, first * span : (last + 1) * span],
+        jnp.concatenate([places[...] for _, places in columns], axis=0),
+        preferred_element_type=jnp.float32,
+    )
+    turned = [pair[half * rows : (half + 1) * rows, :] for pair in pairs]
+    return total + lax.dot_general(
+        jnp.concatenate(turned, axis=0),
+        asked.astype(jnp.bfloat16),
+        (((1,), (1,)), ((), ())),
+        preferred_element_type=jnp.float32,
+    )
+
+
+def early_kernel(inner, pick_ref, *refs):
+    asked, pairs, out = refs[: inner + 1], refs[inner + 1 : -1], refs[-1]
+    total = add_scores(0.0, pick_ref, list(enumerate(asked[:inner])), 0, pairs)
+    out[...] = add_scores(total, pick_ref, [(0, asked[inner])], 1, pairs)
+
+
+def late_kernel(inner, factor, pick_ref, early_ref, *refs):
+    asked, refs = refs[: inner - 1], refs[inner - 1 :]
     pairs, outs = refs[: len(refs) // 2], refs[len(refs) // 2 :]
-    span, rows = columns[0].shape[0], outs[0].shape[0]
-    total = 0.0
-    for half in range(2):
-        asked = 0.0
-        for column in range(inner):
-            asked += jnp.dot(
-                pick_ref[:, column * span : (column + 1) * span],
-                columns[2 * column + half][...],
-                preferred_element_type=jnp.float32,
-            )
-        turned = [pair[half * rows : (half + 1) * rows, :] for pair in pairs]
-        total += lax.dot_general(
-            jnp.concatenate(turned, axis=0),
-            asked.astype(jnp.bfloat16),
-            (((1,), (1,)), ((), ())),
-            preferred_element_type=jnp.float32,
-        )
+    total = add_scores(early_ref[...], pick_ref, list(enumerate(asked, 1)), 1, pairs)
+    rows = outs[0].shape[0]
     for j, out in enumerate(outs):
         out[...] = factor * total[j * rows : (j + 1) * rows, :]
 
 
-def score(pick, columns, pairs, factor):
-    part = jax.ShapeDtypeStruct((pairs[0].shape[0] // 2, pick.shape[0]), jnp.float32)
-    return pl.pallas_call(
-        functools.partial(score_kernel, len(columns) // 2, factor),
-        out_shape=(part,) * len(pairs),
-        in_specs=[VMEM] * (1 + len(columns) + len(pairs)),
-        out_specs=(VMEM,) * len(pairs),
-        compiler_params=PARAMS,
-    )(pick, *columns, *pairs)
+def score(pick, mine, others, turned, factor):
+    inner = 1 + len(others)
+    rows = turned[0].shape[0] // 2
+    early = pl.pallas_call(
+        functools.partial(early_kernel, inner),
+        out_shape=jax.ShapeDtypeStruct((len(turned) * rows, pick.shape[0]), jnp.float32),
+        in_specs=[VMEM] * (2 + inner + len(turned)),
+        out_specs=VMEM,
+        compiler_params=PARAMS,
+    )(pick, mine[0], *(own for own, _ in others), mine[1], *turned)
+    part = jax.ShapeDtypeStruct((rows, pick.shape[0]), jnp.float32)
+    return pl.pallas_call(
+        functools.partial(late_kernel, inner, factor),
+        out_shape=(part,) * len(turned),
+        in_specs=[VMEM] * (1 + inner + len(turned)),
+        out_specs=(VMEM,) * len(turned),
+        compiler_params=PARAMS,
+    )(pick, early, *(other for _, other in others), *turned)
 
 
 def swap(array, axis, bits):
@@ -271,11 +287,10 @@
     mine = ask(send, rotator, inverse, blocks)
     other, turned = turn(after(swap(bases, "module", 1), mine), rotator, pairs[0])
     turned = [turned, *turn_more(rotator, other, sent)]
-    columns = [mine, swap(mine, "module", 1)]
-    for near in range(1, inner):
-        theirs = swap(mine, "group", near)
-        columns += [theirs, swap(after(theirs, *turned), "module", 1)]
-    parts = score(pick, columns, turned, 1.0 / math.sqrt(modules * width))
+    theirs = [swap(mine, "group", near) for near in range(1, inner)]
+    others = [(own, swap(after(own, *turned), "module", 1)) for own in theirs]
+    factor = 1.0 / math.sqrt(modules * width)
+    parts = score(pick, (mine, swap(mine, "module", 1)), others, turned, factor)
     total = parts[0]
     for j in range(1, modules // 2):
         total = total + swap(parts[j], "module", 2 * j)

time: 24.3 us -> 23.6 us (0.971)
  waiting for transfers between devices: 7.23 us -> 6.58 us
    ppermute x9, waiting for transfers between devices: 7.23 us -> 6.58 us  [swap(): lax.ppermute(array, axis, [(i, i ^ bits) for i in range(lax.axis_size(axi...]
    pallas_call x1 -> x2, Pallas kernels: 0.93 us -> 1.1 us  [the longest x1 0.67 us: score(): pl.pallas_call(functools.partial(early_kernel, inner), out_shape=jax.Shap...]
  transfers between devices with their start and end apart: 9 -> 9, of which waited for: 6 -> 6; matrix products, arithmetic and copies ran while one was open for 0% -> 0% of each run, Pallas kernels for 18% -> 21%
where the time goes in v5:
time: 23.6 us; the launch traced here: 23.4 us
  starting transfers between devices  10.9 us (46%)
  waiting for transfers between devices  6.58 us (28%)
  Pallas kernels  5.27 us (22%)
  other arithmetic  0.62 us (3%)
    ppermute x9, starting transfers between devices, swap(): lax.ppermute(array, axis, [(i, i ^ bits) for i in range(lax.axis_size(axi...  10.9 us
    ppermute x9, waiting for transfers between devices, swap(): lax.ppermute(array, axis, [(i, i ^ bits) for i in range(lax.axis_size(axi...  6.58 us
    pallas_call x1, Pallas kernels, prepare(): pl.pallas_call(functools.partial(prepare_kernel, inner, each), out_shape=...  1.69 us
    pallas_call x1, Pallas kernels, turn(): pl.pallas_call(turn_kernel, out_shape=(jax.ShapeDtypeStruct(rotator.shape...  1.05 us
    pallas_call x1, Pallas kernels, turn_more(): pl.pallas_call(turn_more_kernel, out_shape=tuple((jax.ShapeDtypeStruct(pa...  0.84 us
    pallas_call x1, Pallas kernels, score(): pl.pallas_call(functools.partial(early_kernel, inner), out_shape=jax.Shap...  0.67 us
    add x1, other arithmetic, local(): total = total + swap(parts[j], 'module', 2 * j)  0.62 us
    pallas_call x1, Pallas kernels, ask(): pl.pallas_call(functools.partial(ask_kernel, order), out_shape=jax.ShapeD...  0.59 us
  transfers between devices with their start and end apart: 9, of which 6 were waited for; matrix products, arithmetic and copies ran while one was open for 0% of the time, Pallas kernels for 21%

profile of v5, /device:TPU:0, one launch (start us, length us, event | category | flops | bytes accessed | tf_op | source)
XLA Modules:
  0.0 23.4 jit_solution(15021919080652994356)
XLA Ops:
  0.0 4.0 %collective-permute-start = (bf16[32,1024]{1,0:T(8,128)(2,1)}, bf16[32,1024]{1,0:T(8,128)(2,1)S(1)}, u32[]{:S(2)}, u32[]{:S(2)}) collective-permute-start(bf16[32,1024]{1,0:T(8,128)(2,1)} %bitcast.1), channel_id=1, source_target_pairs={{0,16},{4,20},{8,24},{12,28},{16,0},{20,4},{24,8},{28,12},{1,17},{... | collective-permute-start | bytes 196616 | tf_op jit(solution)/shard_map/ppermute | solution.py:260
  4.0 1.3 %collective-permute-start.1 = (bf16[32,1024]{1,0:T(8,128)(2,1)}, bf16[32,1024]{1,0:T(8,128)(2,1)S(1)}, u32[]{:S(2)}, u32[]{:S(2)}) collective-permute-start(bf16[32,1024]{1,0:T(8,128)(2,1)} %bitcast.2), channel_id=1, source_target_pairs={{0,24},{4,28},{8,16},{12,20},{16,8},{20,12},{24,0},{28,4},{1,25},{... | collective-permute-start | bytes 196616 | tf_op jit(solution)/shard_map/ppermute | solution.py:260
  5.4 0.2 collective-permute-start.2
  5.6 1.7 %shard_map.73 = (bf16[1024,1024]{1,0:T(8,128)(2,1)S(1)}, f32[1,1024]{1,0:T(1,128)S(1)}, bf16[96,128]{1,0:T(8,128)(2,1)S(1)}, bf16[128,192]{1,0:T(8,128)(2,1)S(1)...) custom-call(s32[4]{0:T(128)} %order_hbm.1, ...), custom_call_target="tpu_custom_call" | custom-call | tf_op jit(solution)/shard_map/pallas_call | solution.py:116
  7.3 1.6 %collective-permute-start.6 = (bf16[128,1024]{1,0:T(8,128)(2,1)S(1)}, bf16[128,1024]{1,0:T(8,128)(2,1)S(1)}, u32[]{:S(2)}, u32[]{:S(2)}) collective-permute-start(bf16[128,1024]{1,0:T(8,128)(2,1)S(1)} %get-tuple-element.29), channel_id=1, source_target_pairs={{0,2},{1,3},{2,0},{3,1},{4,6},{5,7},{6,4},{7,5},{8,10},{9,11},{10,... | collective-permute-start | bytes 786440 | tf_op jit(solution)/shard_map/ppermute | solution.py:260
  8.9 0.0 collective-permute-done.refs_0_
  8.9 1.6 %collective-permute-done.1.refs_1_ = bf16[32,1024]{1,0:T(8,128)(2,1)S(1)} collective-permute-done((bf16[32,1024]{1,0:T(8,128)(2,1)}, bf16[32,1024]{1,0:T(8,128)(2,1)S(1)}, u32[]{:S(2)}, u32[]{:S(2)}) %collective-permute-start.1) | collective-permute-done | bytes 65568 | tf_op jit(solution)/shard_map/ppermute | solution.py:260
  10.5 0.1 collective-permute-done.2.refs_2_
  10.6 0.6 %shard_map.74.refs_0_ = bf16[96,1024]{1,0:T(8,128)(2,1)S(1)} custom-call(bf16[96,128]{1,0:T(8,128)(2,1)S(1)} %get-tuple-element.20.send_ref, bf16[1024,1024]{1,0:T(8,128)(2,1)S(1)} %get-tuple-element.21.rotator_ref, f32[1,1024]{1,0:T(1,128)S(1)} %get-tuple-element.22.inverse_ref, bf16[32,1024]{1,0:T(8,128)(2,1)S(1)} %collective-permute-done.refs_0_, ...), custom_call_target="tpu_custom_call" | custom-call | tf_op jit(solution)/shard_map/pallas_call | solution.py:155
  11.2 1.6 %collective-permute-start.3 = (bf16[96,1024]{1,0:T(8,128)(2,1)S(1)}, bf16[96,1024]{1,0:T(8,128)(2,1)S(1)}, u32[]{:S(2)}, u32[]{:S(2)}) collective-permute-start(bf16[96,1024]{1,0:T(8,128)(2,1)S(1)} %shard_map.74.refs_0_), channel_id=1, source_target_pairs={{0,4},{4,0},{8,12},{12,8},{16,20},{20,16},{24,28},{28,24},{1,5},{5... | collective-permute-start | bytes 589832 | tf_op jit(solution)/shard_map/ppermute | solution.py:260
  12.7 0.0 collective-permute-start.5
  12.7 0.5 %collective-permute-start.4 = (bf16[96,1024]{1,0:T(8,128)(2,1)S(1)}, bf16[96,1024]{1,0:T(8,128)(2,1)S(1)}, u32[]{:S(2)}, u32[]{:S(2)}) collective-permute-start(bf16[96,1024]{1,0:T(8,128)(2,1)S(1)} %shard_map.74.refs_0_), channel_id=1, source_target_pairs={{0,1},{1,0},{2,3},{3,2},{4,5},{5,4},{6,7},{7,6},{8,9},{9,8},{10,11... | collective-permute-start | bytes 589832 | tf_op jit(solution)/shard_map/ppermute | solution.py:260
  13.2 0.7 %collective-permute-done.5.bases_ref = bf16[64,32]{1,0:T(8,128)(2,1)S(1)} collective-permute-done((bf16[64,32]{1,0:T(8,128)(2,1)S(1)}, bf16[64,32]{1,0:T(8,128)(2,1)S(1)}, u32[]{:S(2)}, u32[]{:S(2)}) %collective-permute-start.5) | collective-permute-done | bytes 4128 | tf_op jit(solution)/shard_map/ppermute | solution.py:260
  13.9 1.1 %shard_map.75 = (bf16[1024,1024]{1,0:T(8,128)(2,1)S(1)}, bf16[128,1024]{1,0:T(8,128)(2,1)S(1)}) custom-call(bf16[64,32]{1,0:T(8,128)(2,1)S(1)} %collective-permute-done.5.bases_ref, bf16[1024,1024]{1,0:T(8,128)(2,1)S(1)} %get-tuple-element.21.rotator_ref, bf16[128,1024]{1,0:T(8,128)(2,1)S(1)} %get-tuple-element.26.pair), custom_call_target="tpu_custom_call" | custom-call | tf_op jit(solution)/shard_map/pallas_call | solution.py:185
  15.0 0.0 collective-permute-done.6.refs_0_
  15.0 0.8 %shard_map.76.refs_4_.refs_2_ = bf16[128,1024]{1,0:T(8,128)(2,1)S(1)} custom-call(bf16[1024,1024]{1,0:T(8,128)(2,1)S(1)} %get-tuple-element.21.rotator_ref, bf16[1024,1024]{1,0:T(8,128)(2,1)S(1)} %get-tuple-element.28.other_ref, bf16[128,1024]{1,0:T(8,128)(2,1)S(1)} %collective-permute-done.6.refs_0_), custom_call_target="tpu_custom_call" | custom-call | tf_op jit(solution)/shard_map/pallas_call | solution.py:198
  15.8 1.1 %collective-permute-done.3.refs_1_ = bf16[96,1024]{1,0:T(8,128)(2,1)S(1)} collective-permute-done((bf16[96,1024]{1,0:T(8,128)(2,1)S(1)}, bf16[96,1024]{1,0:T(8,128)(2,1)S(1)}, u32[]{:S(2)}, u32[]{:S(2)}) %collective-permute-start.3) | collective-permute-done | bytes 196640 | tf_op jit(solution)/shard_map/ppermute | solution.py:260
  16.9 0.0 collective-permute-start.7
  16.9 0.0 collective-permute-done.4.refs_2_
  16.9 0.7 %shard_map.77.early_ref = f32[128,128]{1,0:T(8,128)S(1)} custom-call(bf16[128,192]{1,0:T(8,128)(2,1)S(1)} %get-tuple-element.19.pick_ref, bf16[96,1024]{1,0:T(8,128)(2,1)S(1)} %shard_map.74.refs_0_, bf16[96,1024]{1,0:T(8,128)(2,1)S(1)} %collective-permute-done.3.refs_1_, bf16[96,1024]{1,0:T(8,128)(2,1)S(1)} %collective-permute-done.4.refs_2_, ...), custom_call_target="tpu_custom_call" | custom-call | tf_op jit(solution)/shard_map/pallas_call | solution.py:242
  17.6 0.8 %collective-permute-done.7.refs_0_ = bf16[96,1024]{1,0:T(8,128)(2,1)S(1)} collective-permute-done((bf16[96,1024]{1,0:T(8,128)(2,1)S(1)}, bf16[96,1024]{1,0:T(8,128)(2,1)S(1)}, u32[]{:S(2)}, u32[]{:S(2)}) %collective-permute-start.7) | collective-permute-done | bytes 196640 | tf_op jit(solution)/shard_map/ppermute | solution.py:260
  18.3 0.4 %shard_map.78 = (f32[64,128]{1,0:T(8,128)S(1)}, f32[64,128]{1,0:T(8,128)S(1)}) custom-call(bf16[128,192]{1,0:T(8,128)(2,1)S(1)} %get-tuple-element.19.pick_ref, f32[128,128]{1,0:T(8,128)S(1)} %shard_map.77.early_ref, bf16[96,1024]{1,0:T(8,128)(2,1)S(1)} %collective-permute-done.7.refs_0_, bf16[128,1024]{1,0:T(8,128)(2,1)S(1)} %get-tuple-element.27.refs_3_.refs_1_, ...), custom_call_target="tpu_custom_call" | custom-call | tf_op jit(solution)/shard_map/pallas_call | solution.py:250
  18.8 1.6 %collective-permute-start.8 = (f32[64,128]{1,0:T(8,128)S(1)}, f32[64,128]{1,0:T(8,128)S(1)}, u32[]{:S(2)}, u32[]{:S(2)}) collective-permute-start(f32[64,128]{1,0:T(8,128)S(1)} %get-tuple-element.32), channel_id=1, source_target_pairs={{0,2},{1,3},{2,0},{3,1},{4,6},{5,7},{6,4},{7,5},{8,10},{9,11},{10,... | collective-permute-start | bytes 98312 | tf_op jit(solution)/shard_map/ppermute | solution.py:260
  20.4 2.4 %collective-permute-done.8 = f32[64,128]{1,0:T(8,128)S(1)} collective-permute-done((f32[64,128]{1,0:T(8,128)S(1)}, f32[64,128]{1,0:T(8,128)S(1)}, u32[]{:S(2)}, u32[]{:S(2)}) %collective-permute-start.8) | collective-permute-done | bytes 32800 | tf_op jit(solution)/shard_map/ppermute | solution.py:260
  22.8 0.6 %add.3 = f32[64,128]{1,0:T(8,128)} add(f32[64,128]{1,0:T(8,128)S(1)} %get-tuple-element.31, f32[64,128]{1,0:T(8,128)S(1)} %collective-permute-done.8) | non-fusion elementwise | flops 8192 | bytes 98304 | tf_op jit(solution)/shard_map/add | solution.py:296
Async XLA Ops:
  0.0 8.9 %collective-permute-start = (bf16[32,1024]{1,0:T(8,128)(2,1)}, bf16[32,1024]{1,0:T(8,128)(2,1)S(1)}, u32[]{:S(2)}, u32[]{:S(2)}) collective-permute-start(bf16[32,1024]{1,0:T(8,128)(2,1)} %bitcast.1), channel_id=1, source_target_pairs={{0,16},{4,20},{8,24},{12,28},{16,0},{20,4},{24,8},{28,12},{1,17},{... | collective-permute-start | bytes 196616 | tf_op jit(solution)/shard_map/ppermute | solution.py:260
  4.0 6.4 %collective-permute-start.1 = (bf16[32,1024]{1,0:T(8,128)(2,1)}, bf16[32,1024]{1,0:T(8,128)(2,1)S(1)}, u32[]{:S(2)}, u32[]{:S(2)}) collective-permute-start(bf16[32,1024]{1,0:T(8,128)(2,1)} %bitcast.2), channel_id=1, source_target_pairs={{0,24},{4,28},{8,16},{12,20},{16,8},{20,12},{24,0},{28,4},{1,25},{... | collective-permute-start | bytes 196616 | tf_op jit(solution)/shard_map/ppermute | solution.py:260
  5.4 5.2 %collective-permute-start.2 = (bf16[32,1024]{1,0:T(8,128)(2,1)}, bf16[32,1024]{1,0:T(8,128)(2,1)S(1)}, u32[]{:S(2)}, u32[]{:S(2)}) collective-permute-start(bf16[32,1024]{1,0:T(8,128)(2,1)} %bitcast.3), channel_id=1, source_target_pairs={{0,8},{4,12},{8,0},{12,4},{16,24},{20,28},{24,16},{28,20},{1,9},{5... | collective-permute-start | bytes 196616 | tf_op jit(solution)/shard_map/ppermute | solution.py:260
  7.3 7.6 %collective-permute-start.6 = (bf16[128,1024]{1,0:T(8,128)(2,1)S(1)}, bf16[128,1024]{1,0:T(8,128)(2,1)S(1)}, u32[]{:S(2)}, u32[]{:S(2)}) collective-permute-start(bf16[128,1024]{1,0:T(8,128)(2,1)S(1)} %get-tuple-element.29), channel_id=1, source_target_pairs={{0,2},{1,3},{2,0},{3,1},{4,6},{5,7},{6,4},{7,5},{8,10},{9,11},{10,... | collective-permute-start | bytes 786440 | tf_op jit(solution)/shard_map/ppermute | solution.py:260
  11.2 5.7 %collective-permute-start.3 = (bf16[96,1024]{1,0:T(8,128)(2,1)S(1)}, bf16[96,1024]{1,0:T(8,128)(2,1)S(1)}, u32[]{:S(2)}, u32[]{:S(2)}) collective-permute-start(bf16[96,1024]{1,0:T(8,128)(2,1)S(1)} %shard_map.74.refs_0_), channel_id=1, source_target_pairs={{0,4},{4,0},{8,12},{12,8},{16,20},{20,16},{24,28},{28,24},{1,5},{5... | collective-permute-start | bytes 589832 | tf_op jit(solution)/shard_map/ppermute | solution.py:260
  12.7 1.2 %collective-permute-start.5 = (bf16[64,32]{1,0:T(8,128)(2,1)S(1)}, bf16[64,32]{1,0:T(8,128)(2,1)S(1)}, u32[]{:S(2)}, u32[]{:S(2)}) collective-permute-start(bf16[64,32]{1,0:T(8,128)(2,1)S(1)} %get-tuple-element.24), channel_id=1, source_target_pairs={{0,1},{1,0},{2,3},{3,2},{4,5},{5,4},{6,7},{7,6},{8,9},{9,8},{10,11... | collective-permute-start | bytes 12296 | tf_op jit(solution)/shard_map/ppermute | solution.py:260
  12.7 4.2 %collective-permute-start.4 = (bf16[96,1024]{1,0:T(8,128)(2,1)S(1)}, bf16[96,1024]{1,0:T(8,128)(2,1)S(1)}, u32[]{:S(2)}, u32[]{:S(2)}) collective-permute-start(bf16[96,1024]{1,0:T(8,128)(2,1)S(1)} %shard_map.74.refs_0_), channel_id=1, source_target_pairs={{0,1},{1,0},{2,3},{3,2},{4,5},{5,4},{6,7},{7,6},{8,9},{9,8},{10,11... | collective-permute-start | bytes 589832 | tf_op jit(solution)/shard_map/ppermute | solution.py:260
  16.9 1.4 %collective-permute-start.7 = (bf16[96,1024]{1,0:T(8,128)(2,1)S(1)}, bf16[96,1024]{1,0:T(8,128)(2,1)S(1)}, u32[]{:S(2)}, u32[]{:S(2)}) collective-permute-start(bf16[96,1024]{1,0:T(8,128)(2,1)S(1)} %collective-permute-done.3.refs_1_), channel_id=1, source_target_pairs={{0,1},{1,0},{2,3},{3,2},{4,5},{5,4},{6,7},{7,6},{8,9},{9,8},{10,11... | collective-permute-start | bytes 589832 | tf_op jit(solution)/shard_map/ppermute | solution.py:260
  18.8 4.0 %collective-permute-start.8 = (f32[64,128]{1,0:T(8,128)S(1)}, f32[64,128]{1,0:T(8,128)S(1)}, u32[]{:S(2)}, u32[]{:S(2)}) collective-permute-start(f32[64,128]{1,0:T(8,128)S(1)} %get-tuple-element.32), channel_id=1, source_target_pairs={{0,2},{1,3},{2,0},{3,1},{4,6},{5,7},{6,4},{7,5},{8,10},{9,11},{10,... | collective-permute-start | bytes 98312 | tf_op jit(solution)/shard_map/ppermute | solution.py:260

commit v6 on v5

--- a/solution.py
+++ b/solution.py
@@ -125,7 +125,7 @@
             pltpu.VMEM(basis_in.shape, basis_in.dtype),
             pltpu.VMEM(eigenvalues.shape, eigenvalues.dtype),
             pltpu.VMEM(train_grads.shape, train_grads.dtype),
-            pltpu.VMEM((rows * modules * width // LANES, LANES), jnp.float32),
+            pltpu.VMEM((rows * modules * width // LANES + modules, LANES), jnp.float32),
             pltpu.SemaphoreType.DMA((7,)),
         ],
         compiler_params=PARAMS,

time: 23.6 us -> 23.6 us (level)
  no operation moved by 1% of the time
where the time goes in v6:
time: 23.6 us; the launch traced here: 23.4 us
  starting transfers between devices  10.9 us (46%)
  waiting for transfers between devices  6.58 us (28%)
  Pallas kernels  5.26 us (22%)
  other arithmetic  0.62 us (3%)
    ppermute x9, starting transfers between devices, swap(): lax.ppermute(array, axis, [(i, i ^ bits) for i in range(lax.axis_size(axi...  10.9 us
    ppermute x9, waiting for transfers between devices, swap(): lax.ppermute(array, axis, [(i, i ^ bits) for i in range(lax.axis_size(axi...  6.58 us
    pallas_call x1, Pallas kernels, prepare(): pl.pallas_call(functools.partial(prepare_kernel, inner, each), out_shape=...  1.68 us
    pallas_call x1, Pallas kernels, turn(): pl.pallas_call(turn_kernel, out_shape=(jax.ShapeDtypeStruct(rotator.shape...  1.05 us
    pallas_call x1, Pallas kernels, turn_more(): pl.pallas_call(turn_more_kernel, out_shape=tuple((jax.ShapeDtypeStruct(pa...  0.84 us
    pallas_call x1, Pallas kernels, score(): pl.pallas_call(functools.partial(early_kernel, inner), out_shape=jax.Shap...  0.67 us
    add x1, other arithmetic, local(): total = total + swap(parts[j], 'module', 2 * j)  0.62 us
    pallas_call x1, Pallas kernels, ask(): pl.pallas_call(functools.partial(ask_kernel, order), out_shape=jax.ShapeD...  0.59 us
  transfers between devices with their start and end apart: 9, of which 6 were waited for; matrix products, arithmetic and copies ran while one was open for 0% of the time, Pallas kernels for 21%

profile of v6, /device:TPU:0, one launch (start us, length us, event | category | flops | bytes accessed | tf_op | source)
XLA Modules:
  0.0 23.4 jit_solution(7248611451776894197)
XLA Ops:
  0.0 4.0 %collective-permute-start = (bf16[32,1024]{1,0:T(8,128)(2,1)}, bf16[32,1024]{1,0:T(8,128)(2,1)S(1)}, u32[]{:S(2)}, u32[]{:S(2)}) collective-permute-start(bf16[32,1024]{1,0:T(8,128)(2,1)} %bitcast.1), channel_id=1, source_target_pairs={{0,16},{4,20},{8,24},{12,28},{16,0},{20,4},{24,8},{28,12},{1,17},{... | collective-permute-start | bytes 196616 | tf_op jit(solution)/shard_map/ppermute | solution.py:260
  4.0 1.3 %collective-permute-start.1 = (bf16[32,1024]{1,0:T(8,128)(2,1)}, bf16[32,1024]{1,0:T(8,128)(2,1)S(1)}, u32[]{:S(2)}, u32[]{:S(2)}) collective-permute-start(bf16[32,1024]{1,0:T(8,128)(2,1)} %bitcast.2), channel_id=1, source_target_pairs={{0,24},{4,28},{8,16},{12,20},{16,8},{20,12},{24,0},{28,4},{1,25},{... | collective-permute-start | bytes 196616 | tf_op jit(solution)/shard_map/ppermute | solution.py:260
  5.4 0.2 collective-permute-start.2
  5.6 1.7 %shard_map.73 = (bf16[1024,1024]{1,0:T(8,128)(2,1)S(1)}, f32[1,1024]{1,0:T(1,128)S(1)}, bf16[96,128]{1,0:T(8,128)(2,1)S(1)}, bf16[128,192]{1,0:T(8,128)(2,1)S(1)...) custom-call(s32[4]{0:T(128)} %order_hbm.1, ...), custom_call_target="tpu_custom_call" | custom-call | tf_op jit(solution)/shard_map/pallas_call | solution.py:116
  7.3 1.6 %collective-permute-start.6 = (bf16[128,1024]{1,0:T(8,128)(2,1)S(1)}, bf16[128,1024]{1,0:T(8,128)(2,1)S(1)}, u32[]{:S(2)}, u32[]{:S(2)}) collective-permute-start(bf16[128,1024]{1,0:T(8,128)(2,1)S(1)} %get-tuple-element.29), channel_id=1, source_target_pairs={{0,2},{1,3},{2,0},{3,1},{4,6},{5,7},{6,4},{7,5},{8,10},{9,11},{10,... | collective-permute-start | bytes 786440 | tf_op jit(solution)/shard_map/ppermute | solution.py:260
  8.9 0.0 collective-permute-done.refs_0_
  8.9 1.6 %collective-permute-done.1.refs_1_ = bf16[32,1024]{1,0:T(8,128)(2,1)S(1)} collective-permute-done((bf16[32,1024]{1,0:T(8,128)(2,1)}, bf16[32,1024]{1,0:T(8,128)(2,1)S(1)}, u32[]{:S(2)}, u32[]{:S(2)}) %collective-permute-start.1) | collective-permute-done | bytes 65568 | tf_op jit(solution)/shard_map/ppermute | solution.py:260
  10.5 0.1 collective-permute-done.2.refs_2_
  10.6 0.6 %shard_map.74.refs_0_ = bf16[96,1024]{1,0:T(8,128)(2,1)S(1)} custom-call(bf16[96,128]{1,0:T(8,128)(2,1)S(1)} %get-tuple-element.20.send_ref, bf16[1024,1024]{1,0:T(8,128)(2,1)S(1)} %get-tuple-element.21.rotator_ref, f32[1,1024]{1,0:T(1,128)S(1)} %get-tuple-element.22.inverse_ref, bf16[32,1024]{1,0:T(8,128)(2,1)S(1)} %collective-permute-done.refs_0_, ...), custom_call_target="tpu_custom_call" | custom-call | tf_op jit(solution)/shard_map/pallas_call | solution.py:155
  11.2 1.6 %collective-permute-start.3 = (bf16[96,1024]{1,0:T(8,128)(2,1)S(1)}, bf16[96,1024]{1,0:T(8,128)(2,1)S(1)}, u32[]{:S(2)}, u32[]{:S(2)}) collective-permute-start(bf16[96,1024]{1,0:T(8,128)(2,1)S(1)} %shard_map.74.refs_0_), channel_id=1, source_target_pairs={{0,4},{4,0},{8,12},{12,8},{16,20},{20,16},{24,28},{28,24},{1,5},{5... | collective-permute-start | bytes 589832 | tf_op jit(solution)/shard_map/ppermute | solution.py:260
  12.7 0.0 collective-permute-start.5
  12.7 0.5 %collective-permute-start.4 = (bf16[96,1024]{1,0:T(8,128)(2,1)S(1)}, bf16[96,1024]{1,0:T(8,128)(2,1)S(1)}, u32[]{:S(2)}, u32[]{:S(2)}) collective-permute-start(bf16[96,1024]{1,0:T(8,128)(2,1)S(1)} %shard_map.74.refs_0_), channel_id=1, source_target_pairs={{0,1},{1,0},{2,3},{3,2},{4,5},{5,4},{6,7},{7,6},{8,9},{9,8},{10,11... | collective-permute-start | bytes 589832 | tf_op jit(solution)/shard_map/ppermute | solution.py:260
  13.2 0.7 %collective-permute-done.5.bases_ref = bf16[64,32]{1,0:T(8,128)(2,1)S(1)} collective-permute-done((bf16[64,32]{1,0:T(8,128)(2,1)S(1)}, bf16[64,32]{1,0:T(8,128)(2,1)S(1)}, u32[]{:S(2)}, u32[]{:S(2)}) %collective-permute-start.5) | collective-permute-done | bytes 4128 | tf_op jit(solution)/shard_map/ppermute | solution.py:260
  13.9 1.1 %shard_map.75 = (bf16[1024,1024]{1,0:T(8,128)(2,1)S(1)}, bf16[128,1024]{1,0:T(8,128)(2,1)S(1)}) custom-call(bf16[64,32]{1,0:T(8,128)(2,1)S(1)} %collective-permute-done.5.bases_ref, bf16[1024,1024]{1,0:T(8,128)(2,1)S(1)} %get-tuple-element.21.rotator_ref, bf16[128,1024]{1,0:T(8,128)(2,1)S(1)} %get-tuple-element.26.pair), custom_call_target="tpu_custom_call" | custom-call | tf_op jit(solution)/shard_map/pallas_call | solution.py:185
  15.0 0.0 collective-permute-done.6.refs_0_
  15.0 0.8 %shard_map.76.refs_4_.refs_2_ = bf16[128,1024]{1,0:T(8,128)(2,1)S(1)} custom-call(bf16[1024,1024]{1,0:T(8,128)(2,1)S(1)} %get-tuple-element.21.rotator_ref, bf16[1024,1024]{1,0:T(8,128)(2,1)S(1)} %get-tuple-element.28.other_ref, bf16[128,1024]{1,0:T(8,128)(2,1)S(1)} %collective-permute-done.6.refs_0_), custom_call_target="tpu_custom_call" | custom-call | tf_op jit(solution)/shard_map/pallas_call | solution.py:198
  15.8 1.1 %collective-permute-done.3.refs_1_ = bf16[96,1024]{1,0:T(8,128)(2,1)S(1)} collective-permute-done((bf16[96,1024]{1,0:T(8,128)(2,1)S(1)}, bf16[96,1024]{1,0:T(8,128)(2,1)S(1)}, u32[]{:S(2)}, u32[]{:S(2)}) %collective-permute-start.3) | collective-permute-done | bytes 196640 | tf_op jit(solution)/shard_map/ppermute | solution.py:260
  16.9 0.0 collective-permute-start.7
  16.9 0.0 collective-permute-done.4.refs_2_
  16.9 0.7 %shard_map.77.early_ref = f32[128,128]{1,0:T(8,128)S(1)} custom-call(bf16[128,192]{1,0:T(8,128)(2,1)S(1)} %get-tuple-element.19.pick_ref, bf16[96,1024]{1,0:T(8,128)(2,1)S(1)} %shard_map.74.refs_0_, bf16[96,1024]{1,0:T(8,128)(2,1)S(1)} %collective-permute-done.3.refs_1_, bf16[96,1024]{1,0:T(8,128)(2,1)S(1)} %collective-permute-done.4.refs_2_, ...), custom_call_target="tpu_custom_call" | custom-call | tf_op jit(solution)/shard_map/pallas_call | solution.py:242
  17.6 0.8 %collective-permute-done.7.refs_0_ = bf16[96,1024]{1,0:T(8,128)(2,1)S(1)} collective-permute-done((bf16[96,1024]{1,0:T(8,128)(2,1)S(1)}, bf16[96,1024]{1,0:T(8,128)(2,1)S(1)}, u32[]{:S(2)}, u32[]{:S(2)}) %collective-permute-start.7) | collective-permute-done | bytes 196640 | tf_op jit(solution)/shard_map/ppermute | solution.py:260
  18.3 0.4 %shard_map.78 = (f32[64,128]{1,0:T(8,128)S(1)}, f32[64,128]{1,0:T(8,128)S(1)}) custom-call(bf16[128,192]{1,0:T(8,128)(2,1)S(1)} %get-tuple-element.19.pick_ref, f32[128,128]{1,0:T(8,128)S(1)} %shard_map.77.early_ref, bf16[96,1024]{1,0:T(8,128)(2,1)S(1)} %collective-permute-done.7.refs_0_, bf16[128,1024]{1,0:T(8,128)(2,1)S(1)} %get-tuple-element.27.refs_3_.refs_1_, ...), custom_call_target="tpu_custom_call" | custom-call | tf_op jit(solution)/shard_map/pallas_call | solution.py:250
  18.8 1.6 %collective-permute-start.8 = (f32[64,128]{1,0:T(8,128)S(1)}, f32[64,128]{1,0:T(8,128)S(1)}, u32[]{:S(2)}, u32[]{:S(2)}) collective-permute-start(f32[64,128]{1,0:T(8,128)S(1)} %get-tuple-element.32), channel_id=1, source_target_pairs={{0,2},{1,3},{2,0},{3,1},{4,6},{5,7},{6,4},{7,5},{8,10},{9,11},{10,... | collective-permute-start | bytes 98312 | tf_op jit(solution)/shard_map/ppermute | solution.py:260
  20.4 2.4 %collective-permute-done.8 = f32[64,128]{1,0:T(8,128)S(1)} collective-permute-done((f32[64,128]{1,0:T(8,128)S(1)}, f32[64,128]{1,0:T(8,128)S(1)}, u32[]{:S(2)}, u32[]{:S(2)}) %collective-permute-start.8) | collective-permute-done | bytes 32800 | tf_op jit(solution)/shard_map/ppermute | solution.py:260
  22.8 0.6 %add.3 = f32[64,128]{1,0:T(8,128)} add(f32[64,128]{1,0:T(8,128)S(1)} %get-tuple-element.31, f32[64,128]{1,0:T(8,128)S(1)} %collective-permute-done.8) | non-fusion elementwise | flops 8192 | bytes 98304 | tf_op jit(solution)/shard_map/add | solution.py:296
Async XLA Ops:
  0.0 8.9 %collective-permute-start = (bf16[32,1024]{1,0:T(8,128)(2,1)}, bf16[32,1024]{1,0:T(8,128)(2,1)S(1)}, u32[]{:S(2)}, u32[]{:S(2)}) collective-permute-start(bf16[32,1024]{1,0:T(8,128)(2,1)} %bitcast.1), channel_id=1, source_target_pairs={{0,16},{4,20},{8,24},{12,28},{16,0},{20,4},{24,8},{28,12},{1,17},{... | collective-permute-start | bytes 196616 | tf_op jit(solution)/shard_map/ppermute | solution.py:260
  4.0 6.4 %collective-permute-start.1 = (bf16[32,1024]{1,0:T(8,128)(2,1)}, bf16[32,1024]{1,0:T(8,128)(2,1)S(1)}, u32[]{:S(2)}, u32[]{:S(2)}) collective-permute-start(bf16[32,1024]{1,0:T(8,128)(2,1)} %bitcast.2), channel_id=1, source_target_pairs={{0,24},{4,28},{8,16},{12,20},{16,8},{20,12},{24,0},{28,4},{1,25},{... | collective-permute-start | bytes 196616 | tf_op jit(solution)/shard_map/ppermute | solution.py:260
  5.4 5.2 %collective-permute-start.2 = (bf16[32,1024]{1,0:T(8,128)(2,1)}, bf16[32,1024]{1,0:T(8,128)(2,1)S(1)}, u32[]{:S(2)}, u32[]{:S(2)}) collective-permute-start(bf16[32,1024]{1,0:T(8,128)(2,1)} %bitcast.3), channel_id=1, source_target_pairs={{0,8},{4,12},{8,0},{12,4},{16,24},{20,28},{24,16},{28,20},{1,9},{5... | collective-permute-start | bytes 196616 | tf_op jit(solution)/shard_map/ppermute | solution.py:260
  7.3 7.6 %collective-permute-start.6 = (bf16[128,1024]{1,0:T(8,128)(2,1)S(1)}, bf16[128,1024]{1,0:T(8,128)(2,1)S(1)}, u32[]{:S(2)}, u32[]{:S(2)}) collective-permute-start(bf16[128,1024]{1,0:T(8,128)(2,1)S(1)} %get-tuple-element.29), channel_id=1, source_target_pairs={{0,2},{1,3},{2,0},{3,1},{4,6},{5,7},{6,4},{7,5},{8,10},{9,11},{10,... | collective-permute-start | bytes 786440 | tf_op jit(solution)/shard_map/ppermute | solution.py:260
  11.2 5.7 %collective-permute-start.3 = (bf16[96,1024]{1,0:T(8,128)(2,1)S(1)}, bf16[96,1024]{1,0:T(8,128)(2,1)S(1)}, u32[]{:S(2)}, u32[]{:S(2)}) collective-permute-start(bf16[96,1024]{1,0:T(8,128)(2,1)S(1)} %shard_map.74.refs_0_), channel_id=1, source_target_pairs={{0,4},{4,0},{8,12},{12,8},{16,20},{20,16},{24,28},{28,24},{1,5},{5... | collective-permute-start | bytes 589832 | tf_op jit(solution)/shard_map/ppermute | solution.py:260
  12.7 1.2 %collective-permute-start.5 = (bf16[64,32]{1,0:T(8,128)(2,1)S(1)}, bf16[64,32]{1,0:T(8,128)(2,1)S(1)}, u32[]{:S(2)}, u32[]{:S(2)}) collective-permute-start(bf16[64,32]{1,0:T(8,128)(2,1)S(1)} %get-tuple-element.24), channel_id=1, source_target_pairs={{0,1},{1,0},{2,3},{3,2},{4,5},{5,4},{6,7},{7,6},{8,9},{9,8},{10,11... | collective-permute-start | bytes 12296 | tf_op jit(solution)/shard_map/ppermute | solution.py:260
  12.7 4.2 %collective-permute-start.4 = (bf16[96,1024]{1,0:T(8,128)(2,1)S(1)}, bf16[96,1024]{1,0:T(8,128)(2,1)S(1)}, u32[]{:S(2)}, u32[]{:S(2)}) collective-permute-start(bf16[96,1024]{1,0:T(8,128)(2,1)S(1)} %shard_map.74.refs_0_), channel_id=1, source_target_pairs={{0,1},{1,0},{2,3},{3,2},{4,5},{5,4},{6,7},{7,6},{8,9},{9,8},{10,11... | collective-permute-start | bytes 589832 | tf_op jit(solution)/shard_map/ppermute | solution.py:260
  16.9 1.4 %collective-permute-start.7 = (bf16[96,1024]{1,0:T(8,128)(2,1)S(1)}, bf16[96,1024]{1,0:T(8,128)(2,1)S(1)}, u32[]{:S(2)}, u32[]{:S(2)}) collective-permute-start(bf16[96,1024]{1,0:T(8,128)(2,1)S(1)} %collective-permute-done.3.refs_1_), channel_id=1, source_target_pairs={{0,1},{1,0},{2,3},{3,2},{4,5},{5,4},{6,7},{7,6},{8,9},{9,8},{10,11... | collective-permute-start | bytes 589832 | tf_op jit(solution)/shard_map/ppermute | solution.py:260
  18.8 4.0 %collective-permute-start.8 = (f32[64,128]{1,0:T(8,128)S(1)}, f32[64,128]{1,0:T(8,128)S(1)}, u32[]{:S(2)}, u32[]{:S(2)}) collective-permute-start(f32[64,128]{1,0:T(8,128)S(1)} %get-tuple-element.32), channel_id=1, source_target_pairs={{0,2},{1,3},{2,0},{3,1},{4,6},{5,7},{6,4},{7,5},{8,10},{9,11},{10,... | collective-permute-start | bytes 98312 | tf_op jit(solution)/shard_map/ppermute | solution.py:260

commit v7 on v6

--- a/solution.py
+++ b/solution.py
@@ -93,7 +93,7 @@
             wide[pl.ds((t * rows + e) * modules, modules), :] = example[:, t * LANES : (t + 1) * LANES]
     for j in range(modules):
         held = order[slot ^ j]
-        out, at = pairs[j // 2], j % 2 * rows
+        out, at = (pairs[0], j * rows) if j < 2 else (pairs[j - 1], 0)
         for t in range(tiles):
             piece = wide[pl.ds(t * rows * modules + held, rows, stride=modules), :]
             out[at : at + rows, t * LANES : (t + 1) * LANES] = piece.astype(out.dtype)
@@ -112,7 +112,7 @@
         jax.ShapeDtypeStruct((asked * each, inner * places * each), jnp.bfloat16),
         jax.ShapeDtypeStruct(own.shape, own.dtype),
         jax.ShapeDtypeStruct((2 * basis_out.shape[1], basis_out.shape[2]), basis_out.dtype),
-    ) + (pair,) * (modules // 2)
+    ) + (pair,) + (jax.ShapeDtypeStruct((rows, width), train_grads.dtype),) * (modules - 2)
     return pl.pallas_call(
         functools.partial(prepare_kernel, inner, each),
         out_shape=shapes,
@@ -161,99 +161,84 @@
     )(send, rotator, inverse, *(blocks[b] for b in order))
 
 
-def turn_kernel(bases_ref, rotator_ref, pair, other_ref, turned):
+def turn_kernel(bases_ref, rotator_ref, pair, other_ref, *outs):
     rows, side = pair.shape[0] // 2, bases_ref.shape[1]
     build_rotator(bases_ref[:side, :], bases_ref[side:, :], other_ref)
-    turn_pair(rows, pair, rotator_ref, other_ref, turned)
-
-
-def turn_pair(rows, pair, rotator_ref, other_ref, turned):
-    for half, rotator in enumerate((rotator_ref, other_ref)):
-        at = slice(half * rows, (half + 1) * rows)
-        turned[at, :] = jnp.dot(
-            pair[at, :], rotator[...], preferred_element_type=jnp.float32
-        ).astype(turned.dtype)
+    for half, (rotator, out) in enumerate(zip((rotator_ref, other_ref), outs)):
+        out[...] = jnp.dot(
+            pair[half * rows : (half + 1) * rows, :], rotator[...], preferred_element_type=jnp.float32
+        ).astype(out.dtype)
+
+
+def turn(bases, rotator, pair):
+    half = jax.ShapeDtypeStruct((pair.shape[0] // 2, pair.shape[1]), pair.dtype)
+    return pl.pallas_call(
+        turn_kernel,
+        out_shape=(jax.ShapeDtypeStruct(rotator.shape, rotator.dtype), half, half),
+        in_specs=[VMEM] * 3,
+        out_specs=(VMEM,) * 3,
+        compiler_params=PARAMS,
+    )(bases, rotator, pair)
 
 
 def turn_more_kernel(rotator_ref, other_ref, *refs):
-    count = len(refs) // 2
-    for pair, turned in zip(refs[:count], refs[count:]):
-        turn_pair(pair.shape[0] // 2, pair, rotator_ref, other_ref, turned)
-
-
-def turn(bases, rotator, pair):
-    return pl.pallas_call(
-        turn_kernel,
-        out_shape=(
-            jax.ShapeDtypeStruct(rotator.shape, rotator.dtype),
-            jax.ShapeDtypeStruct(pair.shape, pair.dtype),
-        ),
-        in_specs=[VMEM] * 3,
+    pieces, outs = refs[:-2], refs[-2:]
+    for half, (rotator, out) in enumerate(zip((rotator_ref, other_ref), outs)):
+        out[...] = jnp.dot(
+            jnp.concatenate([piece[...] for piece in pieces[half::2]], axis=0),
+            rotator[...],
+            preferred_element_type=jnp.float32,
+        ).astype(out.dtype)
+
+
+def turn_more(rotator, other, pieces):
+    rows, width = pieces[0].shape
+    shape = jax.ShapeDtypeStruct((rows * (len(pieces) // 2), width), pieces[0].dtype)
+    return pl.pallas_call(
+        turn_more_kernel,
+        out_shape=(shape,) * 2,
+        in_specs=[VMEM] * (2 + len(pieces)),
         out_specs=(VMEM,) * 2,
         compiler_params=PARAMS,
-    )(bases, rotator, pair)
-
-
-def turn_more(rotator, other, pairs):
-    return pl.pallas_call(
-        turn_more_kernel,
-        out_shape=tuple(jax.ShapeDtypeStruct(pair.shape, pair.dtype) for pair in pairs),
-        in_specs=[VMEM] * (2 + len(pairs)),
-        out_specs=(VMEM,) * len(pairs),
-        compiler_params=PARAMS,
-    )(rotator, other, *pairs)
-
-
-def add_scores(total, pick_ref, columns, half, pairs):
-    span, rows = columns[0][1].shape[0], pairs[0].shape[0] // 2
-    first, last = columns[0][0], columns[-1][0]
+    )(rotator, other, *pieces)
+
+
+def scores_of(turned, pick_ref, first, columns):
+    span = columns[0].shape[0]
     asked = jnp.dot(
-        pick_ref[:, first * span : (last + 1) * span],
-        jnp.concatenate([places[...] for _, places in columns], axis=0),
+        pick_ref[:, first * span : (first + len(columns)) * span],
+        jnp.concatenate([places[...] for places in columns], axis=0),
         preferred_element_type=jnp.float32,
-    )
-    turned = [pair[half * rows : (half + 1) * rows, :] for pair in pairs]
-    return total + lax.dot_general(
-        jnp.concatenate(turned, axis=0),
-        asked.astype(jnp.bfloat16),
+    ).astype(jnp.bfloat16)
+    return lax.dot_general(
+        jnp.concatenate([part[...] for part in turned], axis=0),
+        asked,
         (((1,), (1,)), ((), ())),
         preferred_element_type=jnp.float32,
     )
 
 
-def early_kernel(inner, pick_ref, *refs):
-    asked, pairs, out = refs[: inner + 1], refs[inner + 1 : -1], refs[-1]
-    total = add_scores(0.0, pick_ref, list(enumerate(asked[:inner])), 0, pairs)
-    out[...] = add_scores(total, pick_ref, [(0, asked[inner])], 1, pairs)
-
-
-def late_kernel(inner, factor, pick_ref, early_ref, *refs):
-    asked, refs = refs[: inner - 1], refs[inner - 1 :]
-    pairs, outs = refs[: len(refs) // 2], refs[len(refs) // 2 :]
-    total = add_scores(early_ref[...], pick_ref, list(enumerate(asked, 1)), 1, pairs)
-    rows = outs[0].shape[0]
+def score_kernel(factor, pick_ref, mine_ref, *refs):
+    (near, far, near_got, far_got), refs = refs[:4], refs[4:]
+    rows = near.shape[0]
+    count = 2 + 2 * (far.shape[0] // rows)
+    theirs, outs = refs[:-count], refs[-count:]
+    total = scores_of([near, far, near_got, far_got], pick_ref, 0, [mine_ref, *theirs])
     for j, out in enumerate(outs):
-        out[...] = factor * total[j * rows : (j + 1) * rows, :]
-
-
-def score(pick, mine, others, turned, factor):
-    inner = 1 + len(others)
-    rows = turned[0].shape[0] // 2
-    early = pl.pallas_call(
-        functools.partial(early_kernel, inner),
-        out_shape=jax.ShapeDtypeStruct((len(turned) * rows, pick.shape[0]), jnp.float32),
-        in_specs=[VMEM] * (2 + inner + len(turned)),
-        out_specs=VMEM,
-        compiler_params=PARAMS,
-    )(pick, mine[0], *(own for own, _ in others), mine[1], *turned)
-    part = jax.ShapeDtypeStruct((rows, pick.shape[0]), jnp.float32)
-    return pl.pallas_call(
-        functools.partial(late_kernel, inner, factor),
-        out_shape=(part,) * len(turned),
-        in_specs=[VMEM] * (1 + inner + len(turned)),
-        out_specs=(VMEM,) * len(turned),
-        compiler_params=PARAMS,
-    )(pick, early, *(other for _, other in others), *turned)
+        at = (j % 2 * (count // 2) + j // 2) * rows
+        out[...] = factor * total[at : at + rows, :]
+
+
+def score(pick, mine, turned, theirs, factor):
+    rows = turned[0].shape[0]
+    count = 2 + 2 * (turned[1].shape[0] // rows)
+    return pl.pallas_call(
+        functools.partial(score_kernel, factor),
+        out_shape=(jax.ShapeDtypeStruct((rows, pick.shape[0]), jnp.float32),) * count,
+        in_specs=[VMEM] * (2 + len(turned) + len(theirs)),
+        out_specs=(VMEM,) * count,
+        compiler_params=PARAMS,
+    )(pick, mine, *turned, *theirs)
 
 
 def swap(array, axis, bits):
@@ -283,17 +268,17 @@
         len(blocks),
     )
     blocks[0] = own
-    sent = [swap(pairs[j], "module", 2 * j) for j in range(1, modules // 2)]
+    sent = [swap(pairs[j - 1], "module", j - j % 2) for j in range(2, modules)]
     mine = ask(send, rotator, inverse, blocks)
-    other, turned = turn(after(swap(bases, "module", 1), mine), rotator, pairs[0])
-    turned = [turned, *turn_more(rotator, other, sent)]
-    theirs = [swap(mine, "group", near) for near in range(1, inner)]
-    others = [(own, swap(after(own, *turned), "module", 1)) for own in theirs]
+    other, near, near_other = turn(after(swap(bases, "module", 1), mine), rotator, pairs[0])
+    far, far_other = turn_more(rotator, other, sent)
+    theirs = [swap(mine, "group", column) for column in range(1, inner)]
     factor = 1.0 / math.sqrt(modules * width)
-    parts = score(pick, (mine, swap(mine, "module", 1)), others, turned, factor)
+    got = [swap(near_other, "module", 1), swap(far_other, "module", 1)]
+    parts = score(pick, mine, (near, far, *got), theirs, factor)
     total = parts[0]
-    for j in range(1, modules // 2):
-        total = total + swap(parts[j], "module", 2 * j)
+    for j in range(1, modules):
+        total = total + swap(parts[j], "module", j)
     return total
 
 

time: 23.6 us -> 23.8 us (level)
  starting transfers between devices: 10.9 us -> 12.1 us
  Pallas kernels: 5.26 us -> 4.65 us
  waiting for transfers between devices: 6.58 us -> 6.17 us
    ppermute x9 -> x12, starting transfers between devices: 10.9 us -> 12.1 us  [swap(): lax.ppermute(array, axis, [(i, i ^ bits) for i in range(lax.axis_size(axi...]
    pallas_call x3 -> x2, Pallas kernels: 1.94 us -> 1.33 us  [the longest x1 0.85 us: turn_more(): pl.pallas_call(turn_more_kernel, out_shape=(shape,) * 2, in_specs=[VMEM]...]
    ppermute x9 -> x12, waiting for transfers between devices: 6.58 us -> 6.17 us  [swap(): lax.ppermute(array, axis, [(i, i ^ bits) for i in range(lax.axis_size(axi...]
  transfers between devices with their start and end apart: 9 -> 12, of which waited for: 6 -> 6; matrix products, arithmetic and copies ran while one was open for 0% -> 0% of each run, Pallas kernels for 21% -> 18%
where the time goes in v7:
time: 23.8 us; the launch traced here: 23.6 us
  starting transfers between devices  12.1 us (51%)
  waiting for transfers between devices  6.17 us (26%)
  Pallas kernels  4.65 us (20%)
  other arithmetic  0.63 us (3%)
    ppermute x12, starting transfers between devices, swap(): lax.ppermute(array, axis, [(i, i ^ bits) for i in range(lax.axis_size(axi...  12.1 us
    ppermute x12, waiting for transfers between devices, swap(): lax.ppermute(array, axis, [(i, i ^ bits) for i in range(lax.axis_size(axi...  6.17 us
    pallas_call x1, Pallas kernels, prepare(): pl.pallas_call(functools.partial(prepare_kernel, inner, each), out_shape=...  1.68 us
    pallas_call x1, Pallas kernels, turn(): pl.pallas_call(turn_kernel, out_shape=(jax.ShapeDtypeStruct(rotator.shape...  1.05 us
    pallas_call x1, Pallas kernels, turn_more(): pl.pallas_call(turn_more_kernel, out_shape=(shape,) * 2, in_specs=[VMEM]...  0.85 us
    add x1, other arithmetic, local(): total = total + swap(parts[j], 'module', j)  0.63 us
    pallas_call x1, Pallas kernels, ask(): pl.pallas_call(functools.partial(ask_kernel, order), out_shape=jax.ShapeD...  0.59 us
    pallas_call x1, Pallas kernels, score(): pl.pallas_call(functools.partial(score_kernel, factor), out_shape=(jax.Sh...  0.48 us
  transfers between devices with their start and end apart: 12, of which 6 were waited for; matrix products, arithmetic and copies ran while one was open for 0% of the time, Pallas kernels for 18%

profile of v7, /device:TPU:0, one launch (start us, length us, event | category | flops | bytes accessed | tf_op | source)
XLA Modules:
  0.0 23.6 jit_solution(6246103625937554774)
XLA Ops:
  0.0 4.0 %collective-permute-start = (bf16[32,1024]{1,0:T(8,128)(2,1)}, bf16[32,1024]{1,0:T(8,128)(2,1)S(1)}, u32[]{:S(2)}, u32[]{:S(2)}) collective-permute-start(bf16[32,1024]{1,0:T(8,128)(2,1)} %bitcast.1), channel_id=1, source_target_pairs={{0,16},{4,20},{8,24},{12,28},{16,0},{20,4},{24,8},{28,12},{1,17},{... | collective-permute-start | bytes 196616 | tf_op jit(solution)/shard_map/ppermute | solution.py:245
  4.0 1.3 %collective-permute-start.1 = (bf16[32,1024]{1,0:T(8,128)(2,1)}, bf16[32,1024]{1,0:T(8,128)(2,1)S(1)}, u32[]{:S(2)}, u32[]{:S(2)}) collective-permute-start(bf16[32,1024]{1,0:T(8,128)(2,1)} %bitcast.2), channel_id=1, source_target_pairs={{0,24},{4,28},{8,16},{12,20},{16,8},{20,12},{24,0},{28,4},{1,25},{... | collective-permute-start | bytes 196616 | tf_op jit(solution)/shard_map/ppermute | solution.py:245
  5.4 0.2 collective-permute-start.2
  5.6 1.7 %shard_map.73 = (bf16[1024,1024]{1,0:T(8,128)(2,1)S(1)}, f32[1,1024]{1,0:T(1,128)S(1)}, bf16[96,128]{1,0:T(8,128)(2,1)S(1)}, bf16[128,192]{1,0:T(8,128)(2,1)S(1)...) custom-call(s32[4]{0:T(128)} %order_hbm.1, ...), custom_call_target="tpu_custom_call" | custom-call | tf_op jit(solution)/shard_map/pallas_call | solution.py:116
  7.3 1.6 %collective-permute-start.4 = (bf16[64,1024]{1,0:T(8,128)(2,1)S(1)}, bf16[64,1024]{1,0:T(8,128)(2,1)S(1)}, u32[]{:S(2)}, u32[]{:S(2)}) collective-permute-start(bf16[64,1024]{1,0:T(8,128)(2,1)S(1)} %get-tuple-element.34), channel_id=1, source_target_pairs={{0,2},{1,3},{2,0},{3,1},{4,6},{5,7},{6,4},{7,5},{8,10},{9,11},{10,... | collective-permute-start | bytes 393224 | tf_op jit(solution)/shard_map/ppermute | solution.py:245
  8.9 0.5 %collective-permute-start.5 = (bf16[64,1024]{1,0:T(8,128)(2,1)S(1)}, bf16[64,1024]{1,0:T(8,128)(2,1)S(1)}, u32[]{:S(2)}, u32[]{:S(2)}) collective-permute-start(bf16[64,1024]{1,0:T(8,128)(2,1)S(1)} %get-tuple-element.35), channel_id=1, source_target_pairs={{0,2},{1,3},{2,0},{3,1},{4,6},{5,7},{6,4},{7,5},{8,10},{9,11},{10,... | collective-permute-start | bytes 393224 | tf_op jit(solution)/shard_map/ppermute | solution.py:245
  9.4 0.0 collective-permute-done.refs_0_
  9.4 1.1 %collective-permute-done.1.refs_1_ = bf16[32,1024]{1,0:T(8,128)(2,1)S(1)} collective-permute-done((bf16[32,1024]{1,0:T(8,128)(2,1)}, bf16[32,1024]{1,0:T(8,128)(2,1)S(1)}, u32[]{:S(2)}, u32[]{:S(2)}) %collective-permute-start.1) | collective-permute-done | bytes 65568 | tf_op jit(solution)/shard_map/ppermute | solution.py:245
  10.5 0.1 collective-permute-done.2.refs_2_
  10.6 0.6 %shard_map.74.mine_ref = bf16[96,1024]{1,0:T(8,128)(2,1)S(1)} custom-call(bf16[96,128]{1,0:T(8,128)(2,1)S(1)} %get-tuple-element.25.send_ref, bf16[1024,1024]{1,0:T(8,128)(2,1)S(1)} %get-tuple-element.26.rotator_ref, f32[1,1024]{1,0:T(1,128)S(1)} %get-tuple-element.27.inverse_ref, bf16[32,1024]{1,0:T(8,128)(2,1)S(1)} %collective-permute-done.refs_0_, ...), custom_call_target="tpu_custom_call" | custom-call | tf_op jit(solution)/shard_map/pallas_call | solution.py:155
  11.2 1.6 %collective-permute-start.8 = (bf16[96,1024]{1,0:T(8,128)(2,1)S(1)}, bf16[96,1024]{1,0:T(8,128)(2,1)S(1)}, u32[]{:S(2)}, u32[]{:S(2)}) collective-permute-start(bf16[96,1024]{1,0:T(8,128)(2,1)S(1)} %shard_map.74.mine_ref), channel_id=1, source_target_pairs={{0,4},{4,0},{8,12},{12,8},{16,20},{20,16},{24,28},{28,24},{1,5},{5... | collective-permute-start | bytes 589832 | tf_op jit(solution)/shard_map/ppermute | solution.py:245
  12.7 0.0 collective-permute-start.3
  12.7 1.2 %collective-permute-done.3.bases_ref = bf16[64,32]{1,0:T(8,128)(2,1)S(1)} collective-permute-done((bf16[64,32]{1,0:T(8,128)(2,1)S(1)}, bf16[64,32]{1,0:T(8,128)(2,1)S(1)}, u32[]{:S(2)}, u32[]{:S(2)}) %collective-permute-start.3) | collective-permute-done | bytes 4128 | tf_op jit(solution)/shard_map/ppermute | solution.py:245
  13.9 1.1 %shard_map.75 = (bf16[1024,1024]{1,0:T(8,128)(2,1)S(1)}, bf16[64,1024]{1,0:T(8,128)(2,1)S(1)}, bf16[64,1024]{1,0:T(8,128)(2,1)S(1)}) custom-call(bf16[64,32]{1,0:T(8,128)(2,1)S(1)} %collective-permute-done.3.bases_ref, bf16[1024,1024]{1,0:T(8,128)(2,1)S(1)} %get-tuple-element.26.rotator_ref, bf16[128,1024]{1,0:T(8,128)(2,1)S(1)} %get-tuple-element.31.pair), custom_call_target="tpu_custom_call" | custom-call | tf_op jit(solution)/shard_map/pallas_call | solution.py:175
  15.0 0.2 collective-permute-start.6
  15.2 0.0 collective-permute-done.4.refs_0_
  15.2 0.0 collective-permute-done.5.refs_1_
  15.2 0.8 %shard_map.76 = (bf16[64,1024]{1,0:T(8,128)(2,1)S(1)}, bf16[64,1024]{1,0:T(8,128)(2,1)S(1)}) custom-call(bf16[1024,1024]{1,0:T(8,128)(2,1)S(1)} %get-tuple-element.26.rotator_ref, bf16[1024,1024]{1,0:T(8,128)(2,1)S(1)} %get-tuple-element.33.other_ref, bf16[64,1024]{1,0:T(8,128)(2,1)S(1)} %collective-permute-done.4.refs_0_, ...), custom_call_target="tpu_custom_call" | custom-call | tf_op jit(solution)/shard_map/pallas_call | solution.py:197
  16.0 0.4 %collective-permute-start.7 = (bf16[64,1024]{1,0:T(8,128)(2,1)S(1)}, bf16[64,1024]{1,0:T(8,128)(2,1)S(1)}, u32[]{:S(2)}, u32[]{:S(2)}) collective-permute-start(bf16[64,1024]{1,0:T(8,128)(2,1)S(1)} %get-tuple-element.38), channel_id=1, source_target_pairs={{0,1},{1,0},{2,3},{3,2},{4,5},{5,4},{6,7},{7,6},{8,9},{9,8},{10,11... | collective-permute-start | bytes 393224 | tf_op jit(solution)/shard_map/ppermute | solution.py:245
  16.5 0.0 collective-permute-done.6.refs_2_
  16.5 1.0 %collective-permute-done.7.refs_3_ = bf16[64,1024]{1,0:T(8,128)(2,1)S(1)} collective-permute-done((bf16[64,1024]{1,0:T(8,128)(2,1)S(1)}, bf16[64,1024]{1,0:T(8,128)(2,1)S(1)}, u32[]{:S(2)}, u32[]{:S(2)}) %collective-permute-start.7) | collective-permute-done | bytes 131104 | tf_op jit(solution)/shard_map/ppermute | solution.py:245
  17.5 0.0 collective-permute-done.8.refs_4_
  17.5 0.5 %shard_map.77 = (f32[64,128]{1,0:T(8,128)S(1)}, f32[64,128]{1,0:T(8,128)S(1)}, f32[64,128]{1,0:T(8,128)S(1)}, f32[64,128]{1,0:T(8,128)S(1)}) custom-call(bf16[128,192]{1,0:T(8,128)(2,1)S(1)} %get-tuple-element.24.pick_ref, bf16[96,1024]{1,0:T(8,128)(2,1)S(1)} %shard_map.74.mine_ref, bf16[64,1024]{1,0:T(8,128)(2,1)S(1)} %get-tuple-element.32.refs_0_, ...), custom_call_target="tpu_custom_call" | custom-call | tf_op jit(solution)/shard_map/pallas_call | solution.py:235
  18.0 1.6 %collective-permute-start.10 = (f32[64,128]{1,0:T(8,128)S(1)}, f32[64,128]{1,0:T(8,128)S(1)}, u32[]{:S(2)}, u32[]{:S(2)}) collective-permute-start(f32[64,128]{1,0:T(8,128)S(1)} %get-tuple-element.41), channel_id=1, source_target_pairs={{0,2},{1,3},{2,0},{3,1},{4,6},{5,7},{6,4},{7,5},{8,10},{9,11},{10,... | collective-permute-start | bytes 98312 | tf_op jit(solution)/shard_map/ppermute | solution.py:245
  19.5 0.2 collective-permute-start.11
  19.7 0.4 %collective-permute-start.9 = (f32[64,128]{1,0:T(8,128)S(1)}, f32[64,128]{1,0:T(8,128)S(1)}, u32[]{:S(2)}, u32[]{:S(2)}) collective-permute-start(f32[64,128]{1,0:T(8,128)S(1)} %get-tuple-element.40), channel_id=1, source_target_pairs={{0,1},{1,0},{2,3},{3,2},{4,5},{5,4},{6,7},{7,6},{8,9},{9,8},{10,11... | collective-permute-start | bytes 98312 | tf_op jit(solution)/shard_map/ppermute | solution.py:245
  20.2 1.8 %collective-permute-done.10 = f32[64,128]{1,0:T(8,128)S(1)} collective-permute-done((f32[64,128]{1,0:T(8,128)S(1)}, f32[64,128]{1,0:T(8,128)S(1)}, u32[]{:S(2)}, u32[]{:S(2)}) %collective-permute-start.10) | collective-permute-done | bytes 32800 | tf_op jit(solution)/shard_map/ppermute | solution.py:245
  21.9 1.0 %collective-permute-done.11 = f32[64,128]{1,0:T(8,128)S(1)} collective-permute-done((f32[64,128]{1,0:T(8,128)S(1)}, f32[64,128]{1,0:T(8,128)S(1)}, u32[]{:S(2)}, u32[]{:S(2)}) %collective-permute-start.11) | collective-permute-done | bytes 32800 | tf_op jit(solution)/shard_map/ppermute | solution.py:245
  23.0 0.0 collective-permute-done.9
  23.0 0.6 %add_add_fusion = f32[64,128]{1,0:T(8,128)} fusion(f32[64,128]{1,0:T(8,128)S(1)} %collective-permute-done.11, f32[64,128]{1,0:T(8,128)S(1)} %collective-permute-done.10, f32[64,128]{1,0:T(8,128)S(1)} %get-tuple-element.39, f32[64,128]{1,0:T(8,128)S(1)} %collective-permute-done.9), kind=kLoop, calls=%fused_computation | loop fusion | flops 24576 | bytes 163840 | tf_op jit(solution)/shard_map/add | solution.py:281
Async XLA Ops:
  0.0 9.4 %collective-permute-start = (bf16[32,1024]{1,0:T(8,128)(2,1)}, bf16[32,1024]{1,0:T(8,128)(2,1)S(1)}, u32[]{:S(2)}, u32[]{:S(2)}) collective-permute-start(bf16[32,1024]{1,0:T(8,128)(2,1)} %bitcast.1), channel_id=1, source_target_pairs={{0,16},{4,20},{8,24},{12,28},{16,0},{20,4},{24,8},{28,12},{1,17},{... | collective-permute-start | bytes 196616 | tf_op jit(solution)/shard_map/ppermute | solution.py:245
  4.0 6.4 %collective-permute-start.1 = (bf16[32,1024]{1,0:T(8,128)(2,1)}, bf16[32,1024]{1,0:T(8,128)(2,1)S(1)}, u32[]{:S(2)}, u32[]{:S(2)}) collective-permute-start(bf16[32,1024]{1,0:T(8,128)(2,1)} %bitcast.2), channel_id=1, source_target_pairs={{0,24},{4,28},{8,16},{12,20},{16,8},{20,12},{24,0},{28,4},{1,25},{... | collective-permute-start | bytes 196616 | tf_op jit(solution)/shard_map/ppermute | solution.py:245
  5.4 5.2 %collective-permute-start.2 = (bf16[32,1024]{1,0:T(8,128)(2,1)}, bf16[32,1024]{1,0:T(8,128)(2,1)S(1)}, u32[]{:S(2)}, u32[]{:S(2)}) collective-permute-start(bf16[32,1024]{1,0:T(8,128)(2,1)} %bitcast.3), channel_id=1, source_target_pairs={{0,8},{4,12},{8,0},{12,4},{16,24},{20,28},{24,16},{28,20},{1,9},{5... | collective-permute-start | bytes 196616 | tf_op jit(solution)/shard_map/ppermute | solution.py:245
  7.3 7.9 %collective-permute-start.4 = (bf16[64,1024]{1,0:T(8,128)(2,1)S(1)}, bf16[64,1024]{1,0:T(8,128)(2,1)S(1)}, u32[]{:S(2)}, u32[]{:S(2)}) collective-permute-start(bf16[64,1024]{1,0:T(8,128)(2,1)S(1)} %get-tuple-element.34), channel_id=1, source_target_pairs={{0,2},{1,3},{2,0},{3,1},{4,6},{5,7},{6,4},{7,5},{8,10},{9,11},{10,... | collective-permute-start | bytes 393224 | tf_op jit(solution)/shard_map/ppermute | solution.py:245
  8.9 6.3 %collective-permute-start.5 = (bf16[64,1024]{1,0:T(8,128)(2,1)S(1)}, bf16[64,1024]{1,0:T(8,128)(2,1)S(1)}, u32[]{:S(2)}, u32[]{:S(2)}) collective-permute-start(bf16[64,1024]{1,0:T(8,128)(2,1)S(1)} %get-tuple-element.35), channel_id=1, source_target_pairs={{0,2},{1,3},{2,0},{3,1},{4,6},{5,7},{6,4},{7,5},{8,10},{9,11},{10,... | collective-permute-start | bytes 393224 | tf_op jit(solution)/shard_map/ppermute | solution.py:245
  11.2 6.3 %collective-permute-start.8 = (bf16[96,1024]{1,0:T(8,128)(2,1)S(1)}, bf16[96,1024]{1,0:T(8,128)(2,1)S(1)}, u32[]{:S(2)}, u32[]{:S(2)}) collective-permute-start(bf16[96,1024]{1,0:T(8,128)(2,1)S(1)} %shard_map.74.mine_ref), channel_id=1, source_target_pairs={{0,4},{4,0},{8,12},{12,8},{16,20},{20,16},{24,28},{28,24},{1,5},{5... | collective-permute-start | bytes 589832 | tf_op jit(solution)/shard_map/ppermute | solution.py:245
  12.7 1.2 %collective-permute-start.3 = (bf16[64,32]{1,0:T(8,128)(2,1)S(1)}, bf16[64,32]{1,0:T(8,128)(2,1)S(1)}, u32[]{:S(2)}, u32[]{:S(2)}) collective-permute-start(bf16[64,32]{1,0:T(8,128)(2,1)S(1)} %get-tuple-element.29), channel_id=1, source_target_pairs={{0,1},{1,0},{2,3},{3,2},{4,5},{5,4},{6,7},{7,6},{8,9},{9,8},{10,11... | collective-permute-start | bytes 12296 | tf_op jit(solution)/shard_map/ppermute | solution.py:245
  15.0 1.5 %collective-permute-start.6 = (bf16[64,1024]{1,0:T(8,128)(2,1)S(1)}, bf16[64,1024]{1,0:T(8,128)(2,1)S(1)}, u32[]{:S(2)}, u32[]{:S(2)}) collective-permute-start(bf16[64,1024]{1,0:T(8,128)(2,1)S(1)} %get-tuple-element.37), channel_id=1, source_target_pairs={{0,1},{1,0},{2,3},{3,2},{4,5},{5,4},{6,7},{7,6},{8,9},{9,8},{10,11... | collective-permute-start | bytes 393224 | tf_op jit(solution)/shard_map/ppermute | solution.py:245
  16.0 1.4 %collective-permute-start.7 = (bf16[64,1024]{1,0:T(8,128)(2,1)S(1)}, bf16[64,1024]{1,0:T(8,128)(2,1)S(1)}, u32[]{:S(2)}, u32[]{:S(2)}) collective-permute-start(bf16[64,1024]{1,0:T(8,128)(2,1)S(1)} %get-tuple-element.38), channel_id=1, source_target_pairs={{0,1},{1,0},{2,3},{3,2},{4,5},{5,4},{6,7},{7,6},{8,9},{9,8},{10,11... | collective-permute-start | bytes 393224 | tf_op jit(solution)/shard_map/ppermute | solution.py:245
  18.0 4.0 %collective-permute-start.10 = (f32[64,128]{1,0:T(8,128)S(1)}, f32[64,128]{1,0:T(8,128)S(1)}, u32[]{:S(2)}, u32[]{:S(2)}) collective-permute-start(f32[64,128]{1,0:T(8,128)S(1)} %get-tuple-element.41), channel_id=1, source_target_pairs={{0,2},{1,3},{2,0},{3,1},{4,6},{5,7},{6,4},{7,5},{8,10},{9,11},{10,... | collective-permute-start | bytes 98312 | tf_op jit(solution)/shard_map/ppermute | solution.py:245
  19.5 3.4 %collective-permute-start.11 = (f32[64,128]{1,0:T(8,128)S(1)}, f32[64,128]{1,0:T(8,128)S(1)}, u32[]{:S(2)}, u32[]{:S(2)}) collective-permute-start(f32[64,128]{1,0:T(8,128)S(1)} %get-tuple-element.42), channel_id=1, source_target_pairs={{0,3},{1,2},{2,1},{3,0},{4,7},{5,6},{6,5},{7,4},{8,11},{9,10},{10,... | collective-permute-start | bytes 98312 | tf_op jit(solution)/shard_map/ppermute | solution.py:245
  19.7 3.3 %collective-permute-start.9 = (f32[64,128]{1,0:T(8,128)S(1)}, f32[64,128]{1,0:T(8,128)S(1)}, u32[]{:S(2)}, u32[]{:S(2)}) collective-permute-start(f32[64,128]{1,0:T(8,128)S(1)} %get-tuple-element.40), channel_id=1, source_target_pairs={{0,1},{1,0},{2,3},{3,2},{4,5},{5,4},{6,7},{7,6},{8,9},{9,8},{10,11... | collective-permute-start | bytes 98312 | tf_op jit(solution)/shard_map/ppermute | solution.py:245
